TPU v7x, 32 devices: a whole 2x2x4 slice. The times are simulated.
32 devices in a mesh: layer: 4 (over y, x), feat: 8 (over z, core).
Axes of the slice: x: 2, y: 2, z: 4, core: 2. Of those that a mesh axis runs over, the one named last changes fastest.
Arguments:
- inputs: bfloat16 [4, 128, 2304], P('layer'), may hold values from -6 to 6
- targets: bfloat16 [4, 128, 2304], P('layer', None, 'feat'), may hold values from -6 to 6
- w_enc: bfloat16 [4, 2304, 2048], P('layer', None, 'feat'), may hold values from -0.125 to 0.125
- b_enc: float32 [4, 2048], P('layer', 'feat'), may hold values from -3 to 3
- w_dec: bfloat16 [4, 4, 2048, 2304], P('layer', None, 'feat'), may hold values from -0.0625 to 0.0625
Outputs:
- grad_enc: bfloat16 [4, 2304, 2048], P('layer', None, 'feat')
- grad_dec: bfloat16 [4, 4, 2048, 2304], P('layer', None, 'feat')
- grad_benc: float32 [4, 2048], P('layer', 'feat')
All inputs are finite; a program needn't handle non-finite values.
Results may differ from a plain program's by a relative error of at most 0.0085.
Values may be sent and summed in bfloat16 or wider, within the bound.
No kernel may reach another device: no remote copies, remote signals or barrier semaphores. Data moves between devices by JAX's collectives and lax.ppermute only.
A program may use at most 64 MiB of HBM per device.

v0:
```python
import jax
import jax.numpy as jnp
from jax import lax
from jax.sharding import PartitionSpec as P


def shards(inputs, targets, w_enc, b_enc, w_dec):
    layer_count = w_dec.shape[1]
    feat_count = lax.axis_size("feat")
    tok_count = inputs.shape[1]
    model_width = inputs.shape[2]
    col_count = model_width // feat_count
    slab_width = w_dec.shape[2]
    grad_scale = tok_count ** (-0.5)
    own_layer = lax.axis_index("layer")
    pre_act = jnp.dot(inputs[0], w_enc[0], preferred_element_type=jnp.float32) + b_enc[0]
    active = jax.nn.relu(pre_act).astype(jnp.bfloat16)
    later_mask = jnp.arange(layer_count) >= own_layer
    later_float = later_mask.astype(jnp.float32)
    later_half = later_mask.astype(jnp.bfloat16)
    weights = w_dec[0]
    blocks = weights.reshape(layer_count, slab_width, feat_count, col_count)
    partials = jnp.einsum("tf,mfnc->mntc", active, blocks, preferred_element_type=jnp.float32)
    partials = partials * later_float[:, None, None, None]
    partials = partials.reshape(layer_count * feat_count, tok_count, col_count)
    rebuilt = lax.psum_scatter(partials, ("layer", "feat"), scatter_dimension=0, tiled=True)[0]
    errors = (rebuilt - targets[0].astype(jnp.float32)).astype(jnp.bfloat16)
    err_block = errors[None, None]
    err_rows = lax.all_gather(err_block, "feat", axis=1, tiled=True)
    masked = lax.all_gather(err_rows, "layer", axis=0, tiled=True) * later_half[:, None, None, None]
    act_sum = jnp.einsum("mntc,mfnc->tf", masked, blocks, preferred_element_type=jnp.float32)
    update = jnp.einsum("tf,mntc->mfnc", active, masked, preferred_element_type=jnp.float32)
    dw_all = update
    act_sum, dw_all = (act_sum, dw_all)
    act_grad = grad_scale * act_sum
    dec_grad = dw_all * grad_scale
    grad_dec = dec_grad.astype(jnp.bfloat16).reshape(layer_count, slab_width, model_width)
    pre_grad = jnp.where(pre_act > 0, act_grad, 0.0).astype(jnp.bfloat16)
    grad_enc = jnp.einsum(
        "td,tf->df", inputs[0], pre_grad, preferred_element_type=jnp.float32
    ).astype(jnp.bfloat16)
    grad_benc = jnp.sum(pre_grad.astype(jnp.float32), axis=0)
    return (grad_enc[None], grad_dec[None], grad_benc[None])


def solution(mesh):
    in_specs = (
        P("layer", None, None),
        P("layer", None, "feat"),
        P("layer", None, "feat"),
        P("layer", "feat"),
        P("layer", None, "feat", None),
    )
    out_specs = (P("layer", None, "feat"), P("layer", None, "feat", None), P("layer", "feat"))
    return jax.shard_map(shards, mesh=mesh, in_specs=in_specs, out_specs=out_specs, check_vma=False)
```

profile of v0, /device:TPU:0, one launch (start us, length us, event | category | flops | bytes accessed | tf_op | source)
XLA Modules:
  0.0 207.4 jit_solution(4107269156842166839)
XLA Ops:
  7.2 0.0 copy-start
  7.2 0.0 reduce-scatter.2.cloned.1.call-start
  7.2 0.0 copy-start.2
  7.3 0.0 copy-start.4
  7.3 6.7 %copy.15 = bf16[1,4,256,2304]{2,3,1,0:T(8,128)(2,1)} copy(bf16[1,4,256,2304]{3,2,1,0:T(8,128)(2,1)} %param.9) | data formatting | bytes 9437184 | tf_op args[4]
  14.0 0.0 copy-done
  14.0 0.0 copy-done.2
  14.0 0.0 copy-done.4
  14.0 0.3 fusion.8
  14.3 5.9 %broadcast_multiply_fusion = f32[128,4,8,288]{0,3,2,1:T(8,128)} fusion(f32[4]{0:T(128)S(1)} %compare_convert_fusion.1, bf16[4,256,8,288]{1,3,2,0:T(8,128)(2,1)} %bitcast.43, f32[128,256]{1,0:T(8,128)S(1)} %fusion.8), kind=kOutput, calls=%fused_computation.3 | convolution fusion | flops 605224960 | bytes 9568272 | tf_op jit(solution)/shard_map/tf,mfnc->mntc/dot_general | solution.py:23
  20.2 0.0 copy-start.3
  20.2 0.0 reduce-scatter.2.cloned.1.call-update
  20.2 0.0 all-gather.4.cloned.1.call-start
  20.3 109.8 %reduce-scatter.2.cloned.1.call-done = f32[1,128,288]{1,2,0:T(8,128)} async-done(((f32[32,128,288]{1,2,0:T(8,128)}), f32[1,128,288]{1,2,0:T(8,128)}) %reduce-scatter.2.cloned.1.call-update) | async-done | bytes 147472 | tf_op jit(solution)/shard_map/reduce_scatter | solution.py:26
  130.1 0.0 copy-done.3
  130.1 0.9 subtract_convert_fusion
  131.0 16.0 %all-gather = bf16[8,128,288]{1,2,0:T(8,128)(2,1)} all-gather(bf16[1,128,288]{1,2,0:T(8,128)(2,1)S(1)} %subtract_convert_fusion), channel_id=2, replica_groups=mesh['layer'=4,'feat'=8] {'feat'}, dimensions={0}, use_global_device_ids=true | all-gather | bytes 663552 | tf_op jit(solution)/shard_map/all_gather | solution.py:29
  147.0 0.0 all-gather.4.cloned.1.call-update
  147.0 36.7 %all-gather.4.cloned.1.call-done = bf16[32,128,288]{1,2,0:T(8,128)(2,1)} async-done(((bf16[8,128,288]{1,2,0:T(8,128)(2,1)}), bf16[32,128,288]{1,2,0:T(8,128)(2,1)}) %all-gather.4.cloned.1.call-update) | async-done | bytes 2359312 | tf_op jit(solution)/shard_map/all_gather | solution.py:30
  183.7 0.0 copy-start.1
  183.7 4.7 %convert_reduce_fusion = (f32[256]{0:T(256)}, bf16[128,256]{1,0:T(8,128)(2,1)S(1)}) fusion(bf16[4,256,8,288]{1,3,2,0:T(8,128)(2,1)} %bitcast.44, bf16[4,8,128,288]{2,3,1,0:T(8,128)(2,1)} %bitcast.46, bf16[4]{0:T(256)(128)(2,1)S(1)} %compare_convert_fusion, f32[128,256]{1,0:T(8,128)S(1)} %fusion.8), kind=kOutput, calls=%fused_computation.19 | convolution fusion | flops 605355776 | bytes 7275528 | tf_op jit(solution)/shard_map/mntc,mfnc->tf/dot_general | solution.py:31
  188.5 0.0 copy-done.1
  188.5 3.6 %multiply_convert_fusion = bf16[4,8,288,256]{3,2,1,0:T(8,128)(2,1)} fusion(bf16[4,8,128,288]{2,3,1,0:T(8,128)(2,1)S(1)} %bitcast.47, bf16[4]{0:T(256)(128)(2,1)S(1)} %compare_convert_fusion, f32[128,256]{1,0:T(8,128)S(1)} %fusion.8), kind=kOutput, calls=%fused_computation | convolution fusion | flops 609943552 | bytes 7208968 | tf_op jit(solution)/shard_map/tf,mntc->mfnc/dot_general | solution.py:32
  192.0 0.5 fusion
  192.5 1.4 copy.16
  193.9 6.6 %copy.17 = bf16[1,4,256,2304]{3,2,1,0:T(8,128)(2,1)} copy(bf16[1,4,256,2304]{2,3,1,0:T(8,128)(2,1)} %bitcast.45) | data formatting | bytes 9437184
  (2 shorter events, 0.0 us)
Async XLA Ops:
  7.2 6.8 %copy-start = (bf16[1,2304,256]{2,1,0:T(8,128)(2,1)S(1)}, bf16[1,2304,256]{2,1,0:T(8,128)(2,1)}, u32[]{:S(2)}) copy-start(bf16[1,2304,256]{2,1,0:T(8,128)(2,1)} %param.7) | copy-start | bytes 3538948
  7.2 122.9 %reduce-scatter.2.cloned.1.call-start = ((), (), s32[]{:S(2)}) async-start(), calls=%async_computation.1 | async-start | bytes 4866048 | tf_op jit(solution)/shard_map/reduce_scatter | solution.py:26
  7.2 6.8 %copy-start.2 = (bf16[1,128,2304]{2,1,0:T(8,128)(2,1)S(1)}, bf16[1,128,2304]{2,1,0:T(8,128)(2,1)}, u32[]{:S(2)}) copy-start(bf16[1,128,2304]{2,1,0:T(8,128)(2,1)} %param.5) | copy-start | bytes 1769476
  7.3 6.7 %copy-start.4 = (f32[1,256]{1,0:T(1,128)S(1)}, f32[1,256]{1,0:T(1,128)}, u32[]{:S(2)}) copy-start(f32[1,256]{1,0:T(1,128)} %param.8) | copy-start | bytes 3076
  20.2 109.9 %copy-start.3 = (bf16[1,128,288]{1,2,0:T(8,128)(2,1)S(1)}, bf16[1,128,288]{1,2,0:T(8,128)(2,1)}, u32[]{:S(2)}) copy-start(bf16[1,128,288]{1,2,0:T(8,128)(2,1)} %param.6) | copy-start | bytes 221188
  20.2 163.5 %all-gather.4.cloned.1.call-start = ((), (), s32[]{:S(2)}) async-start(), calls=%async_computation.2 | async-start | bytes 2949120 | tf_op jit(solution)/shard_map/all_gather | solution.py:30
  183.7 4.7 %copy-start.1 = (bf16[32,128,288]{1,2,0:T(8,128)(2,1)S(1)}, bf16[32,128,288]{1,2,0:T(8,128)(2,1)}, u32[]{:S(2)}) copy-start(bf16[32,128,288]{1,2,0:T(8,128)(2,1)} %all-gather.4.cloned.1.call-done) | copy-start | bytes 7077892
Sparse Core Ops, SparseCore 0:
  20.3 109.6 reduce-scatter.1
  147.2 36.5 all-gather.3
where the time goes:
time: 208 us; the launch traced here: 207 us
  waiting for transfers between devices  146 us (70%)
  blocking collectives  16 us (8%)
  matrix products  15 us (7%)
  local copies, waits for them, and re-layouts  14.8 us (7%)
  between operations  14.1 us (7%)
    reduce_scatter x1, waiting for transfers between devices, shards(): lax.psum_scatter(partials, ('layer', 'feat'), scatter_dimension=0, tiled=...  110 us
    all_gather x1, waiting for transfers between devices, shards(): lax.all_gather(err_rows, 'layer', axis=0, tiled=True)  36.7 us
    all_gather x1, blocking collectives, shards(): err_rows = lax.all_gather(err_block, 'feat', axis=1, tiled=True)  16 us
    unnamed x13, local copies, waits for them, and re-layouts  14.8 us
    dot_general x1, matrix products, shards(): jnp.einsum('tf,mfnc->mntc', active, blocks, preferred_element_type=jnp.fl...  5.86 us
    dot_general x1, matrix products, shards(): jnp.einsum('mntc,mfnc->tf', masked, blocks, preferred_element_type=jnp.fl...  4.73 us
  transfers between devices with their start and end apart: 2, of which 2 were waited for; matrix products, arithmetic and copies ran while one was open for 0% of the time, Pallas kernels for 0%

commit v1 on v0

v1 whole, which is shorter than its diff:
```python
import functools

import jax
import jax.numpy as jnp
from jax import lax
from jax.experimental import pallas as pl
from jax.experimental.pallas import tpu as pltpu
from jax.sharding import PartitionSpec as P

F32 = jnp.float32
BF16 = jnp.bfloat16
VMEM_LIMIT = 48 * 1024 * 1024


def slot_offset(slot, core, bits):
    mirrored = 0
    for k in range(bits):
        mirrored = mirrored | (((slot >> k) & 1) << (bits - 1 - k))
    return jnp.where(core == 1, slot, mirrored)


def layer_bit(step, core, bits):
    return bits - 1 - step if core == 1 else step


def call(kernel, grid, in_specs, out_specs, out_shape, flops, nbytes, aliases=None, scratch=()):
    return pl.pallas_call(
        kernel,
        grid_spec=pltpu.PrefetchScalarGridSpec(
            num_scalar_prefetch=1,
            grid=grid,
            in_specs=in_specs,
            out_specs=out_specs,
            scratch_shapes=list(scratch),
        ),
        out_shape=out_shape,
        input_output_aliases=aliases or {},
        compiler_params=pltpu.CompilerParams(
            vmem_limit_bytes=VMEM_LIMIT,
            dimension_semantics=("arbitrary",) * len(grid),
        ),
        cost_estimate=pl.CostEstimate(flops=flops, bytes_accessed=nbytes, transcendentals=0),
    )


def fixed(shape):
    return pl.BlockSpec(shape, lambda *_: (0,) * len(shape))


def encode(pos, x, w_enc, b_enc, w_dec):
    layers, width, cols = w_dec.shape
    toks, half = x.shape[0], cols // 2
    bits = layers.bit_length() - 1

    def target(slot, pos):
        return pos[0] ^ slot_offset(slot, 1 - pos[1], bits)

    def kernel(pos, x_ref, we_ref, b_ref, wd_ref, pre_ref, act_ref, act_t_ref, send_ref):
        slot = pl.program_id(0)

        @pl.when(slot == 0)
        def _():
            pre = jnp.dot(x_ref[...], we_ref[...], preferred_element_type=F32) + b_ref[...]
            pre_ref[...] = pre
            act = jnp.maximum(pre, 0.0).astype(BF16)
            act_ref[...] = act
            act_t_ref[...] = act.T

        live = target(slot, pos) >= pos[0]

        @pl.when(live)
        def _():
            send_ref[0] = jnp.dot(act_ref[...], wd_ref[0], preferred_element_type=F32).astype(BF16)

        @pl.when(jnp.logical_not(live))
        def _():
            send_ref[...] = jnp.zeros_like(send_ref)

    return call(
        kernel,
        (layers,),
        [
            fixed(x.shape),
            fixed(w_enc.shape),
            fixed(b_enc.shape),
            pl.BlockSpec((1, width, half), lambda s, pos: (target(s, pos), 0, 1 - pos[1])),
        ],
        [
            fixed((toks, width)),
            fixed((toks, width)),
            fixed((width, toks)),
            pl.BlockSpec((1, toks, half), lambda s, pos: (s, 0, 0)),
        ],
        [
            jax.ShapeDtypeStruct((toks, width), F32),
            jax.ShapeDtypeStruct((toks, width), BF16),
            jax.ShapeDtypeStruct((width, toks), BF16),
            jax.ShapeDtypeStruct((layers, toks, half), BF16),
        ],
        2 * toks * width * cols + layers * toks * width * cols,
        w_enc.size * 2 + w_dec.size,
    )(pos, x, w_enc, b_enc, w_dec)


def decode_kept(pos, act, w_dec):
    layers, width, cols = w_dec.shape
    toks, half = act.shape[0], cols // 2
    bits = layers.bit_length() - 1

    def target(slot, pos):
        return pos[0] ^ slot_offset(slot, pos[1], bits)

    def kernel(pos, act_ref, wd_ref, keep_ref):
        live = target(pl.program_id(0), pos) >= pos[0]

        @pl.when(live)
        def _():
            keep_ref[0] = jnp.dot(act_ref[...], wd_ref[0], preferred_element_type=F32)

        @pl.when(jnp.logical_not(live))
        def _():
            keep_ref[...] = jnp.zeros_like(keep_ref)

    return call(
        kernel,
        (layers,),
        [
            fixed(act.shape),
            pl.BlockSpec((1, width, half), lambda s, pos: (target(s, pos), 0, pos[1])),
        ],
        pl.BlockSpec((1, toks, half), lambda s, pos: (s, 0, 0)),
        jax.ShapeDtypeStruct((layers, toks, half), F32),
        layers * toks * width * cols,
        w_dec.size,
    )(pos, act, w_dec)


def backward(pos, first, own, other, act_t, w_dec, carry):
    layers, width, cols = w_dec.shape
    count, toks, half = own.shape
    bits = layers.bit_length() - 1
    scale = toks ** (-0.5)

    def side(part, pos):
        return jnp.where(part == 0, pos[1], 1 - pos[1])

    def target(j, part, pos):
        return pos[0] ^ slot_offset(first + j, side(part, pos), bits)

    def kernel(pos, own_ref, oth_ref, act_t_ref, wd_ref, *refs):
        sum_ref, grad_ref = refs[-2:]
        j, part = pl.program_id(0), pl.program_id(1)

        @pl.when((j == 0) & (part == 0))
        def _():
            sum_ref[...] = jnp.zeros_like(sum_ref) if carry is None else refs[0][...]

        live = target(j, part, pos) >= pos[0]

        def work(err):
            sum_ref[...] += lax.dot_general(
                err, wd_ref[0], (((1,), (1,)), ((), ())), preferred_element_type=F32
            )
            grad = jnp.dot(act_t_ref[...], err, preferred_element_type=F32)
            grad_ref[0] = (grad * scale).astype(BF16)

        @pl.when(live & (part == 0))
        def _():
            work(own_ref[0])

        @pl.when(live & (part == 1))
        def _():
            work(oth_ref[0])

        @pl.when(jnp.logical_not(live))
        def _():
            grad_ref[...] = jnp.zeros_like(grad_ref)

    block = pl.BlockSpec(
        (1, width, half), lambda j, part, pos: (target(j, part, pos), 0, side(part, pos))
    )
    err_spec = pl.BlockSpec((1, toks, half), lambda j, part, pos: (j, 0, 0))
    in_specs = [err_spec, err_spec, fixed(act_t.shape), block]
    args = [pos, own, other, act_t, w_dec]
    aliases = {}
    if carry is not None:
        in_specs += [fixed((toks, width)), pl.BlockSpec(memory_space=pl.ANY)]
        args += list(carry)
        aliases = {len(args) - 1: 1}
    return call(
        kernel,
        (count, 2),
        in_specs,
        [fixed((toks, width)), block],
        [jax.ShapeDtypeStruct((toks, width), F32), jax.ShapeDtypeStruct(w_dec.shape, BF16)],
        4 * count * toks * width * cols,
        4 * count * width * cols,
        aliases,
    )(*args)


def encoder_grads(pos, x, pre, act_sum):
    toks, cols = x.shape
    width = pre.shape[1]
    half = cols // 2
    scale = toks ** (-0.5)

    def kernel(pos, x_ref, pre_ref, sum_ref, genc_ref, gb_ref):
        pre_grad = jnp.where(pre_ref[...] > 0, sum_ref[...] * scale, 0.0).astype(BF16)
        genc_ref[...] = lax.dot_general(
            x_ref[...], pre_grad, (((0,), (0,)), ((), ())), preferred_element_type=F32
        ).astype(BF16)
        gb_ref[...] = jnp.sum(pre_grad.astype(F32), axis=0, keepdims=True)

    return call(
        kernel,
        (2,),
        [
            pl.BlockSpec((toks, half), lambda i, pos: (0, i)),
            fixed(pre.shape),
            fixed(act_sum.shape),
        ],
        [pl.BlockSpec((half, width), lambda i, pos: (i, 0)), fixed((1, width))],
        [jax.ShapeDtypeStruct((cols, width), BF16), jax.ShapeDtypeStruct((1, width), F32)],
        2 * toks * cols * width,
        2 * cols * width,
    )(pos, x, pre, act_sum)


def shards(inputs, targets, w_enc, b_enc, w_dec):
    layers, cols = w_dec.shape[1], w_dec.shape[3]
    feats = lax.axis_size("feat")
    bits, feat_bits = layers.bit_length() - 1, feats.bit_length() - 1
    half = cols // 2
    own_layer, own_feat = lax.axis_index("layer"), lax.axis_index("feat")
    core = own_feat & 1
    pos = jnp.stack([own_layer, core]).astype(jnp.int32)
    x, tgt, wd = inputs[0], targets[0], w_dec[0]

    def swap_feat(value, bit):
        return lax.ppermute(value, "feat", [(f, f ^ (1 << bit)) for f in range(feats)])

    def swap_layer(value, step):
        pairs = [
            (l * feats + f, (l ^ (1 << layer_bit(step, f & 1, bits))) * feats + f)
            for l in range(layers)
            for f in range(feats)
        ]
        return lax.ppermute(value, ("layer", "feat"), pairs)

    pre, act, act_t, send = encode(pos, x, w_enc[0], b_enc, wd)
    got = swap_feat(send, 0)
    keep = decode_kept(pos, act, wd)

    pair_tgt = swap_feat(tgt, 0)
    wide = jnp.zeros((x.shape[0], cols), BF16)
    wide = lax.dynamic_update_slice(wide, tgt, (0, own_feat * tgt.shape[1]))
    wide = lax.dynamic_update_slice(wide, pair_tgt, (0, (own_feat ^ 1) * tgt.shape[1]))
    wide = jnp.where(core == 0, wide[:, :half], wide[:, half:])

    slots = [keep[s] + got[s].astype(F32) for s in range(layers)]
    for step in range(bits):
        n = len(slots) // 2
        cut = n // 2
        parts = [(n + cut, 2 * n), (n, n + cut)] if cut else [(n, 2 * n)]
        arrived = {}
        for low, high in parts:
            piece = jnp.stack([slots[s] for s in range(low, high)]).astype(BF16)
            piece = swap_layer(piece, step)
            for s in range(low, high):
                arrived[s - n] = piece[s - low]
        slots = [slots[s] + arrived[s].astype(F32) for s in range(n)]
    rows = slots[0] - wide.astype(F32)

    for bit in range(1, feat_bits - 1):
        n = rows.shape[0] // 2
        high = ((own_feat >> bit) & 1) == 1
        away = jnp.where(high, rows[:n], rows[n:]).astype(BF16)
        rows = jnp.where(high, rows[n:], rows[:n]) + swap_feat(away, bit).astype(F32)
    rows = rows + swap_feat(rows.astype(BF16), feat_bits - 1).astype(F32)
    err = rows.astype(BF16)

    for bit in reversed(range(1, feat_bits - 1)):
        high = ((own_feat >> bit) & 1) == 1
        far = swap_feat(err, bit)
        err = jnp.concatenate([jnp.where(high, far, err), jnp.where(high, err, far)])

    slots = [err]
    own = err[None]
    carry = None
    first = 0
    for step in reversed(range(-1, bits)):
        carry = backward(pos, first, own, swap_feat(own, 0), act_t, wd, carry)
        if step < 0:
            break
        first = len(slots)
        cut = first // 2
        parts = [(0, cut), (cut, first)] if cut else [(0, first)]
        new = []
        for low, high in parts:
            piece = swap_layer(jnp.stack(slots[low:high]), step)
            new += [piece[i] for i in range(high - low)]
        slots = slots + new
        own = jnp.stack(new)
    act_sum, grad_dec = carry
    grad_enc, grad_benc = encoder_grads(pos, x, pre, act_sum)
    return grad_enc[None], grad_dec[None], grad_benc


def solution(mesh):
    in_specs = (
        P("layer", None, None),
        P("layer", None, "feat"),
        P("layer", None, "feat"),
        P("layer", "feat"),
        P("layer", None, "feat", None),
    )
    out_specs = (P("layer", None, "feat"), P("layer", None, "feat", None), P("layer", "feat"))
    return jax.shard_map(shards, mesh=mesh, in_specs=in_specs, out_specs=out_specs, check_vma=False)
```

time: 208 us -> 81.2 us (0.39)
  waiting for transfers between devices: 146 us -> 33.1 us
  Pallas kernels: 0 us -> 20.1 us
  starting transfers between devices: 0.08 us -> 16.1 us
  blocking collectives: 16 us -> 0 us
  matrix products: 15 us -> 0 us
  between operations: 14.1 us -> 0.8 us
  local copies, waits for them, and re-layouts: 14.8 us -> 8.06 us
    reduce_scatter x1 -> x0, waiting for transfers between devices: 110 us -> none  [shards(): lax.psum_scatter(partials, ('layer', 'feat'), scatter_dimension=0, tiled=...]
    all_gather x1 -> x0, waiting for transfers between devices: 36.7 us -> none  [shards(): lax.all_gather(err_rows, 'layer', axis=0, tiled=True)]
    ppermute x0 -> x14, waiting for transfers between devices: none -> 33.1 us  [the longest x6 18.4 us: swap_layer(): return lax.ppermute(value, ('layer', 'feat'), pairs)]
    pallas_call x0 -> x6, Pallas kernels: none -> 20.1 us  [the longest x3 10.4 us: backward(): call(kernel, (count, 2), in_specs, [fixed((toks, width)), block], [jax.Sh...]
    ppermute x0 -> x14, starting transfers between devices: none -> 16.1 us  [the longest x6 8.7 us: swap_layer(): return lax.ppermute(value, ('layer', 'feat'), pairs)]
    all_gather x1 -> x0, blocking collectives: 16 us -> none  [shards(): err_rows = lax.all_gather(err_block, 'feat', axis=1, tiled=True)]
    dot_general x5 -> x0, matrix products: 15 us -> none  [the longest x1 5.86 us: shards(): jnp.einsum('tf,mfnc->mntc', active, blocks, preferred_element_type=jnp.fl...]
    unnamed x13 -> x16, local copies, waits for them, and re-layouts: 14.8 us -> 5.51 us
  transfers between devices with their start and end apart: 2 -> 14, of which waited for: 2 -> 9; matrix products, arithmetic and copies ran while one was open for 0% -> 4% of each run, Pallas kernels for 0% -> 11%
where the time goes in v1:
time: 81.2 us; the launch traced here: 80.7 us
  waiting for transfers between devices  33.1 us (41%)
  Pallas kernels  20.1 us (25%)
  starting transfers between devices  16.1 us (20%)
  local copies, waits for them, and re-layouts  8.06 us (10%)
  other arithmetic  2.56 us (3%)
    ppermute x6, waiting for transfers between devices, swap_layer(): return lax.ppermute(value, ('layer', 'feat'), pairs)  18.4 us
    ppermute x8, waiting for transfers between devices, swap_feat(): lax.ppermute(value, 'feat', [(f, f ^ 1 << bit) for f in range(feats)])  14.8 us
    pallas_call x3, Pallas kernels, backward(): call(kernel, (count, 2), in_specs, [fixed((toks, width)), block], [jax.Sh...  10.4 us
    ppermute x6, starting transfers between devices, swap_layer(): return lax.ppermute(value, ('layer', 'feat'), pairs)  8.7 us
    ppermute x8, starting transfers between devices, swap_feat(): lax.ppermute(value, 'feat', [(f, f ^ 1 << bit) for f in range(feats)])  7.4 us
    unnamed x16, local copies, waits for them, and re-layouts  5.51 us
    pallas_call x1, Pallas kernels, encode(): call(kernel, (layers,), [fixed(x.shape), fixed(w_enc.shape), fixed(b_enc....  3.98 us
    pallas_call x1, Pallas kernels, decode_kept(): call(kernel, (layers,), [fixed(act.shape), pl.BlockSpec((1, width, half),...  3.56 us
  transfers between devices with their start and end apart: 14, of which 9 were waited for; matrix products, arithmetic and copies ran while one was open for 4% of the time, Pallas kernels for 11%

profile of v1, /device:TPU:0, one launch (start us, length us, event | category | flops | bytes accessed | tf_op | source)
XLA Modules:
  0.0 80.7 jit_solution(367144462192381797)
XLA Ops:
  0.7 1.1 %copy-done.1 = bf16[1,128,2304]{2,1,0:T(8,128)(2,1)S(1)} copy-done((bf16[1,128,2304]{2,1,0:T(8,128)(2,1)S(1)}, bf16[1,128,2304]{2,1,0:T(8,128)(2,1)}, u32[]{:S(2)}) %copy-start.1) | copy-done | bytes 589848
  1.8 1.3 %copy-done.3 = bf16[1,2304,256]{2,1,0:T(8,128)(2,1)S(1)} copy-done((bf16[1,2304,256]{2,1,0:T(8,128)(2,1)S(1)}, bf16[1,2304,256]{2,1,0:T(8,128)(2,1)}, u32[]{:S(2)}) %copy-start.3) | copy-done | bytes 1179672
  3.0 0.7 copy-done.4
  3.7 4.0 %shard_map.76 = (f32[128,256]{1,0:T(8,128)S(1)}, bf16[128,256]{1,0:T(8,128)(2,1)S(1)}, bf16[256,128]{1,0:T(8,128)(2,1)S(1)}, bf16[4,128,1152]{2,1,0:T(8,128)(2,1)S(1)}) custom-call(s32[2]{0:T(128)S(1)} %pad_add_fusion.pos, bf16[128,2304]{1,0:T(8,128)(2,1)S(1)} %bitcast.19, bf16[2304,256]{1,0:T(8,128)(2,1)S(1)} %bitcast.21, f32[1,256]{1,0:T(1,128)S(1)} %copy-done.4, ...), custom_call_target="tpu_custom_call" | custom-call | flops 452984832 | bytes 3538944 | tf_op jit(solution)/shard_map/pallas_call | solution.py:79
  7.7 0.5 collective-permute-start
  8.2 3.6 %shard_map.77 = f32[4,128,1152]{2,1,0:T(8,128)S(1)} custom-call(s32[2]{0:T(128)S(1)} %pad_add_fusion.pos, bf16[128,256]{1,0:T(8,128)(2,1)S(1)} %get-tuple-element.16.act_ref, bf16[4,256,2304]{2,1,0:T(8,128)(2,1)} %bitcast.15), custom_call_target="tpu_custom_call" | custom-call | flops 301989888 | bytes 2359296 | tf_op jit(solution)/shard_map/pallas_call | solution.py:124
  11.9 2.5 %collective-permute-start.2 = (bf16[1,128,1152]{2,1,0:T(8,128)(2,1)S(1)}, bf16[1,128,1152]{2,1,0:T(8,128)(2,1)S(1)}, u32[]{:S(2)}, u32[]{:S(2)}) collective-permute-start(bf16[1,128,1152]{2,1,0:T(8,128)(2,1)S(1)} %get-tuple-element.28), channel_id=1, source_target_pairs={{0,8},{1,17},{2,10},{3,19},{4,12},{5,21},{6,14},{7,23},{8,0},{9,25... | collective-permute-start | bytes 884744 | tf_op jit(solution)/shard_map/ppermute | solution.py:249
  14.5 4.6 %collective-permute-done.2 = bf16[1,128,1152]{2,1,0:T(8,128)(2,1)S(1)} collective-permute-done((bf16[1,128,1152]{2,1,0:T(8,128)(2,1)S(1)}, bf16[1,128,1152]{2,1,0:T(8,128)(2,1)S(1)}, u32[]{:S(2)}, u32[]{:S(2)}) %collective-permute-start.2) | collective-permute-done | bytes 294944 | tf_op jit(solution)/shard_map/ppermute | solution.py:249
  19.2 0.8 fusion.2
  20.0 1.6 %collective-permute-start.3 = (bf16[1,128,1152]{2,1,0:T(8,128)(2,1)}, bf16[1,128,1152]{2,1,0:T(8,128)(2,1)}, u32[]{:S(2)}, u32[]{:S(2)}) collective-permute-start(bf16[1,128,1152]{2,1,0:T(8,128)(2,1)} %fusion.2), channel_id=1, source_target_pairs={{0,16},{1,9},{2,18},{3,11},{4,20},{5,13},{6,22},{7,15},{8,24},{9,1... | collective-permute-start | bytes 884744 | tf_op jit(solution)/shard_map/ppermute | solution.py:249
  21.8 0.8 dynamic_update_slice.6
  22.7 0.5 collective-permute-done.4
  23.2 1.7 %dynamic_update_slice.7 = bf16[128,2304]{1,0:T(8,128)(2,1)S(1)} dynamic-update-slice(bf16[128,2304]{1,0:T(8,128)(2,1)S(1)} %dynamic_update_slice.6, bf16[128,288]{1,0:T(8,128)(2,1)} %collective-permute-done.4, s32[]{:T(128)} %constant.5.clone.1, s32[]{:T(128)S(6)} %select_n.39) | dynamic-update-slice | bytes 147460 | tf_op jit(solution)/shard_map/dynamic_update_slice | solution.py:258
  24.9 2.1 %collective-permute-done.3 = bf16[1,128,1152]{2,1,0:T(8,128)(2,1)} collective-permute-done((bf16[1,128,1152]{2,1,0:T(8,128)(2,1)}, bf16[1,128,1152]{2,1,0:T(8,128)(2,1)}, u32[]{:S(2)}, u32[]{:S(2)}) %collective-permute-start.3) | collective-permute-done | bytes 294944 | tf_op jit(solution)/shard_map/ppermute | solution.py:249
  27.0 1.4 %fusion.7 = f32[128,1152]{1,0:T(8,128)S(1)} fusion(f32[4,128,1152]{2,1,0:T(8,128)S(1)} %shard_map.77, bf16[1,128,1152]{2,1,0:T(8,128)(2,1)} %collective-permute-done.3, bf16[1,128,1152]{2,1,0:T(8,128)(2,1)} %collective-permute-done.1, bf16[128,2304]{1,0:T(8,128)(2,1)S(1)} %dynamic_update_slice.7, bf16[4,128,1152]{2,1,0:T(8,128)(2,1)} %copy-done.5, pred[]{:T(512)S(6)} %eq.8), kind=kLoop, calls=%fused_computation.11 | loop fusion | flops 1327104 | bytes 2654209 | tf_op jit(solution)/shard_map/sub | solution.py:273
  28.4 2.2 %collective-permute-start.5 = (bf16[64,1152]{1,0:T(8,128)(2,1)S(1)}, bf16[64,1152]{1,0:T(8,128)(2,1)S(1)}, u32[]{:S(2)}, u32[]{:S(2)}) collective-permute-start(bf16[64,1152]{1,0:T(8,128)(2,1)S(1)} %select_convert_fusion), channel_id=1, source_target_pairs={{0,2},{1,3},{2,0},{3,1},{4,6},{5,7},{6,4},{7,5},{8,10},{9,11},{10,... | collective-permute-start | bytes 442376 | tf_op jit(solution)/shard_map/ppermute | solution.py:241
  30.6 3.1 %collective-permute-done.5 = bf16[64,1152]{1,0:T(8,128)(2,1)S(1)} collective-permute-done((bf16[64,1152]{1,0:T(8,128)(2,1)S(1)}, bf16[64,1152]{1,0:T(8,128)(2,1)S(1)}, u32[]{:S(2)}, u32[]{:S(2)}) %collective-permute-start.5) | collective-permute-done | bytes 147488 | tf_op jit(solution)/shard_map/ppermute | solution.py:241
  33.8 3.1 %collective-permute-start.6 = (bf16[64,1152]{1,0:T(8,128)(2,1)S(1)}, bf16[64,1152]{1,0:T(8,128)(2,1)S(1)}, u32[]{:S(2)}, u32[]{:S(2)}) collective-permute-start(bf16[64,1152]{1,0:T(8,128)(2,1)S(1)} %fusion.8), channel_id=1, source_target_pairs={{0,4},{1,5},{2,6},{3,7},{4,0},{5,1},{6,2},{7,3},{8,12},{9,13},{10,... | collective-permute-start | bytes 442376 | tf_op jit(solution)/shard_map/ppermute | solution.py:241
  36.9 4.9 %collective-permute-done.6 = bf16[64,1152]{1,0:T(8,128)(2,1)S(1)} collective-permute-done((bf16[64,1152]{1,0:T(8,128)(2,1)S(1)}, bf16[64,1152]{1,0:T(8,128)(2,1)S(1)}, u32[]{:S(2)}, u32[]{:S(2)}) %collective-permute-start.6) | collective-permute-done | bytes 147488 | tf_op jit(solution)/shard_map/ppermute | solution.py:241
  41.9 0.9 %collective-permute-start.7 = (bf16[64,1152]{1,0:T(8,128)(2,1)S(1)}, bf16[64,1152]{1,0:T(8,128)(2,1)S(1)}, u32[]{:S(2)}, u32[]{:S(2)}) collective-permute-start(bf16[64,1152]{1,0:T(8,128)(2,1)S(1)} %add_convert_fusion), channel_id=1, source_target_pairs={{0,2},{1,3},{2,0},{3,1},{4,6},{5,7},{6,4},{7,5},{8,10},{9,11},{10,... | collective-permute-start | bytes 442376 | tf_op jit(solution)/shard_map/ppermute | solution.py:241
  42.8 4.4 %collective-permute-done.7 = bf16[64,1152]{1,0:T(8,128)(2,1)S(1)} collective-permute-done((bf16[64,1152]{1,0:T(8,128)(2,1)S(1)}, bf16[64,1152]{1,0:T(8,128)(2,1)S(1)}, u32[]{:S(2)}, u32[]{:S(2)}) %collective-permute-start.7) | collective-permute-done | bytes 147488 | tf_op jit(solution)/shard_map/ppermute | solution.py:241
  47.2 1.3 %collective-permute-start.9 = (bf16[1,128,1152]{2,1,0:T(8,128)(2,1)S(1)}, bf16[1,128,1152]{2,1,0:T(8,128)(2,1)S(1)}, u32[]{:S(2)}, u32[]{:S(2)}) collective-permute-start(bf16[1,128,1152]{2,1,0:T(8,128)(2,1)S(1)} %maximum_bitcast_fusion.own_ref), channel_id=1, source_target_pairs={{0,16},{1,9},{2,18},{3,11},{4,20},{5,13},{6,22},{7,15},{8,24},{9,1... | collective-permute-start | bytes 884744 | tf_op jit(solution)/shard_map/ppermute | solution.py:249
  48.5 1.2 %collective-permute-start.8 = (bf16[1,128,1152]{2,1,0:T(8,128)(2,1)S(1)}, bf16[1,128,1152]{2,1,0:T(8,128)(2,1)S(1)}, u32[]{:S(2)}, u32[]{:S(2)}) collective-permute-start(bf16[1,128,1152]{2,1,0:T(8,128)(2,1)S(1)} %maximum_bitcast_fusion.own_ref), channel_id=1, source_target_pairs={{0,8},{1,17},{2,10},{3,19},{4,12},{5,21},{6,14},{7,23},{8,0},{9,25... | collective-permute-start | bytes 884744 | tf_op jit(solution)/shard_map/ppermute | solution.py:249
  49.7 6.9 %collective-permute-done.9.own_ref = bf16[1,128,1152]{2,1,0:T(8,128)(2,1)S(1)} collective-permute-done((bf16[1,128,1152]{2,1,0:T(8,128)(2,1)S(1)}, bf16[1,128,1152]{2,1,0:T(8,128)(2,1)S(1)}, u32[]{:S(2)}, u32[]{:S(2)}) %collective-permute-start.9) | collective-permute-done | bytes 294944 | tf_op jit(solution)/shard_map/ppermute | solution.py:249
  56.6 1.9 %collective-permute-start.10 = (bf16[1,128,1152]{2,1,0:T(8,128)(2,1)S(1)}, bf16[1,128,1152]{2,1,0:T(8,128)(2,1)S(1)}, u32[]{:S(2)}, u32[]{:S(2)}) collective-permute-start(bf16[1,128,1152]{2,1,0:T(8,128)(2,1)S(1)} %collective-permute-done.9.own_ref), channel_id=1, source_target_pairs={{0,8},{1,17},{2,10},{3,19},{4,12},{5,21},{6,14},{7,23},{8,0},{9,25... | collective-permute-start | bytes 884744 | tf_op jit(solution)/shard_map/ppermute | solution.py:249
  58.6 4.8 %collective-permute-done.10 = bf16[1,128,1152]{2,1,0:T(8,128)(2,1)S(1)} collective-permute-done((bf16[1,128,1152]{2,1,0:T(8,128)(2,1)S(1)}, bf16[1,128,1152]{2,1,0:T(8,128)(2,1)S(1)}, u32[]{:S(2)}, u32[]{:S(2)}) %collective-permute-start.10) | collective-permute-done | bytes 294944 | tf_op jit(solution)/shard_map/ppermute | solution.py:249
  64.0 1.8 %collective-permute-done.13.oth_ref = bf16[1,128,1152]{2,1,0:T(8,128)(2,1)S(1)} collective-permute-done((bf16[1,128,1152]{2,1,0:T(8,128)(2,1)S(1)}, bf16[1,128,1152]{2,1,0:T(8,128)(2,1)S(1)}, u32[]{:S(2)}, u32[]{:S(2)}) %collective-permute-start.13) | collective-permute-done | bytes 294944 | tf_op jit(solution)/shard_map/ppermute | solution.py:241
  65.9 2.3 %copy-done = bf16[1,4,256,2304]{3,2,1,0:T(8,128)(2,1)S(1)} copy-done((bf16[1,4,256,2304]{3,2,1,0:T(8,128)(2,1)S(1)}, bf16[1,4,256,2304]{3,2,1,0:T(8,128)(2,1)}, u32[]{:S(2)}) %copy-start) | copy-done | bytes 4718616
  68.2 2.5 %shard_map.78 = (f32[128,256]{1,0:T(8,128)S(1)}, bf16[4,256,2304]{2,1,0:T(8,128)(2,1)}) custom-call(s32[2]{0:T(128)S(1)} %pad_add_fusion.pos, bf16[1,128,1152]{2,1,0:T(8,128)(2,1)S(1)} %maximum_bitcast_fusion.own_ref, bf16[1,128,1152]{2,1,0:T(8,128)(2,1)S(1)} %collective-permute-done.13.oth_ref, bf16[256,128]{1,0:T(8,128)(2,1)S(1)} %get-tuple-element.18.act_t_ref, ...), custom_call_target="tpu_custom_call" | custom-call | flops 301989888 | bytes 2359296 | tf_op jit(solution)/shard_map/pallas_call | solution.py:190
  70.7 2.5 %shard_map.79 = (f32[128,256]{1,0:T(8,128)S(1)}, bf16[4,256,2304]{2,1,0:T(8,128)(2,1)}) custom-call(s32[2]{0:T(128)S(1)} %pad_add_fusion.pos, bf16[1,128,1152]{2,1,0:T(8,128)(2,1)S(1)} %collective-permute-done.9.own_ref, bf16[1,128,1152]{2,1,0:T(8,128)(2,1)S(1)} %collective-permute-done.12.oth_ref, ...), custom_call_target="tpu_custom_call", output_to_operand_aliasing={{1}: (6, {})} | custom-call | flops 301989888 | bytes 2359296 | tf_op jit(solution)/shard_map/pallas_call | solution.py:190
  73.2 5.3 %shard_map.80 = (f32[128,256]{1,0:T(8,128)S(1)}, bf16[4,256,2304]{2,1,0:T(8,128)(2,1)}) custom-call(s32[2]{0:T(128)S(1)} %pad_add_fusion.pos, bf16[2,128,1152]{2,1,0:T(8,128)(2,1)S(1)} %constant_dynamic-update-slice_fusion.own_ref, bf16[2,128,1152]{2,1,0:T(8,128)(2,1)S(1)} %collective-permute-done.11.oth_ref, ...), custom_call_target="tpu_custom_call", output_to_operand_aliasing={{1}: (6, {})} | custom-call | flops 603979776 | bytes 4718592 | tf_op jit(solution)/shard_map/pallas_call | solution.py:190
  78.6 2.2 %shard_map.81 = (bf16[2304,256]{1,0:T(8,128)(2,1)}, f32[1,256]{1,0:T(1,128)}) custom-call(s32[2]{0:T(128)S(1)} %pad_add_fusion.pos, bf16[128,2304]{1,0:T(8,128)(2,1)S(1)} %bitcast.20, f32[128,256]{1,0:T(8,128)S(1)} %get-tuple-element.15.pre_ref, f32[128,256]{1,0:T(8,128)S(1)} %get-tuple-element.23.sum_ref), custom_call_target="tpu_custom_call" | custom-call | flops 150994944 | bytes 1179648 | tf_op jit(solution)/shard_map/pallas_call | solution.py:215
  (31 shorter events, 1.4 us)
Async XLA Ops:
  0.7 1.1 %copy-start.1 = (bf16[1,128,2304]{2,1,0:T(8,128)(2,1)S(1)}, bf16[1,128,2304]{2,1,0:T(8,128)(2,1)}, u32[]{:S(2)}) copy-start(bf16[1,128,2304]{2,1,0:T(8,128)(2,1)} %param.5) | copy-start | bytes 1769476
  1.8 1.3 %copy-start.3 = (bf16[1,2304,256]{2,1,0:T(8,128)(2,1)S(1)}, bf16[1,2304,256]{2,1,0:T(8,128)(2,1)}, u32[]{:S(2)}) copy-start(bf16[1,2304,256]{2,1,0:T(8,128)(2,1)} %param.7) | copy-start | bytes 3538948
  3.0 0.7 copy-start.4
  7.7 4.1 %collective-permute-start = (bf16[4,128,1152]{2,1,0:T(8,128)(2,1)S(1)}, bf16[4,128,1152]{2,1,0:T(8,128)(2,1)S(1)}, u32[]{:S(2)}, u32[]{:S(2)}) collective-permute-start(bf16[4,128,1152]{2,1,0:T(8,128)(2,1)S(1)} %get-tuple-element.17), channel_id=1, source_target_pairs={{0,1},{1,0},{2,3},{3,2},{4,5},{5,4},{6,7},{7,6},{8,9},{9,8},{10,11... | collective-permute-start | bytes 3538952 | tf_op jit(solution)/shard_map/ppermute | solution.py:241
  11.8 9.8 %copy-start.6 = (bf16[1,128,288]{1,2,0:T(8,128)(2,1)S(1)}, bf16[1,128,288]{1,2,0:T(8,128)(2,1)}, u32[]{:S(2)}) copy-start(bf16[1,128,288]{1,2,0:T(8,128)(2,1)} %param.6) | copy-start | bytes 221188
  11.8 7.4 %copy-start.5 = (bf16[4,128,1152]{2,1,0:T(8,128)(2,1)}, bf16[4,128,1152]{2,1,0:T(8,128)(2,1)S(1)}, u32[]{:S(2)}) copy-start(bf16[4,128,1152]{2,1,0:T(8,128)(2,1)S(1)} %collective-permute-done) | copy-start | bytes 3538948
  11.9 7.2 %collective-permute-start.2 = (bf16[1,128,1152]{2,1,0:T(8,128)(2,1)S(1)}, bf16[1,128,1152]{2,1,0:T(8,128)(2,1)S(1)}, u32[]{:S(2)}, u32[]{:S(2)}) collective-permute-start(bf16[1,128,1152]{2,1,0:T(8,128)(2,1)S(1)} %get-tuple-element.28), channel_id=1, source_target_pairs={{0,8},{1,17},{2,10},{3,19},{4,12},{5,21},{6,14},{7,23},{8,0},{9,25... | collective-permute-start | bytes 884744 | tf_op jit(solution)/shard_map/ppermute | solution.py:249
  14.5 10.4 %collective-permute-start.1 = (bf16[1,128,1152]{2,1,0:T(8,128)(2,1)S(1)}, bf16[1,128,1152]{2,1,0:T(8,128)(2,1)}, u32[]{:S(2)}, u32[]{:S(2)}) collective-permute-start(bf16[1,128,1152]{2,1,0:T(8,128)(2,1)S(1)} %get-tuple-element.27), channel_id=1, source_target_pairs={{0,8},{1,17},{2,10},{3,19},{4,12},{5,21},{6,14},{7,23},{8,0},{9,25... | collective-permute-start | bytes 884744 | tf_op jit(solution)/shard_map/ppermute | solution.py:249
  20.0 7.0 %collective-permute-start.3 = (bf16[1,128,1152]{2,1,0:T(8,128)(2,1)}, bf16[1,128,1152]{2,1,0:T(8,128)(2,1)}, u32[]{:S(2)}, u32[]{:S(2)}) collective-permute-start(bf16[1,128,1152]{2,1,0:T(8,128)(2,1)} %fusion.2), channel_id=1, source_target_pairs={{0,16},{1,9},{2,18},{3,11},{4,20},{5,13},{6,22},{7,15},{8,24},{9,1... | collective-permute-start | bytes 884744 | tf_op jit(solution)/shard_map/ppermute | solution.py:249
  21.7 1.5 %collective-permute-start.4 = (bf16[128,288]{1,0:T(8,128)(2,1)S(1)}, bf16[128,288]{1,0:T(8,128)(2,1)}, u32[]{:S(2)}, u32[]{:S(2)}) collective-permute-start(bf16[128,288]{1,0:T(8,128)(2,1)S(1)} %bitcast.23), channel_id=1, source_target_pairs={{0,1},{1,0},{2,3},{3,2},{4,5},{5,4},{6,7},{7,6},{8,9},{9,8},{10,11... | collective-permute-start | bytes 221192 | tf_op jit(solution)/shard_map/ppermute | solution.py:241
  28.4 5.3 %collective-permute-start.5 = (bf16[64,1152]{1,0:T(8,128)(2,1)S(1)}, bf16[64,1152]{1,0:T(8,128)(2,1)S(1)}, u32[]{:S(2)}, u32[]{:S(2)}) collective-permute-start(bf16[64,1152]{1,0:T(8,128)(2,1)S(1)} %select_convert_fusion), channel_id=1, source_target_pairs={{0,2},{1,3},{2,0},{3,1},{4,6},{5,7},{6,4},{7,5},{8,10},{9,11},{10,... | collective-permute-start | bytes 442376 | tf_op jit(solution)/shard_map/ppermute | solution.py:241
  33.8 8.0 %collective-permute-start.6 = (bf16[64,1152]{1,0:T(8,128)(2,1)S(1)}, bf16[64,1152]{1,0:T(8,128)(2,1)S(1)}, u32[]{:S(2)}, u32[]{:S(2)}) collective-permute-start(bf16[64,1152]{1,0:T(8,128)(2,1)S(1)} %fusion.8), channel_id=1, source_target_pairs={{0,4},{1,5},{2,6},{3,7},{4,0},{5,1},{6,2},{7,3},{8,12},{9,13},{10,... | collective-permute-start | bytes 442376 | tf_op jit(solution)/shard_map/ppermute | solution.py:241
  41.9 5.2 %collective-permute-start.7 = (bf16[64,1152]{1,0:T(8,128)(2,1)S(1)}, bf16[64,1152]{1,0:T(8,128)(2,1)S(1)}, u32[]{:S(2)}, u32[]{:S(2)}) collective-permute-start(bf16[64,1152]{1,0:T(8,128)(2,1)S(1)} %add_convert_fusion), channel_id=1, source_target_pairs={{0,2},{1,3},{2,0},{3,1},{4,6},{5,7},{6,4},{7,5},{8,10},{9,11},{10,... | collective-permute-start | bytes 442376 | tf_op jit(solution)/shard_map/ppermute | solution.py:241
  47.2 9.4 %collective-permute-start.9 = (bf16[1,128,1152]{2,1,0:T(8,128)(2,1)S(1)}, bf16[1,128,1152]{2,1,0:T(8,128)(2,1)S(1)}, u32[]{:S(2)}, u32[]{:S(2)}) collective-permute-start(bf16[1,128,1152]{2,1,0:T(8,128)(2,1)S(1)} %maximum_bitcast_fusion.own_ref), channel_id=1, source_target_pairs={{0,16},{1,9},{2,18},{3,11},{4,20},{5,13},{6,22},{7,15},{8,24},{9,1... | collective-permute-start | bytes 884744 | tf_op jit(solution)/shard_map/ppermute | solution.py:249
  48.5 10.0 %collective-permute-start.8 = (bf16[1,128,1152]{2,1,0:T(8,128)(2,1)S(1)}, bf16[1,128,1152]{2,1,0:T(8,128)(2,1)S(1)}, u32[]{:S(2)}, u32[]{:S(2)}) collective-permute-start(bf16[1,128,1152]{2,1,0:T(8,128)(2,1)S(1)} %maximum_bitcast_fusion.own_ref), channel_id=1, source_target_pairs={{0,8},{1,17},{2,10},{3,19},{4,12},{5,21},{6,14},{7,23},{8,0},{9,25... | collective-permute-start | bytes 884744 | tf_op jit(solution)/shard_map/ppermute | solution.py:249
  56.6 6.7 %collective-permute-start.10 = (bf16[1,128,1152]{2,1,0:T(8,128)(2,1)S(1)}, bf16[1,128,1152]{2,1,0:T(8,128)(2,1)S(1)}, u32[]{:S(2)}, u32[]{:S(2)}) collective-permute-start(bf16[1,128,1152]{2,1,0:T(8,128)(2,1)S(1)} %collective-permute-done.9.own_ref), channel_id=1, source_target_pairs={{0,8},{1,17},{2,10},{3,19},{4,12},{5,21},{6,14},{7,23},{8,0},{9,25... | collective-permute-start | bytes 884744 | tf_op jit(solution)/shard_map/ppermute | solution.py:249
  63.4 9.9 %collective-permute-start.11 = (bf16[2,128,1152]{2,1,0:T(8,128)(2,1)S(1)}, bf16[2,128,1152]{2,1,0:T(8,128)(2,1)S(1)}, u32[]{:S(2)}, u32[]{:S(2)}) collective-permute-start(bf16[2,128,1152]{2,1,0:T(8,128)(2,1)S(1)} %constant_dynamic-update-slice_fusion.own_ref), channel_id=1, source_target_pairs={{0,1},{1,0},{2,3},{3,2},{4,5},{5,4},{6,7},{7,6},{8,9},{9,8},{10,11... | collective-permute-start | bytes 1769480 | tf_op jit(solution)/shard_map/ppermute | solution.py:241
  63.4 2.4 %collective-permute-start.13 = (bf16[1,128,1152]{2,1,0:T(8,128)(2,1)S(1)}, bf16[1,128,1152]{2,1,0:T(8,128)(2,1)S(1)}, u32[]{:S(2)}, u32[]{:S(2)}) collective-permute-start(bf16[1,128,1152]{2,1,0:T(8,128)(2,1)S(1)} %maximum_bitcast_fusion.own_ref), channel_id=1, source_target_pairs={{0,1},{1,0},{2,3},{3,2},{4,5},{5,4},{6,7},{7,6},{8,9},{9,8},{10,11... | collective-permute-start | bytes 884744 | tf_op jit(solution)/shard_map/ppermute | solution.py:241
  63.9 6.7 %collective-permute-start.12 = (bf16[1,128,1152]{2,1,0:T(8,128)(2,1)S(1)}, bf16[1,128,1152]{2,1,0:T(8,128)(2,1)S(1)}, u32[]{:S(2)}, u32[]{:S(2)}) collective-permute-start(bf16[1,128,1152]{2,1,0:T(8,128)(2,1)S(1)} %collective-permute-done.9.own_ref), channel_id=1, source_target_pairs={{0,1},{1,0},{2,3},{3,2},{4,5},{5,4},{6,7},{7,6},{8,9},{9,8},{10,11... | collective-permute-start | bytes 884744 | tf_op jit(solution)/shard_map/ppermute | solution.py:241
  65.9 2.3 %copy-start = (bf16[1,4,256,2304]{3,2,1,0:T(8,128)(2,1)S(1)}, bf16[1,4,256,2304]{3,2,1,0:T(8,128)(2,1)}, u32[]{:S(2)}) copy-start(bf16[1,4,256,2304]{3,2,1,0:T(8,128)(2,1)} %param.9) | copy-start | bytes 14155780
  73.2 5.4 %copy-start.2 = (bf16[1,128,2304]{2,1,0:T(8,128)(2,1)S(1)}, bf16[1,128,2304]{2,1,0:T(8,128)(2,1)}, u32[]{:S(2)}) copy-start(bf16[1,128,2304]{2,1,0:T(8,128)(2,1)} %param.5) | copy-start | bytes 1769476

commit v2 on v0

v2 whole, which is shorter than its diff:
```python
import jax
import jax.numpy as jnp
from jax import lax
from jax.experimental import pallas as pl
from jax.experimental.pallas import tpu as pltpu
from jax.sharding import PartitionSpec as P

F32 = jnp.float32
BF16 = jnp.bfloat16
VMEM_LIMIT = 16 * 1024 * 1024
IN_VMEM = pl.BlockSpec(memory_space=pltpu.VMEM)
IN_PLACE = pl.BlockSpec(memory_space=pl.ANY)
IN_SMEM = pl.BlockSpec(memory_space=pltpu.SMEM)


def slot_offset(slot, core, bits):
    mirrored = 0
    for k in range(bits):
        mirrored = mirrored | (((slot >> k) & 1) << (bits - 1 - k))
    return jnp.where(core == 1, slot, mirrored)


def layer_bit(step, core, bits):
    return bits - 1 - step if core == 1 else step


def params():
    return dict(
        compiler_params=pltpu.CompilerParams(vmem_limit_bytes=VMEM_LIMIT),
        cost_estimate=pl.CostEstimate(flops=1, bytes_accessed=1, transcendentals=0),
    )


def in_hbm(value):
    return pltpu.with_memory_space_constraint(value, pltpu.HBM)


def in_vmem(value):
    return pltpu.with_memory_space_constraint(value, pltpu.VMEM)


def after(value, *others):
    return lax.optimization_barrier((value, *others))[0]


def weight_copies(pos, jobs, layers, wd_hbm, w_ref, sems):
    half = w_ref.shape[-1]
    bits = layers.bit_length() - 1
    copies, live = [], []
    for i, (slot, part) in enumerate(jobs):
        side = pos[1] if part == 0 else 1 - pos[1]
        target = pos[0] ^ slot_offset(slot, side, bits)
        cols = pl.ds(pl.multiple_of(side * half, half), half)
        copies.append(pltpu.make_async_copy(wd_hbm.at[target, :, cols], w_ref.at[i], sems.at[i]))
        live.append(target >= pos[0])
    return copies, live


def partial_sums(copies, live, act, w_ref, out_refs):
    for i, out_ref in enumerate(out_refs):
        copies[i].wait()

        @pl.when(live[i])
        def _():
            out_ref[...] = jnp.dot(act, w_ref[i], preferred_element_type=F32).astype(out_ref.dtype)

        @pl.when(jnp.logical_not(live[i]))
        def _():
            out_ref[...] = jnp.zeros_like(out_ref)


def job_shapes(jobs, toks, half):
    return [pltpu.VMEM((toks, half), F32 if part == 0 else BF16) for _, part in jobs]


def encode(pos, x, w_enc, b_enc, w_dec, jobs):
    layers, width, cols = w_dec.shape
    toks, half = x.shape[0], cols // 2
    pieces = 3 if cols % (3 * 128) == 0 else 1
    rows = cols // pieces

    def kernel(pos, x_hbm, we_hbm, b_hbm, wd_hbm, pre_ref, act_ref, act_t_ref, *refs):
        out_refs, (w_ref, x_ref, we_ref, b_ref, sems, w_sems) = refs[: len(jobs)], refs[len(jobs):]
        loads = [pltpu.make_async_copy(b_hbm, b_ref, sems.at[0])]
        for i in range(pieces):
            span = pl.ds(i * rows, rows)
            loads.append(pltpu.make_async_copy(x_hbm.at[:, span], x_ref.at[:, span], sems.at[2 * i + 1]))
            loads.append(pltpu.make_async_copy(we_hbm.at[span], we_ref.at[span], sems.at[2 * i + 2]))
        for load in loads:
            load.start()
        copies, live = weight_copies(pos, jobs, layers, wd_hbm, w_ref, w_sems)
        for copy in copies:
            copy.start()
        loads[0].wait()
        pre = jnp.broadcast_to(b_ref[...], (toks, width))
        for i in range(pieces):
            loads[2 * i + 1].wait()
            loads[2 * i + 2].wait()
            span = pl.ds(i * rows, rows)
            pre += jnp.dot(x_ref[:, span], we_ref[span], preferred_element_type=F32)
        pre_ref[...] = pre
        act = jnp.maximum(pre, 0.0).astype(BF16)
        act_ref[...] = act
        partial_sums(copies, live, act, w_ref, out_refs)
        act_t_ref[...] = act.T

    out = pl.pallas_call(
        kernel,
        in_specs=[IN_SMEM] + [IN_PLACE] * 4,
        out_specs=[IN_VMEM] * (3 + len(jobs)),
        out_shape=[
            pltpu.VMEM((toks, width), F32),
            pltpu.VMEM((toks, width), BF16),
            pltpu.VMEM((width, toks), BF16),
        ]
        + job_shapes(jobs, toks, half),
        scratch_shapes=[
            pltpu.VMEM((len(jobs), width, half), BF16),
            pltpu.VMEM(x.shape, BF16),
            pltpu.VMEM(w_enc.shape, BF16),
            pltpu.VMEM(b_enc.shape, F32),
            pltpu.SemaphoreType.DMA((2 * pieces + 1,)),
            pltpu.SemaphoreType.DMA((len(jobs),)),
        ],
        **params(),
    )(pos, in_hbm(x), in_hbm(w_enc), in_hbm(b_enc), in_hbm(w_dec))
    return out[0], out[1], out[2], dict(zip(jobs, out[3:]))


def decode(pos, act, w_dec, jobs):
    layers, width, cols = w_dec.shape
    toks, half = act.shape[0], cols // 2

    def kernel(pos, act_ref, wd_hbm, *refs):
        out_refs, (w_ref, w_sems) = refs[: len(jobs)], refs[len(jobs):]
        copies, live = weight_copies(pos, jobs, layers, wd_hbm, w_ref, w_sems)
        for copy in copies:
            copy.start()
        partial_sums(copies, live, act_ref[...], w_ref, out_refs)

    out = pl.pallas_call(
        kernel,
        in_specs=[IN_SMEM, IN_VMEM, IN_PLACE],
        out_specs=[IN_VMEM] * len(jobs),
        out_shape=job_shapes(jobs, toks, half),
        scratch_shapes=[
            pltpu.VMEM((len(jobs), width, half), BF16),
            pltpu.SemaphoreType.DMA((len(jobs),)),
        ],
        **params(),
    )(pos, in_vmem(act), in_hbm(w_dec))
    return dict(zip(jobs, out))


def backward(pos, slot, errs, act_t, w_dec, carry, last=None):
    layers, width, cols = w_dec.shape
    toks, half = errs[0].shape
    bits = layers.bit_length() - 1
    scale = toks ** (-0.5)
    ahead = slot == layers - 2

    def kernel(pos, *refs):
        err_refs, act_t_ref, wd_hbm, refs = refs[:2], refs[2], refs[3], refs[4:]
        if carry is not None:
            (old_ref, _), refs = refs[:2], refs[2:]
        if last is not None:
            (w_ref, x_ref, pre_ref), refs = refs[:3], refs[3:]
        sum_ref, grad_hbm, refs = refs[0], refs[1], refs[2:]
        if ahead:
            next_ref, refs = refs[0], refs[1:]
        if last is not None:
            (genc_hbm, gb_ref), refs = refs[:2], refs[2:]
        grad_ref, sems, refs = refs[0], refs[1], refs[2:]

        loads, writes, live, prefetch = [], [], [], []
        for part in range(2):
            side = pos[1] if part == 0 else 1 - pos[1]
            target = pos[0] ^ slot_offset(slot, side, bits)
            span = pl.ds(pl.multiple_of(side * half, half), half)
            writes.append(pltpu.make_async_copy(grad_ref.at[part], grad_hbm.at[target, :, span], sems.at[part]))
            live.append(target >= pos[0])
            if last is None:
                loads.append(pltpu.make_async_copy(wd_hbm.at[target, :, span], refs[0].at[part], refs[1].at[part]))
            if ahead:
                target = pos[0] ^ slot_offset(slot + 1, side, bits)
                prefetch.append(pltpu.make_async_copy(wd_hbm.at[target, :, span], next_ref.at[part], refs[1].at[2 + part]))
        if last is None:
            w_ref = refs[0]
        for copy in loads + prefetch:
            copy.start()

        def decoder_part(part):
            @pl.when(live[part])
            def _():
                grad = jnp.dot(act_t_ref[...], err_refs[part][...], preferred_element_type=F32)
                grad_ref[part] = (grad * scale).astype(BF16)

            @pl.when(jnp.logical_not(live[part]))
            def _():
                grad_ref[part] = jnp.zeros((width, half), BF16)

            writes[part].start()

        if last is None:
            decoder_part(0)
            decoder_part(1)
        sum_ref[...] = jnp.zeros_like(sum_ref) if carry is None else old_ref[...]
        for part in range(2):
            if loads:
                loads[part].wait()

            @pl.when(live[part])
            def _():
                sum_ref[...] += lax.dot_general(
                    err_refs[part][...], w_ref[part], (((1,), (1,)), ((), ())), preferred_element_type=F32
                )

        if last is not None:
            genc_ref, enc_sems = refs
            pre_grad = jnp.where(pre_ref[...] > 0, sum_ref[...] * scale, 0.0).astype(BF16)
            gb_ref[...] = jnp.sum(pre_grad.astype(F32), axis=0, keepdims=True)
            for i in range(2):
                span = pl.ds(i * half, half)
                genc_ref[span] = lax.dot_general(
                    x_ref[:, span], pre_grad, (((0,), (0,)), ((), ())), preferred_element_type=F32
                ).astype(BF16)
                write = pltpu.make_async_copy(genc_ref.at[span], genc_hbm.at[span], enc_sems.at[i])
                write.start()
                writes.append(write)
            decoder_part(0)
            decoder_part(1)
        for copy in prefetch + writes:
            copy.wait()

    in_specs = [IN_SMEM] + [IN_VMEM] * 3 + [IN_PLACE]
    args = [pos] + [in_vmem(a) for a in (*errs, act_t)] + [in_hbm(w_dec)]
    out_specs = [IN_VMEM, IN_PLACE]
    out_shape = [pltpu.VMEM((toks, width), F32), pltpu.HBM((layers, width, cols), BF16)]
    scratch = [pltpu.VMEM((2, width, half), BF16), pltpu.SemaphoreType.DMA((2,))]
    aliases = {}
    if carry is not None:
        in_specs += [IN_VMEM, IN_PLACE]
        args += [in_vmem(carry[0]), carry[1]]
        aliases = {len(args) - 1: 1}
    if ahead:
        out_specs += [IN_VMEM]
        out_shape += [pltpu.VMEM((2, width, half), BF16)]
    if last is None:
        scratch += [pltpu.VMEM((2, width, half), BF16), pltpu.SemaphoreType.DMA((4,))]
    else:
        in_specs += [IN_VMEM] * 3
        args += [in_vmem(a) for a in (carry[2], *last)]
        out_specs += [IN_PLACE, IN_VMEM]
        out_shape += [pltpu.HBM((cols, width), BF16), jax.ShapeDtypeStruct((1, width), F32)]
        scratch += [pltpu.VMEM((cols, width), BF16), pltpu.SemaphoreType.DMA((2,))]
    return pl.pallas_call(
        kernel,
        in_specs=in_specs,
        out_specs=out_specs,
        out_shape=out_shape,
        scratch_shapes=scratch,
        input_output_aliases=aliases,
        **params(),
    )(*args)


def add_up(values, dtype):
    def kernel(*refs):
        total = refs[0][...].astype(F32)
        for ref in refs[1:-1]:
            total += ref[...].astype(F32)
        refs[-1][...] = total.astype(dtype)

    return pl.pallas_call(
        kernel,
        in_specs=[IN_VMEM] * len(values),
        out_specs=IN_VMEM,
        out_shape=pltpu.VMEM(values[0].shape, dtype),
        **params(),
    )(*[in_vmem(v) for v in values])


def split_rows(high, minus, values):
    toks, cols = minus.shape
    n = toks // 2

    def kernel(high, minus_ref, *refs):
        def rows(start):
            span = pl.ds(pl.multiple_of(start, n), n)
            total = -minus_ref[span].astype(F32)
            for ref in refs[:-2]:
                total += ref[span].astype(F32)
            return total

        refs[-1][...] = rows((1 - high[0]) * n).astype(BF16)
        refs[-2][...] = rows(high[0] * n)

    return pl.pallas_call(
        kernel,
        in_specs=[IN_SMEM] + [IN_VMEM] * (1 + len(values)),
        out_specs=[IN_VMEM] * 2,
        out_shape=[pltpu.VMEM((n, cols), F32), pltpu.VMEM((n, cols), BF16)],
        **params(),
    )(high, *[in_vmem(v) for v in (minus, *values)])


def shards(inputs, targets, w_enc, b_enc, w_dec):
    layers, cols = w_dec.shape[1], w_dec.shape[3]
    feats = lax.axis_size("feat")
    bits, feat_bits = layers.bit_length() - 1, feats.bit_length() - 1
    half = cols // 2
    own_layer, own_feat = lax.axis_index("layer"), lax.axis_index("feat")
    core = own_feat & 1
    pos = jnp.stack([own_layer, core]).astype(jnp.int32)
    x, tgt, wd = inputs[0], targets[0], w_dec[0]

    def swap_feat(value, bit):
        return lax.ppermute(value, "feat", [(f, f ^ (1 << bit)) for f in range(feats)])

    def swap_layer(value, step):
        pairs = [
            (l * feats + f, (l ^ (1 << layer_bit(step, f & 1, bits))) * feats + f)
            for l in range(layers)
            for f in range(feats)
        ]
        return lax.ppermute(value, ("layer", "feat"), pairs)

    def jobs(low, high):
        return [(s, part) for s in reversed(range(low, high)) for part in (1, 0)]

    mid = layers // 2
    pre, act, act_t, sums = encode(pos, x, w_enc[0], b_enc, wd, jobs(layers - 1, layers))
    got = {layers - 1: swap_feat(sums[layers - 1, 1], 0)}
    sums |= decode(pos, act, wd, jobs(mid, layers - 1))
    for s in reversed(range(mid, layers - 1)):
        got[s] = swap_feat(sums[s, 1], 0)
    away = add_up([after(sums[layers - 1, 0], *[sums[j] for j in jobs(mid, layers - 1)]), got[layers - 1]], BF16)
    arrived = {layers - 1 - mid: swap_layer(away, 0)}
    sums |= decode(pos, after(act, away), wd, jobs(0, mid))
    for s in reversed(range(mid)):
        got[s] = swap_feat(sums[s, 1], 0)
    tgt = after(tgt, away)
    for s in reversed(range(mid, layers - 1)):
        away = add_up([after(sums[s, 0], sums[0, 0]), got[s]], BF16)
        arrived[s - mid] = swap_layer(away, 0)
    slots = [[sums[s, 0], got[s], arrived[s]] for s in range(mid)]
    for step in range(1, bits):
        n = len(slots) // 2
        for s in reversed(range(n)):
            slots[s].append(swap_layer(add_up(slots[n + s], BF16), step))
        slots = slots[:n]

    pair_tgt = swap_feat(tgt, 0)
    pair = jnp.where(core == 0, jnp.stack([tgt, pair_tgt]), jnp.stack([pair_tgt, tgt]))
    pair = jnp.concatenate([pair[0], pair[1]], axis=1)
    span = pair.shape[1]
    chip, chips = own_feat >> 1, feats // 2
    spread = jnp.zeros((x.shape[0], half), BF16)
    for i in range(chips // 2):
        padded = jnp.pad(pair, ((0, 0), (i * span, half - (i + 1) * span)))
        spread = jnp.where(chip == core * (chips // 2) + i, padded, spread)

    for bit in range(1, feat_bits - 1):
        high = (own_feat >> bit) & 1
        if bit == 1:
            rows, away = split_rows(high.reshape(1), spread, slots[0])
        else:
            n = rows.shape[0] // 2
            away = jnp.where(high == 1, rows[:n], rows[n:]).astype(BF16)
            rows = jnp.where(high == 1, rows[n:], rows[:n])
        rows = rows + swap_feat(away, bit).astype(F32)
    rows = rows + swap_feat(rows.astype(BF16), feat_bits - 1).astype(F32)
    err = rows.astype(BF16)

    for bit in reversed(range(1, feat_bits - 1)):
        high = ((own_feat >> bit) & 1) == 1
        far = swap_feat(err, bit)
        err = jnp.concatenate([jnp.where(high, far, err), jnp.where(high, err, far)])

    other = swap_feat(err, 0)
    carry = backward(pos, 0, (err, other), act_t, wd, None)
    slots = [err]
    for step in reversed(range(bits)):
        for s in range(len(slots)):
            value = slots[s]
            if step == 0 and s == 0:
                value = after(value, other)
            elif step == 0 and s == 1:
                value = after(value, carry[0])
            slots.append(swap_layer(value, step))
    for s in range(1, layers):
        own = slots[s]
        if s < layers // 2 + 1:
            own = after(own, slots[layers // 2])
        elif s == layers - 1:
            own = after(own, carry[0])
        last = (x, pre) if s == layers - 1 else None
        carry = backward(pos, s, (own, swap_feat(own, 0)), act_t, wd, carry, last)
    act_sum, grad_dec, grad_enc, grad_benc = carry
    return grad_enc[None], grad_dec[None], grad_benc


def solution(mesh):
    in_specs = (
        P("layer", None, None),
        P("layer", None, "feat"),
        P("layer", None, "feat"),
        P("layer", "feat"),
        P("layer", None, "feat", None),
    )
    out_specs = (P("layer", None, "feat"), P("layer", None, "feat", None), P("layer", "feat"))
    return jax.shard_map(shards, mesh=mesh, in_specs=in_specs, out_specs=out_specs, check_vma=False)
```

time: 208 us -> 66.9 us (0.32)
  waiting for transfers between devices: 146 us -> 32.4 us
  Pallas kernels: 0 us -> 20.2 us
  blocking collectives: 16 us -> 0 us
  matrix products: 15 us -> 0 us
  local copies, waits for them, and re-layouts: 14.8 us -> 0.15 us
  between operations: 14.1 us -> 0.82 us
  starting transfers between devices: 0.08 us -> 12.6 us
    reduce_scatter x1 -> x0, waiting for transfers between devices: 110 us -> none  [shards(): lax.psum_scatter(partials, ('layer', 'feat'), scatter_dimension=0, tiled=...]
    all_gather x1 -> x0, waiting for transfers between devices: 36.7 us -> none  [shards(): lax.all_gather(err_rows, 'layer', axis=0, tiled=True)]
    ppermute x0 -> x18, waiting for transfers between devices: none -> 32.4 us  [the longest x12 20.4 us: swap_feat(): lax.ppermute(value, 'feat', [(f, f ^ 1 << bit) for f in range(feats)])]
    pallas_call x0 -> x11, Pallas kernels: none -> 20.2 us  [the longest x4 12 us: backward(): pl.pallas_call(kernel, in_specs=in_specs, out_specs=out_specs, out_shape=...]
    all_gather x1 -> x0, blocking collectives: 16 us -> none  [shards(): err_rows = lax.all_gather(err_block, 'feat', axis=1, tiled=True)]
    dot_general x5 -> x0, matrix products: 15 us -> none  [the longest x1 5.86 us: shards(): jnp.einsum('tf,mfnc->mntc', active, blocks, preferred_element_type=jnp.fl...]
    unnamed x13 -> x5, local copies, waits for them, and re-layouts: 14.8 us -> 0.13 us
    ppermute x0 -> x18, starting transfers between devices: none -> 12.6 us  [the longest x12 7.39 us: swap_feat(): lax.ppermute(value, 'feat', [(f, f ^ 1 << bit) for f in range(feats)])]
  transfers between devices with their start and end apart: 2 -> 18, of which waited for: 2 -> 12; matrix products, arithmetic and copies ran while one was open for 0% -> 1% of each run, Pallas kernels for 0% -> 20%
where the time goes in v2:
time: 66.9 us; the launch traced here: 66.6 us
  waiting for transfers between devices  32.4 us (48%)
  Pallas kernels  20.2 us (30%)
  starting transfers between devices  12.6 us (19%)
  between operations  0.82 us (1%)
    ppermute x12, waiting for transfers between devices, swap_feat(): lax.ppermute(value, 'feat', [(f, f ^ 1 << bit) for f in range(feats)])  20.4 us
    pallas_call x4, Pallas kernels, backward(): pl.pallas_call(kernel, in_specs=in_specs, out_specs=out_specs, out_shape=...  12 us
    ppermute x6, waiting for transfers between devices, swap_layer(): return lax.ppermute(value, ('layer', 'feat'), pairs)  11.9 us
    ppermute x12, starting transfers between devices, swap_feat(): lax.ppermute(value, 'feat', [(f, f ^ 1 << bit) for f in range(feats)])  7.39 us
    ppermute x6, starting transfers between devices, swap_layer(): return lax.ppermute(value, ('layer', 'feat'), pairs)  5.24 us
    pallas_call x2, Pallas kernels, decode(): pl.pallas_call(kernel, in_specs=[IN_SMEM, IN_VMEM, IN_PLACE], out_specs=[...  4.84 us
    pallas_call x1, Pallas kernels, encode(): pl.pallas_call(kernel, in_specs=[IN_SMEM] + [IN_PLACE] * 4, out_specs=[IN...  2.93 us
  transfers between devices with their start and end apart: 18, of which 12 were waited for; matrix products, arithmetic and copies ran while one was open for 1% of the time, Pallas kernels for 20%

profile of v2, /device:TPU:0, one launch (start us, length us, event | category | flops | bytes accessed | tf_op | source)
XLA Modules:
  0.0 66.6 jit_solution(11905444909695380500)
XLA Ops:
  0.7 2.9 %shard_map.76 = (f32[128,256]{1,0:T(8,128)S(1)}, bf16[128,256]{1,0:T(8,128)(2,1)S(1)}, bf16[256,128]{1,0:T(8,128)(2,1)S(1)}, bf16[128,1152]{1,0:T(8,128)(2,1)S(1)}, f32[128,1152]{1,0:T(8,128)S(1)}) custom-call(s32[2]{0:T(128)S(1)} %pad_add_fusion.pos, bf16[128,2304]{1,0:T(8,128)(2,1)} %bitcast.15, bf16[2304,256]{1,0:T(8,128)(2,1)} %bitcast.25, ...), custom_call_target="tpu_custom_call" | custom-call | flops 1 | bytes 1 | tf_op jit(solution)/shard_map/pallas_call | solution.py:107
  3.6 0.5 collective-permute-start
  4.2 2.1 %shard_map.77 = (bf16[128,1152]{1,0:T(8,128)(2,1)S(1)}, f32[128,1152]{1,0:T(8,128)S(1)}) custom-call(s32[2]{0:T(128)S(1)} %pad_add_fusion.pos, bf16[128,256]{1,0:T(8,128)(2,1)S(1)} %get-tuple-element.42.act_ref, bf16[4,256,2304]{2,1,0:T(8,128)(2,1)} %bitcast.18), custom_call_target="tpu_custom_call" | custom-call | flops 1 | bytes 1 | tf_op jit(solution)/shard_map/pallas_call | solution.py:141
  6.3 0.1 collective-permute-start.3
  6.6 0.5 collective-permute-start.1
  7.2 2.5 %collective-permute-start.6 = (bf16[128,1152]{1,0:T(8,128)(2,1)S(1)}, bf16[128,1152]{1,0:T(8,128)(2,1)S(1)}, u32[]{:S(2)}, u32[]{:S(2)}) collective-permute-start(bf16[128,1152]{1,0:T(8,128)(2,1)S(1)} %shard_map.78), channel_id=1, source_target_pairs={{0,8},{1,17},{2,10},{3,19},{4,12},{5,21},{6,14},{7,23},{8,0},{9,25... | collective-permute-start | bytes 884744 | tf_op jit(solution)/shard_map/ppermute | solution.py:326
  9.7 2.7 %shard_map.79 = (bf16[128,1152]{1,0:T(8,128)(2,1)S(1)}, f32[128,1152]{1,0:T(8,128)S(1)}, bf16[128,1152]{1,0:T(8,128)(2,1)S(1)}, f32[128,1152]{1,0:T(8,128)S(1)}) custom-call(s32[2]{0:T(128)S(1)} %pad_add_fusion.pos, bf16[128,256]{1,0:T(8,128)(2,1)S(1)} %get-tuple-element.42.act_ref, bf16[4,256,2304]{2,1,0:T(8,128)(2,1)} %bitcast.19), custom_call_target="tpu_custom_call" | custom-call | flops 1 | bytes 1 | tf_op jit(solution)/shard_map/pallas_call | solution.py:141
  12.6 0.5 collective-permute-start.5
  13.2 1.2 %collective-permute-done.6.refs_2_ = bf16[128,1152]{1,0:T(8,128)(2,1)S(1)} collective-permute-done((bf16[128,1152]{1,0:T(8,128)(2,1)S(1)}, bf16[128,1152]{1,0:T(8,128)(2,1)S(1)}, u32[]{:S(2)}, u32[]{:S(2)}) %collective-permute-start.6) | collective-permute-done | bytes 294944 | tf_op jit(solution)/shard_map/ppermute | solution.py:326
  14.4 0.2 collective-permute-done.5.refs_1_
  14.7 1.5 %collective-permute-start.7 = (bf16[128,1152]{1,0:T(8,128)(2,1)S(1)}, bf16[128,1152]{1,0:T(8,128)(2,1)S(1)}, u32[]{:S(2)}, u32[]{:S(2)}) collective-permute-start(bf16[128,1152]{1,0:T(8,128)(2,1)S(1)} %shard_map.81), channel_id=1, source_target_pairs={{0,16},{1,9},{2,18},{3,11},{4,20},{5,13},{6,22},{7,15},{8,24},{9,1... | collective-permute-start | bytes 884744 | tf_op jit(solution)/shard_map/ppermute | solution.py:326
  16.4 4.3 %collective-permute-done.4.refs_2_ = bf16[128,1152]{1,0:T(8,128)(2,1)S(1)} collective-permute-done((bf16[128,1152]{1,0:T(8,128)(2,1)S(1)}, bf16[128,1152]{1,0:T(8,128)(2,1)S(1)}, u32[]{:S(2)}, u32[]{:S(2)}) %collective-permute-start.4) | collective-permute-done | bytes 294944 | tf_op jit(solution)/shard_map/ppermute | solution.py:326
  20.7 0.8 %collective-permute-done.7.refs_3_ = bf16[128,1152]{1,0:T(8,128)(2,1)S(1)} collective-permute-done((bf16[128,1152]{1,0:T(8,128)(2,1)S(1)}, bf16[128,1152]{1,0:T(8,128)(2,1)S(1)}, u32[]{:S(2)}, u32[]{:S(2)}) %collective-permute-start.7) | collective-permute-done | bytes 294944 | tf_op jit(solution)/shard_map/ppermute | solution.py:326
  21.5 0.2 shard_map.82
  21.7 2.1 %collective-permute-start.8 = (bf16[64,1152]{1,0:T(8,128)(2,1)S(1)}, bf16[64,1152]{1,0:T(8,128)(2,1)S(1)}, u32[]{:S(2)}, u32[]{:S(2)}) collective-permute-start(bf16[64,1152]{1,0:T(8,128)(2,1)S(1)} %get-tuple-element.49), channel_id=1, source_target_pairs={{0,2},{1,3},{2,0},{3,1},{4,6},{5,7},{6,4},{7,5},{8,10},{9,11},{10,... | collective-permute-start | bytes 442376 | tf_op jit(solution)/shard_map/ppermute | solution.py:318
  23.8 4.5 %collective-permute-done.8 = bf16[64,1152]{1,0:T(8,128)(2,1)S(1)} collective-permute-done((bf16[64,1152]{1,0:T(8,128)(2,1)S(1)}, bf16[64,1152]{1,0:T(8,128)(2,1)S(1)}, u32[]{:S(2)}, u32[]{:S(2)}) %collective-permute-start.8) | collective-permute-done | bytes 147488 | tf_op jit(solution)/shard_map/ppermute | solution.py:318
  28.3 2.7 %collective-permute-start.9 = (bf16[64,1152]{1,0:T(8,128)(2,1)S(1)}, bf16[64,1152]{1,0:T(8,128)(2,1)S(1)}, u32[]{:S(2)}, u32[]{:S(2)}) collective-permute-start(bf16[64,1152]{1,0:T(8,128)(2,1)S(1)} %fusion), channel_id=1, source_target_pairs={{0,4},{1,5},{2,6},{3,7},{4,0},{5,1},{6,2},{7,3},{8,12},{9,13},{10,... | collective-permute-start | bytes 442376 | tf_op jit(solution)/shard_map/ppermute | solution.py:318
  30.9 7.1 %collective-permute-done.9 = bf16[64,1152]{1,0:T(8,128)(2,1)S(1)} collective-permute-done((bf16[64,1152]{1,0:T(8,128)(2,1)S(1)}, bf16[64,1152]{1,0:T(8,128)(2,1)S(1)}, u32[]{:S(2)}, u32[]{:S(2)}) %collective-permute-start.9) | collective-permute-done | bytes 147488 | tf_op jit(solution)/shard_map/ppermute | solution.py:318
  38.1 0.3 collective-permute-start.10
  38.4 4.9 %collective-permute-done.10 = bf16[64,1152]{1,0:T(8,128)(2,1)S(1)} collective-permute-done((bf16[64,1152]{1,0:T(8,128)(2,1)S(1)}, bf16[64,1152]{1,0:T(8,128)(2,1)S(1)}, u32[]{:S(2)}, u32[]{:S(2)}) %collective-permute-start.10) | collective-permute-done | bytes 147488 | tf_op jit(solution)/shard_map/ppermute | solution.py:318
  43.4 1.6 %collective-permute-done.12.refs_1_ = bf16[128,1152]{1,0:T(8,128)(2,1)S(1)} collective-permute-done((bf16[128,1152]{1,0:T(8,128)(2,1)S(1)}, bf16[128,1152]{1,0:T(8,128)(2,1)S(1)}, u32[]{:S(2)}, u32[]{:S(2)}) %collective-permute-start.12) | collective-permute-done | bytes 294944 | tf_op jit(solution)/shard_map/ppermute | solution.py:318
  45.0 0.7 %collective-permute-start.11 = (bf16[128,1152]{1,0:T(8,128)(2,1)S(1)}, bf16[128,1152]{1,0:T(8,128)(2,1)S(1)}, u32[]{:S(2)}, u32[]{:S(2)}) collective-permute-start(bf16[128,1152]{1,0:T(8,128)(2,1)S(1)} %pad_maximum_fusion.refs_0_), channel_id=1, source_target_pairs={{0,16},{1,9},{2,18},{3,11},{4,20},{5,13},{6,22},{7,15},{8,24},{9,1... | collective-permute-start | bytes 884744 | tf_op jit(solution)/shard_map/ppermute | solution.py:326
  45.7 3.3 %shard_map.83 = (f32[128,256]{1,0:T(8,128)S(1)}, bf16[4,256,2304]{2,1,0:T(8,128)(2,1)}) custom-call(s32[2]{0:T(128)S(1)} %pad_add_fusion.pos, bf16[128,1152]{1,0:T(8,128)(2,1)S(1)} %pad_maximum_fusion.refs_0_, bf16[128,1152]{1,0:T(8,128)(2,1)S(1)} %collective-permute-done.12.refs_1_, bf16[256,128]{1,0:T(8,128)(2,1)S(1)} %get-tuple-element.50.refs_2_, ...), custom_call_target="tpu_custom_call" | custom-call | flops 1 | bytes 1 | tf_op jit(solution)/shard_map/pallas_call | solution.py:256
  49.0 5.0 %collective-permute-done.14.refs_0_ = bf16[128,1152]{1,0:T(8,128)(2,1)S(1)} collective-permute-done((bf16[128,1152]{1,0:T(8,128)(2,1)S(1)}, bf16[128,1152]{1,0:T(8,128)(2,1)S(1)}, u32[]{:S(2)}, u32[]{:S(2)}) %collective-permute-start.14) | collective-permute-done | bytes 294944 | tf_op jit(solution)/shard_map/ppermute | solution.py:326
  54.1 0.5 collective-permute-start.15
  54.6 0.5 collective-permute-start.13
  55.0 0.6 collective-permute-done.16.refs_1_
  55.6 2.3 %shard_map.84 = (f32[128,256]{1,0:T(8,128)S(1)}, bf16[4,256,2304]{2,1,0:T(8,128)(2,1)}) custom-call(s32[2]{0:T(128)S(1)} %pad_add_fusion.pos, bf16[128,1152]{1,0:T(8,128)(2,1)S(1)} %collective-permute-done.11.refs_0_, bf16[128,1152]{1,0:T(8,128)(2,1)S(1)} %collective-permute-done.16.refs_1_, ...), custom_call_target="tpu_custom_call", output_to_operand_aliasing={{1}: (6, {})} | custom-call | flops 1 | bytes 1 | tf_op jit(solution)/shard_map/pallas_call | solution.py:256
  58.0 2.6 %shard_map.85 = (f32[128,256]{1,0:T(8,128)S(1)}, bf16[4,256,2304]{2,1,0:T(8,128)(2,1)}, bf16[2,256,1152]{2,1,0:T(8,128)(2,1)S(1)}) custom-call(s32[2]{0:T(128)S(1)} %pad_add_fusion.pos, bf16[128,1152]{1,0:T(8,128)(2,1)S(1)} %collective-permute-done.14.refs_0_, ...), custom_call_target="tpu_custom_call", output_to_operand_aliasing={{1}: (6, {})} | custom-call | flops 1 | bytes 1 | tf_op jit(solution)/shard_map/pallas_call | solution.py:256
  60.6 0.6 collective-permute-done.13.refs_0_
  61.3 1.6 %collective-permute-done.17.refs_1_ = bf16[128,1152]{1,0:T(8,128)(2,1)S(1)} collective-permute-done((bf16[128,1152]{1,0:T(8,128)(2,1)S(1)}, bf16[128,1152]{1,0:T(8,128)(2,1)S(1)}, u32[]{:S(2)}, u32[]{:S(2)}) %collective-permute-start.17) | collective-permute-done | bytes 294944 | tf_op jit(solution)/shard_map/ppermute | solution.py:318
  62.9 3.7 %shard_map.86 = (f32[128,256]{1,0:T(8,128)}, bf16[4,256,2304]{2,1,0:T(8,128)(2,1)}, bf16[2304,256]{1,0:T(8,128)(2,1)}, f32[1,256]{1,0:T(1,128)}) custom-call(s32[2]{0:T(128)S(1)} %pad_add_fusion.pos, bf16[128,1152]{1,0:T(8,128)(2,1)S(1)} %collective-permute-done.13.refs_0_, ...), custom_call_target="tpu_custom_call", output_to_operand_aliasing={{1}: (6, {})} | custom-call | flops 1 | bytes 1 | tf_op jit(solution)/shard_map/pallas_call | solution.py:256
  (29 shorter events, 1.1 us)
Async XLA Ops:
  0.7 5.7 %copy-start.1 = (bf16[1,128,288]{1,2,0:T(8,128)(2,1)S(1)}, bf16[1,128,288]{1,2,0:T(8,128)(2,1)}, u32[]{:S(2)}) copy-start(bf16[1,128,288]{1,2,0:T(8,128)(2,1)} %param.6) | copy-start | bytes 221188
  3.6 2.9 %collective-permute-start = (bf16[128,1152]{1,0:T(8,128)(2,1)S(1)}, bf16[128,1152]{1,0:T(8,128)(2,1)S(1)}, u32[]{:S(2)}, u32[]{:S(2)}) collective-permute-start(bf16[128,1152]{1,0:T(8,128)(2,1)S(1)} %get-tuple-element.40), channel_id=1, source_target_pairs={{0,1},{1,0},{2,3},{3,2},{4,5},{5,4},{6,7},{7,6},{8,9},{9,8},{10,11... | collective-permute-start | bytes 884744 | tf_op jit(solution)/shard_map/ppermute | solution.py:318
  6.3 6.1 %collective-permute-start.3 = (bf16[128,1152]{1,0:T(8,128)(2,1)S(1)}, bf16[128,1152]{1,0:T(8,128)(2,1)S(1)}, u32[]{:S(2)}, u32[]{:S(2)}) collective-permute-start(bf16[128,1152]{1,0:T(8,128)(2,1)S(1)} %get-tuple-element.37), channel_id=1, source_target_pairs={{0,1},{1,0},{2,3},{3,2},{4,5},{5,4},{6,7},{7,6},{8,9},{9,8},{10,11... | collective-permute-start | bytes 884744 | tf_op jit(solution)/shard_map/ppermute | solution.py:318
  6.6 6.5 %collective-permute-start.1 = (bf16[128,288]{1,0:T(8,128)(2,1)S(1)}, bf16[128,288]{1,0:T(8,128)(2,1)S(1)}, u32[]{:S(2)}, u32[]{:S(2)}) collective-permute-start(bf16[128,288]{1,0:T(8,128)(2,1)S(1)} %bitcast.26), channel_id=1, source_target_pairs={{0,1},{1,0},{2,3},{3,2},{4,5},{5,4},{6,7},{7,6},{8,9},{9,8},{10,11... | collective-permute-start | bytes 221192 | tf_op jit(solution)/shard_map/ppermute | solution.py:318
  7.2 7.2 %collective-permute-start.6 = (bf16[128,1152]{1,0:T(8,128)(2,1)S(1)}, bf16[128,1152]{1,0:T(8,128)(2,1)S(1)}, u32[]{:S(2)}, u32[]{:S(2)}) collective-permute-start(bf16[128,1152]{1,0:T(8,128)(2,1)S(1)} %shard_map.78), channel_id=1, source_target_pairs={{0,8},{1,17},{2,10},{3,19},{4,12},{5,21},{6,14},{7,23},{8,0},{9,25... | collective-permute-start | bytes 884744 | tf_op jit(solution)/shard_map/ppermute | solution.py:326
  12.4 8.3 %collective-permute-start.4 = (bf16[128,1152]{1,0:T(8,128)(2,1)S(1)}, bf16[128,1152]{1,0:T(8,128)(2,1)S(1)}, u32[]{:S(2)}, u32[]{:S(2)}) collective-permute-start(bf16[128,1152]{1,0:T(8,128)(2,1)S(1)} %shard_map.80), channel_id=1, source_target_pairs={{0,8},{1,17},{2,10},{3,19},{4,12},{5,21},{6,14},{7,23},{8,0},{9,25... | collective-permute-start | bytes 884744 | tf_op jit(solution)/shard_map/ppermute | solution.py:326
  12.5 8.2 %collective-permute-start.2 = (bf16[128,1152]{1,0:T(8,128)(2,1)S(1)}, bf16[128,1152]{1,0:T(8,128)(2,1)S(1)}, u32[]{:S(2)}, u32[]{:S(2)}) collective-permute-start(bf16[128,1152]{1,0:T(8,128)(2,1)S(1)} %get-tuple-element.44), channel_id=1, source_target_pairs={{0,1},{1,0},{2,3},{3,2},{4,5},{5,4},{6,7},{7,6},{8,9},{9,8},{10,11... | collective-permute-start | bytes 884744 | tf_op jit(solution)/shard_map/ppermute | solution.py:318
  12.6 2.0 %collective-permute-start.5 = (bf16[128,1152]{1,0:T(8,128)(2,1)S(1)}, bf16[128,1152]{1,0:T(8,128)(2,1)S(1)}, u32[]{:S(2)}, u32[]{:S(2)}) collective-permute-start(bf16[128,1152]{1,0:T(8,128)(2,1)S(1)} %get-tuple-element.47), channel_id=1, source_target_pairs={{0,1},{1,0},{2,3},{3,2},{4,5},{5,4},{6,7},{7,6},{8,9},{9,8},{10,11... | collective-permute-start | bytes 884744 | tf_op jit(solution)/shard_map/ppermute | solution.py:318
  14.7 6.8 %collective-permute-start.7 = (bf16[128,1152]{1,0:T(8,128)(2,1)S(1)}, bf16[128,1152]{1,0:T(8,128)(2,1)S(1)}, u32[]{:S(2)}, u32[]{:S(2)}) collective-permute-start(bf16[128,1152]{1,0:T(8,128)(2,1)S(1)} %shard_map.81), channel_id=1, source_target_pairs={{0,16},{1,9},{2,18},{3,11},{4,20},{5,13},{6,22},{7,15},{8,24},{9,1... | collective-permute-start | bytes 884744 | tf_op jit(solution)/shard_map/ppermute | solution.py:326
  21.7 6.6 %collective-permute-start.8 = (bf16[64,1152]{1,0:T(8,128)(2,1)S(1)}, bf16[64,1152]{1,0:T(8,128)(2,1)S(1)}, u32[]{:S(2)}, u32[]{:S(2)}) collective-permute-start(bf16[64,1152]{1,0:T(8,128)(2,1)S(1)} %get-tuple-element.49), channel_id=1, source_target_pairs={{0,2},{1,3},{2,0},{3,1},{4,6},{5,7},{6,4},{7,5},{8,10},{9,11},{10,... | collective-permute-start | bytes 442376 | tf_op jit(solution)/shard_map/ppermute | solution.py:318
  28.3 9.7 %collective-permute-start.9 = (bf16[64,1152]{1,0:T(8,128)(2,1)S(1)}, bf16[64,1152]{1,0:T(8,128)(2,1)S(1)}, u32[]{:S(2)}, u32[]{:S(2)}) collective-permute-start(bf16[64,1152]{1,0:T(8,128)(2,1)S(1)} %fusion), channel_id=1, source_target_pairs={{0,4},{1,5},{2,6},{3,7},{4,0},{5,1},{6,2},{7,3},{8,12},{9,13},{10,... | collective-permute-start | bytes 442376 | tf_op jit(solution)/shard_map/ppermute | solution.py:318
  38.1 5.2 %collective-permute-start.10 = (bf16[64,1152]{1,0:T(8,128)(2,1)S(1)}, bf16[64,1152]{1,0:T(8,128)(2,1)S(1)}, u32[]{:S(2)}, u32[]{:S(2)}) collective-permute-start(bf16[64,1152]{1,0:T(8,128)(2,1)S(1)} %add_convert_fusion), channel_id=1, source_target_pairs={{0,2},{1,3},{2,0},{3,1},{4,6},{5,7},{6,4},{7,5},{8,10},{9,11},{10,... | collective-permute-start | bytes 442376 | tf_op jit(solution)/shard_map/ppermute | solution.py:318
  43.3 1.6 %collective-permute-start.12 = (bf16[128,1152]{1,0:T(8,128)(2,1)S(1)}, bf16[128,1152]{1,0:T(8,128)(2,1)S(1)}, u32[]{:S(2)}, u32[]{:S(2)}) collective-permute-start(bf16[128,1152]{1,0:T(8,128)(2,1)S(1)} %pad_maximum_fusion.refs_0_), channel_id=1, source_target_pairs={{0,1},{1,0},{2,3},{3,2},{4,5},{5,4},{6,7},{7,6},{8,9},{9,8},{10,11... | collective-permute-start | bytes 884744 | tf_op jit(solution)/shard_map/ppermute | solution.py:318
  45.0 9.1 %collective-permute-start.14 = (bf16[128,1152]{1,0:T(8,128)(2,1)S(1)}, bf16[128,1152]{1,0:T(8,128)(2,1)S(1)}, u32[]{:S(2)}, u32[]{:S(2)}) collective-permute-start(bf16[128,1152]{1,0:T(8,128)(2,1)S(1)} %pad_maximum_fusion.refs_0_), channel_id=1, source_target_pairs={{0,8},{1,17},{2,10},{3,19},{4,12},{5,21},{6,14},{7,23},{8,0},{9,25... | collective-permute-start | bytes 884744 | tf_op jit(solution)/shard_map/ppermute | solution.py:326
  45.0 9.1 %collective-permute-start.11 = (bf16[128,1152]{1,0:T(8,128)(2,1)S(1)}, bf16[128,1152]{1,0:T(8,128)(2,1)S(1)}, u32[]{:S(2)}, u32[]{:S(2)}) collective-permute-start(bf16[128,1152]{1,0:T(8,128)(2,1)S(1)} %pad_maximum_fusion.refs_0_), channel_id=1, source_target_pairs={{0,16},{1,9},{2,18},{3,11},{4,20},{5,13},{6,22},{7,15},{8,24},{9,1... | collective-permute-start | bytes 884744 | tf_op jit(solution)/shard_map/ppermute | solution.py:326
  54.0 1.6 %collective-permute-start.16 = (bf16[128,1152]{1,0:T(8,128)(2,1)S(1)}, bf16[128,1152]{1,0:T(8,128)(2,1)S(1)}, u32[]{:S(2)}, u32[]{:S(2)}) collective-permute-start(bf16[128,1152]{1,0:T(8,128)(2,1)S(1)} %collective-permute-done.11.refs_0_), channel_id=1, source_target_pairs={{0,1},{1,0},{2,3},{3,2},{4,5},{5,4},{6,7},{7,6},{8,9},{9,8},{10,11... | collective-permute-start | bytes 884744 | tf_op jit(solution)/shard_map/ppermute | solution.py:318
  54.1 3.9 %collective-permute-start.15 = (bf16[128,1152]{1,0:T(8,128)(2,1)S(1)}, bf16[128,1152]{1,0:T(8,128)(2,1)S(1)}, u32[]{:S(2)}, u32[]{:S(2)}) collective-permute-start(bf16[128,1152]{1,0:T(8,128)(2,1)S(1)} %collective-permute-done.14.refs_0_), channel_id=1, source_target_pairs={{0,1},{1,0},{2,3},{3,2},{4,5},{5,4},{6,7},{7,6},{8,9},{9,8},{10,11... | collective-permute-start | bytes 884744 | tf_op jit(solution)/shard_map/ppermute | solution.py:318
  54.6 6.7 %collective-permute-start.13 = (bf16[128,1152]{1,0:T(8,128)(2,1)S(1)}, bf16[128,1152]{1,0:T(8,128)(2,1)S(1)}, u32[]{:S(2)}, u32[]{:S(2)}) collective-permute-start(bf16[128,1152]{1,0:T(8,128)(2,1)S(1)} %collective-permute-done.11.refs_0_), channel_id=1, source_target_pairs={{0,8},{1,17},{2,10},{3,19},{4,12},{5,21},{6,14},{7,23},{8,0},{9,25... | collective-permute-start | bytes 884744 | tf_op jit(solution)/shard_map/ppermute | solution.py:326
  58.0 4.9 %copy-start = (bf16[1,128,2304]{2,1,0:T(8,128)(2,1)S(1)}, bf16[1,128,2304]{2,1,0:T(8,128)(2,1)}, u32[]{:S(2)}) copy-start(bf16[1,128,2304]{2,1,0:T(8,128)(2,1)} %param.5) | copy-start | bytes 1769476
  61.3 1.6 %collective-permute-start.17 = (bf16[128,1152]{1,0:T(8,128)(2,1)S(1)}, bf16[128,1152]{1,0:T(8,128)(2,1)S(1)}, u32[]{:S(2)}, u32[]{:S(2)}) collective-permute-start(bf16[128,1152]{1,0:T(8,128)(2,1)S(1)} %collective-permute-done.13.refs_0_), channel_id=1, source_target_pairs={{0,1},{1,0},{2,3},{3,2},{4,5},{5,4},{6,7},{7,6},{8,9},{9,8},{10,11... | collective-permute-start | bytes 884744 | tf_op jit(solution)/shard_map/ppermute | solution.py:318

commit v3 on v2

v3 whole, which is shorter than its diff:
```python
import jax
import jax.numpy as jnp
from jax import lax
from jax.experimental import pallas as pl
from jax.experimental.pallas import tpu as pltpu
from jax.sharding import PartitionSpec as P

F32 = jnp.float32
BF16 = jnp.bfloat16
VMEM_LIMIT = 16 * 1024 * 1024
IN_VMEM = pl.BlockSpec(memory_space=pltpu.VMEM)
IN_PLACE = pl.BlockSpec(memory_space=pl.ANY)
IN_SMEM = pl.BlockSpec(memory_space=pltpu.SMEM)


def slot_offset(slot, core, bits):
    mirrored = 0
    for k in range(bits):
        mirrored = mirrored | (((slot >> k) & 1) << (bits - 1 - k))
    return jnp.where(core == 1, slot, mirrored)


def layer_bit(step, core, bits):
    return bits - 1 - step if core == 1 else step


def params(cost=1):
    return dict(
        compiler_params=pltpu.CompilerParams(vmem_limit_bytes=VMEM_LIMIT),
        cost_estimate=pl.CostEstimate(flops=cost, bytes_accessed=1, transcendentals=0),
    )


def in_hbm(value):
    return pltpu.with_memory_space_constraint(value, pltpu.HBM)


def in_vmem(value):
    return pltpu.with_memory_space_constraint(value, pltpu.VMEM)


def after(value, *others):
    return lax.optimization_barrier((value, *others))[0]


def weight_copies(pos, jobs, layers, wd_hbm, w_ref, sems):
    half = w_ref.shape[-1]
    bits = layers.bit_length() - 1
    copies, live = [], []
    for i, (slot, part) in enumerate(jobs):
        side = pos[1] if part == 0 else 1 - pos[1]
        target = pos[0] ^ slot_offset(slot, side, bits)
        cols = pl.ds(pl.multiple_of(side * half, half), half)
        copies.append(pltpu.make_async_copy(wd_hbm.at[target, :, cols], w_ref.at[i], sems.at[i]))
        live.append(target >= pos[0])
    return copies, live


def partial_sums(copies, live, act, w_ref, out_refs):
    for i, out_ref in enumerate(out_refs):
        copies[i].wait()

        @pl.when(live[i])
        def _():
            out_ref[...] = jnp.dot(act, w_ref[i], preferred_element_type=F32).astype(out_ref.dtype)

        @pl.when(jnp.logical_not(live[i]))
        def _():
            out_ref[...] = jnp.zeros_like(out_ref)


def job_shapes(jobs, toks, half):
    return [pltpu.VMEM((toks, half), F32 if part == 0 else BF16) for _, part in jobs]


def encode(pos, x, w_enc, b_enc, w_dec, jobs):
    layers, width, cols = w_dec.shape
    toks, half = x.shape[0], cols // 2
    pieces = 3 if cols % (3 * 128) == 0 else 1
    rows = cols // pieces

    def kernel(pos, x_hbm, we_hbm, b_hbm, wd_hbm, pre_ref, act_ref, act_t_ref, *refs):
        out_refs, (w_ref, x_ref, we_ref, b_ref, sems, w_sems) = refs[: len(jobs)], refs[len(jobs):]
        loads = [pltpu.make_async_copy(b_hbm, b_ref, sems.at[0])]
        for i in range(pieces):
            span = pl.ds(i * rows, rows)
            loads.append(pltpu.make_async_copy(x_hbm.at[:, span], x_ref.at[:, span], sems.at[2 * i + 1]))
            loads.append(pltpu.make_async_copy(we_hbm.at[span], we_ref.at[span], sems.at[2 * i + 2]))
        for load in loads:
            load.start()
        copies, live = weight_copies(pos, jobs, layers, wd_hbm, w_ref, w_sems)
        for copy in copies:
            copy.start()
        loads[0].wait()
        pre = jnp.broadcast_to(b_ref[...], (toks, width))
        for i in range(pieces):
            loads[2 * i + 1].wait()
            loads[2 * i + 2].wait()
            span = pl.ds(i * rows, rows)
            pre += jnp.dot(x_ref[:, span], we_ref[span], preferred_element_type=F32)
        pre_ref[...] = pre
        act = jnp.maximum(pre, 0.0).astype(BF16)
        act_ref[...] = act
        partial_sums(copies, live, act, w_ref, out_refs)
        act_t_ref[...] = act.T

    out = pl.pallas_call(
        kernel,
        in_specs=[IN_SMEM] + [IN_PLACE] * 4,
        out_specs=[IN_VMEM] * (3 + len(jobs)),
        out_shape=[
            pltpu.VMEM((toks, width), F32),
            pltpu.VMEM((toks, width), BF16),
            pltpu.VMEM((width, toks), BF16),
        ]
        + job_shapes(jobs, toks, half),
        scratch_shapes=[
            pltpu.VMEM((len(jobs), width, half), BF16),
            pltpu.VMEM(x.shape, BF16),
            pltpu.VMEM(w_enc.shape, BF16),
            pltpu.VMEM(b_enc.shape, F32),
            pltpu.SemaphoreType.DMA((2 * pieces + 1,)),
            pltpu.SemaphoreType.DMA((len(jobs),)),
        ],
        **params(),
    )(pos, in_hbm(x), in_hbm(w_enc), in_hbm(b_enc), in_hbm(w_dec))
    return out[0], out[1], out[2], dict(zip(jobs, out[3:]))


def decode(pos, act, w_dec, jobs):
    layers, width, cols = w_dec.shape
    toks, half = act.shape[0], cols // 2

    def kernel(pos, act_ref, wd_hbm, *refs):
        out_refs, (w_ref, w_sems) = refs[: len(jobs)], refs[len(jobs):]
        copies, live = weight_copies(pos, jobs, layers, wd_hbm, w_ref, w_sems)
        for copy in copies:
            copy.start()
        partial_sums(copies, live, act_ref[...], w_ref, out_refs)

    out = pl.pallas_call(
        kernel,
        in_specs=[IN_SMEM, IN_VMEM, IN_PLACE],
        out_specs=[IN_VMEM] * len(jobs),
        out_shape=job_shapes(jobs, toks, half),
        scratch_shapes=[
            pltpu.VMEM((len(jobs), width, half), BF16),
            pltpu.SemaphoreType.DMA((len(jobs),)),
        ],
        **params(),
    )(pos, in_vmem(act), in_hbm(w_dec))
    return dict(zip(jobs, out))


def backward(pos, jobs, errs, act_t, w_dec, carry, weights=None, ahead=(), last=None, cost=1):
    layers, width, cols = w_dec.shape
    toks, half = errs[0].shape
    bits = layers.bit_length() - 1
    scale = toks ** (-0.5)
    count = len(jobs)
    pieces = 3 if cols % (3 * 128) == 0 else 1

    def kernel(pos, *refs):
        refs = list(refs)
        take = lambda n: [refs.pop(0) for _ in range(n)]
        err_refs, (act_t_ref, wd_hbm) = take(count), take(2)
        old_ref = take(2)[0] if carry is not None else None
        w_refs = take(count) if weights is not None else None
        x_ref, pre_ref = take(2) if last is not None else (None, None)
        sum_ref, grad_hbm = take(2)
        ahead_refs = take(len(ahead))
        genc_hbm, gb_ref = take(2) if last is not None else (None, None)
        grad_ref, grad_sems = take(2)
        load_ref, load_sems = take(2) if weights is None else (None, None)
        ahead_sems = take(1)[0] if ahead else None
        genc_ref, enc_sems = take(2) if last is not None else (None, None)

        def place(slot, part):
            side = pos[1] if part == 0 else 1 - pos[1]
            target = pos[0] ^ slot_offset(slot, side, bits)
            return target, pl.ds(pl.multiple_of(side * half, half), half)

        loads, writes, live, later = [], [], [], []
        for i, job in enumerate(jobs):
            target, span = place(*job)
            live.append(target >= pos[0])
            writes.append(pltpu.make_async_copy(grad_ref.at[i], grad_hbm.at[target, :, span], grad_sems.at[i]))
            if weights is None:
                loads.append(pltpu.make_async_copy(wd_hbm.at[target, :, span], load_ref.at[i], load_sems.at[i]))
        for i, job in enumerate(ahead):
            target, span = place(*job)
            later.append(pltpu.make_async_copy(wd_hbm.at[target, :, span], ahead_refs[i], ahead_sems.at[i]))
        for copy in loads + later:
            copy.start()
        if weights is None:
            w_refs = [load_ref.at[i] for i in range(count)]

        sum_ref[...] = jnp.zeros_like(sum_ref) if carry is None else old_ref[...]
        for i in range(count):

            @pl.when(live[i])
            def _():
                grad = jnp.dot(act_t_ref[...], err_refs[i][...], preferred_element_type=F32)
                grad_ref[i] = (grad * scale).astype(BF16)

            @pl.when(jnp.logical_not(live[i]))
            def _():
                grad_ref[i] = jnp.zeros((width, half), BF16)

            writes[i].start()
        for i in range(count):
            if weights is None:
                loads[i].wait()

            @pl.when(live[i])
            def _():
                sum_ref[...] += lax.dot_general(
                    err_refs[i][...], w_refs[i][...], (((1,), (1,)), ((), ())), preferred_element_type=F32
                )

        if last is not None:
            pre_grad = jnp.where(pre_ref[...] > 0, sum_ref[...] * scale, 0.0).astype(BF16)
            gb_ref[...] = jnp.sum(pre_grad.astype(F32), axis=0, keepdims=True)
            for i in range(pieces):
                span = pl.ds(i * (cols // pieces), cols // pieces)
                genc_ref[span] = lax.dot_general(
                    x_ref[:, span], pre_grad, (((0,), (0,)), ((), ())), preferred_element_type=F32
                ).astype(BF16)
                write = pltpu.make_async_copy(genc_ref.at[span], genc_hbm.at[span], enc_sems.at[i])
                write.start()
                writes.append(write)
        for copy in later + writes:
            copy.wait()

    in_specs = [IN_SMEM] + [IN_VMEM] * (count + 1) + [IN_PLACE]
    args = [pos] + [in_vmem(a) for a in (*errs, act_t)] + [in_hbm(w_dec)]
    out_specs = [IN_VMEM, IN_PLACE] + [IN_VMEM] * len(ahead)
    out_shape = [pltpu.VMEM((toks, width), F32), pltpu.HBM((layers, width, cols), BF16)]
    out_shape += [pltpu.VMEM((width, half), BF16)] * len(ahead)
    scratch = [pltpu.VMEM((count, width, half), BF16), pltpu.SemaphoreType.DMA((count,))]
    aliases = {}
    if carry is not None:
        in_specs += [IN_VMEM, IN_PLACE]
        args += [in_vmem(carry[0]), carry[1]]
        aliases = {len(args) - 1: 1}
    if weights is None:
        scratch += [pltpu.VMEM((count, width, half), BF16), pltpu.SemaphoreType.DMA((count,))]
    else:
        in_specs += [IN_VMEM] * count
        args += [in_vmem(a) for a in weights]
    if ahead:
        scratch += [pltpu.SemaphoreType.DMA((len(ahead),))]
    if last is not None:
        in_specs += [IN_VMEM] * 2
        args += [in_vmem(a) for a in last]
        out_specs += [IN_PLACE, IN_VMEM]
        out_shape += [pltpu.HBM((cols, width), BF16), jax.ShapeDtypeStruct((1, width), F32)]
        scratch += [pltpu.VMEM((cols, width), BF16), pltpu.SemaphoreType.DMA((pieces,))]
    return pl.pallas_call(
        kernel,
        in_specs=in_specs,
        out_specs=out_specs,
        out_shape=out_shape,
        scratch_shapes=scratch,
        input_output_aliases=aliases,
        **params(cost),
    )(*args)


def add_up(values, dtype, cost=1):
    def kernel(*refs):
        total = refs[0][...].astype(F32)
        for ref in refs[1:-1]:
            total += ref[...].astype(F32)
        refs[-1][...] = total.astype(dtype)

    return pl.pallas_call(
        kernel,
        in_specs=[IN_VMEM] * len(values),
        out_specs=IN_VMEM,
        out_shape=pltpu.VMEM(values[0].shape, dtype),
        **params(cost),
    )(*[in_vmem(v) for v in values])


def add_rows(high, parts, whole, pieces, dtype):
    n, cols = whole[0].shape[0] // 2, whole[0].shape[1]

    def kernel(high, *refs):
        rest = list(refs[len(whole):])
        for i, part in enumerate(parts):
            start = (high[0] if part == 0 else 1 - high[0]) * n
            total = jnp.zeros((n, cols), F32)
            for ref in refs[: len(whole)]:
                total += ref[pl.ds(pl.multiple_of(start, n), n)].astype(F32)
            for _ in pieces[i]:
                total += rest.pop(0)[...].astype(F32)
            refs[i - len(parts)][...] = total.astype(dtype)

    values = [*whole, *[p for group in pieces for p in group]]
    return pl.pallas_call(
        kernel,
        in_specs=[IN_SMEM] + [IN_VMEM] * len(values),
        out_specs=[IN_VMEM] * len(parts),
        out_shape=[pltpu.VMEM((n, cols), dtype)] * len(parts),
        **params(),
    )(high, *[in_vmem(v) for v in values])


def join_rows(high, kept, far, cost=1):
    n, cols = kept.shape

    def kernel(high, kept_ref, far_ref, out_ref):
        out_ref[pl.ds(pl.multiple_of(high[0] * n, n), n)] = kept_ref[...]
        out_ref[pl.ds(pl.multiple_of((1 - high[0]) * n, n), n)] = far_ref[...]

    return pl.pallas_call(
        kernel,
        in_specs=[IN_SMEM] + [IN_VMEM] * 2,
        out_specs=IN_VMEM,
        out_shape=pltpu.VMEM((2 * n, cols), kept.dtype),
        **params(cost),
    )(high, in_vmem(kept), in_vmem(far))


def shards(inputs, targets, w_enc, b_enc, w_dec):
    layers, cols = w_dec.shape[1], w_dec.shape[3]
    feats = lax.axis_size("feat")
    bits, feat_bits = layers.bit_length() - 1, feats.bit_length() - 1
    half = cols // 2
    own_layer, own_feat = lax.axis_index("layer"), lax.axis_index("feat")
    core = own_feat & 1
    pos = jnp.stack([own_layer, core]).astype(jnp.int32)
    x, tgt, wd = inputs[0], targets[0], w_dec[0]

    def swap_feat(value, bit):
        return lax.ppermute(value, "feat", [(f, f ^ (1 << bit)) for f in range(feats)])

    def swap_layer(value, step, cross=False):
        pairs = [
            (l * feats + f, (l ^ (1 << layer_bit(step, f & 1, bits))) * feats + (f ^ 2 if cross else f))
            for l in range(layers)
            for f in range(feats)
        ]
        return lax.ppermute(value, ("layer", "feat"), pairs)

    def jobs(low, high):
        return [(s, part) for s in reversed(range(low, high)) for part in (1, 0)]

    mid, final = layers // 2, layers - 1
    high = ((own_feat >> 1) & 1).reshape(1)
    pre, act, act_t, sums = encode(pos, x, w_enc[0], b_enc, wd, [(final, 1)])
    got = {final: swap_feat(sums[final, 1], 0)}
    sums |= decode(pos, act, wd, [(final, 0)] + [(s, 1) for s in reversed(range(mid, final))])
    for s in reversed(range(mid, final)):
        got[s] = swap_feat(sums[s, 1], 0)
    away = add_up([sums[final, 0], got[final]], BF16)
    slots = [[] for _ in range(mid)]
    slots[final - mid].append(swap_layer(away, 0))
    sums |= decode(pos, after(act, away), wd, [(s, 0) for s in reversed(range(mid, final))] + jobs(0, mid))
    for s in reversed(range(mid)):
        got[s] = swap_feat(sums[s, 1], 0)
        slots[s] += [sums[s, 0], got[s]]
    for s in range(mid, final):
        slots.append([after(sums[s, 0], sums[0, 0]), got[s]])
    tgt = after(tgt, away)
    rows = []
    for step in range(bits):
        n = layers >> (step + 1)
        for s in reversed(range(n)):
            if step == 0 and n + s == final:
                continue
            if s > 0:
                slots[s].append(swap_layer(add_up(slots[n + s], BF16), step))
            else:
                kept, away = add_rows(high, (0, 1), slots[n], ([], []), BF16)
                rows += [swap_layer(kept, step), swap_layer(away, step, cross=True)]

    pair_tgt = swap_feat(tgt, 0)
    pair = jnp.where(core == 0, jnp.stack([tgt, pair_tgt]), jnp.stack([pair_tgt, tgt]))
    pair = -jnp.concatenate([pair[0], pair[1]], axis=1)
    span = pair.shape[1]
    chip, chips = own_feat >> 1, feats // 2
    spread = jnp.zeros((x.shape[0], half), BF16)
    for i in range(chips // 2):
        padded = jnp.pad(pair, ((0, 0), (i * span, half - (i + 1) * span)))
        spread = jnp.where(chip == core * (chips // 2) + i, padded, spread)

    (away,) = add_rows(high, (1,), [*slots[0], spread], ([],), BF16)
    rows.append(swap_feat(away, 1))
    (rows,) = add_rows(high, (0,), [*slots[0], spread], (rows,), F32)
    for bit in range(2, feat_bits - 1):
        n = rows.shape[0] // 2
        upper = ((own_feat >> bit) & 1) == 1
        away = jnp.where(upper, rows[:n], rows[n:]).astype(BF16)
        rows = jnp.where(upper, rows[n:], rows[:n]) + swap_feat(away, bit).astype(F32)
    rows = rows + swap_feat(rows.astype(BF16), feat_bits - 1).astype(F32)
    err = rows.astype(BF16)
    for bit in reversed(range(2, feat_bits - 1)):
        upper = ((own_feat >> bit) & 1) == 1
        far = swap_feat(err, bit)
        err = jnp.concatenate([jnp.where(upper, far, err), jnp.where(upper, err, far)])

    near = [swap_layer(err, step) for step in reversed(range(bits))]
    cross = swap_layer(err, bits - 1, cross=True)
    far = swap_feat(err, 1)
    slots = [join_rows(high, err, far)]
    start = backward(pos, [(0, 0)], [slots[0]], act_t, wd, None)
    for i, step in enumerate(reversed(range(bits))):
        for s in range(len(slots)):
            if s > 0:
                slots.append(swap_layer(slots[s], step))
            elif i > 0:
                slots.append(join_rows(high, near[i], swap_layer(far, step)))
            else:
                slots.append(join_rows(high, near[i], after(cross, start[0]), 1))
    middle = [(0, 1)] + [(s, part) for s in range(1, final) for part in (0, 1)]
    errs = [slots[s] if part == 0 else swap_feat(slots[0] if s == 0 else slots[s], 0) for s, part in middle]
    *carry, w_own, w_other = backward(pos, middle, errs, act_t, wd, start, ahead=[(final, 0), (final, 1)])
    own = add_up([after(slots[final], carry[0])], BF16, 100000000000)
    other = swap_feat(own, 0)
    carry = backward(pos, [(final, 0)], [own], act_t, wd, carry, [w_own])
    carry = backward(pos, [(final, 1)], [other], act_t, wd, carry, [w_other], last=(x, pre))
    act_sum, grad_dec, grad_enc, grad_benc = carry
    return grad_enc[None], grad_dec[None], grad_benc


def solution(mesh):
    in_specs = (
        P("layer", None, None),
        P("layer", None, "feat"),
        P("layer", None, "feat"),
        P("layer", "feat"),
        P("layer", None, "feat", None),
    )
    out_specs = (P("layer", None, "feat"), P("layer", None, "feat", None), P("layer", "feat"))
    return jax.shard_map(shards, mesh=mesh, in_specs=in_specs, out_specs=out_specs, check_vma=False)
```

time: 66.9 us -> 59.7 us (0.89)
  waiting for transfers between devices: 32.4 us -> 15.8 us
  starting transfers between devices: 12.6 us -> 22.6 us
    ppermute x6 -> x10, starting transfers between devices: 5.24 us -> 16.2 us  [swap_layer(): return lax.ppermute(value, ('layer', 'feat'), pairs)]
    ppermute x12, waiting for transfers between devices: 20.4 us -> 11.5 us  [swap_feat(): lax.ppermute(value, 'feat', [(f, f ^ 1 << bit) for f in range(feats)])]
    ppermute x6 -> x10, waiting for transfers between devices: 11.9 us -> 4.27 us  [swap_layer(): return lax.ppermute(value, ('layer', 'feat'), pairs)]
    ppermute x12, starting transfers between devices: 7.39 us -> 6.34 us  [swap_feat(): lax.ppermute(value, 'feat', [(f, f ^ 1 << bit) for f in range(feats)])]
  transfers between devices with their start and end apart: 18 -> 22, of which waited for: 12 -> 7; matrix products, arithmetic and copies ran while one was open for 1% -> 1% of each run, Pallas kernels for 20% -> 23%
where the time goes in v3:
time: 59.7 us; the launch traced here: 59.4 us
  starting transfers between devices  22.6 us (38%)
  Pallas kernels  19.6 us (33%)
  waiting for transfers between devices  15.8 us (26%)
  between operations  0.87 us (1%)
    ppermute x10, starting transfers between devices, swap_layer(): return lax.ppermute(value, ('layer', 'feat'), pairs)  16.2 us
    ppermute x12, waiting for transfers between devices, swap_feat(): lax.ppermute(value, 'feat', [(f, f ^ 1 << bit) for f in range(feats)])  11.5 us
    pallas_call x4, Pallas kernels, backward(): pl.pallas_call(kernel, in_specs=in_specs, out_specs=out_specs, out_shape=...  11.4 us
    ppermute x12, starting transfers between devices, swap_feat(): lax.ppermute(value, 'feat', [(f, f ^ 1 << bit) for f in range(feats)])  6.34 us
    pallas_call x2, Pallas kernels, decode(): pl.pallas_call(kernel, in_specs=[IN_SMEM, IN_VMEM, IN_PLACE], out_specs=[...  5.1 us
    ppermute x10, waiting for transfers between devices, swap_layer(): return lax.ppermute(value, ('layer', 'feat'), pairs)  4.27 us
    pallas_call x1, Pallas kernels, encode(): pl.pallas_call(kernel, in_specs=[IN_SMEM] + [IN_PLACE] * 4, out_specs=[IN...  2.66 us
  transfers between devices with their start and end apart: 22, of which 7 were waited for; matrix products, arithmetic and copies ran while one was open for 1% of the time, Pallas kernels for 23%

profile of v3, /device:TPU:0, one launch (start us, length us, event | category | flops | bytes accessed | tf_op | source)
XLA Modules:
  0.0 59.4 jit_solution(3460761232410607357)
XLA Ops:
  0.7 2.7 %shard_map.76 = (f32[128,256]{1,0:T(8,128)S(1)}, bf16[128,256]{1,0:T(8,128)(2,1)S(1)}, bf16[256,128]{1,0:T(8,128)(2,1)S(1)}, bf16[128,1152]{1,0:T(8,128)(2,1)S(1)}) custom-call(s32[2]{0:T(128)S(1)} %pad_add_fusion.pos, bf16[128,2304]{1,0:T(8,128)(2,1)} %bitcast.15, bf16[2304,256]{1,0:T(8,128)(2,1)} %bitcast.25, f32[1,256]{1,0:T(1,128)} %b_hbm.1, ...), custom_call_target="tpu_custom_call" | custom-call | flops 1 | bytes 1 | tf_op jit(solution)/shard_map/pallas_call | solution.py:107
  3.4 0.5 collective-permute-start
  3.9 2.1 %shard_map.77 = (f32[128,1152]{1,0:T(8,128)S(1)}, bf16[128,1152]{1,0:T(8,128)(2,1)S(1)}) custom-call(s32[2]{0:T(128)S(1)} %pad_add_fusion.pos, bf16[128,256]{1,0:T(8,128)(2,1)S(1)} %get-tuple-element.37.act_ref, bf16[4,256,2304]{2,1,0:T(8,128)(2,1)} %bitcast.18), custom_call_target="tpu_custom_call" | custom-call | flops 1 | bytes 1 | tf_op jit(solution)/shard_map/pallas_call | solution.py:141
  6.0 0.1 collective-permute-start.3
  6.4 0.5 collective-permute-start.2
  6.9 2.5 %collective-permute-start.6 = (bf16[128,1152]{1,0:T(8,128)(2,1)S(1)}, bf16[128,1152]{1,0:T(8,128)(2,1)S(1)}, u32[]{:S(2)}, u32[]{:S(2)}) collective-permute-start(bf16[128,1152]{1,0:T(8,128)(2,1)S(1)} %shard_map.78), channel_id=1, source_target_pairs={{0,8},{1,17},{2,10},{3,19},{4,12},{5,21},{6,14},{7,23},{8,0},{9,25... | collective-permute-start | bytes 884744 | tf_op jit(solution)/shard_map/ppermute | solution.py:345
  9.4 3.0 %shard_map.79 = (f32[128,1152]{1,0:T(8,128)S(1)}, bf16[128,1152]{1,0:T(8,128)(2,1)S(1)}, f32[128,1152]{1,0:T(8,128)S(1)}, bf16[128,1152]{1,0:T(8,128)(2,1)S(1)}, f32[128,1152]{1,0:T(8,128)S(1)}) custom-call(s32[2]{0:T(128)S(1)} %pad_add_fusion.pos, bf16[128,256]{1,0:T(8,128)(2,1)S(1)} %get-tuple-element.37.act_ref, bf16[4,256,2304]{2,1,0:T(8,128)(2,1)} %bitcast.19), custom_call_target="tpu_custom_call" | custom-call | flops 1 | bytes 1 | tf_op jit(solution)/shard_map/pallas_call | solution.py:141
  12.5 3.0 %collective-permute-start.5 = (bf16[64,1152]{1,0:T(8,128)(2,1)S(1)}, bf16[64,1152]{1,0:T(8,128)(2,1)S(1)}, u32[]{:S(2)}, u32[]{:S(2)}) collective-permute-start(bf16[64,1152]{1,0:T(8,128)(2,1)S(1)} %get-tuple-element.45), channel_id=1, source_target_pairs={{0,10},{1,19},{2,8},{3,17},{4,14},{5,23},{6,12},{7,21},{8,2},{9,27... | collective-permute-start | bytes 442376 | tf_op jit(solution)/shard_map/ppermute | solution.py:345
  15.6 0.5 collective-permute-start.7
  16.4 0.7 %collective-permute-done.1.refs_1_ = bf16[128,1152]{1,0:T(8,128)(2,1)S(1)} collective-permute-done((bf16[128,1152]{1,0:T(8,128)(2,1)S(1)}, bf16[128,1152]{1,0:T(8,128)(2,1)S(1)}, u32[]{:S(2)}, u32[]{:S(2)}) %collective-permute-start.1) | collective-permute-done | bytes 294944 | tf_op jit(solution)/shard_map/ppermute | solution.py:337
  17.2 0.5 collective-permute-start.10
  17.8 0.9 %collective-permute-start.8 = (bf16[64,1152]{1,0:T(8,128)(2,1)S(1)}, bf16[64,1152]{1,0:T(8,128)(2,1)S(1)}, u32[]{:S(2)}, u32[]{:S(2)}) collective-permute-start(bf16[64,1152]{1,0:T(8,128)(2,1)S(1)} %get-tuple-element.48), channel_id=1, source_target_pairs={{0,16},{1,9},{2,18},{3,11},{4,20},{5,13},{6,22},{7,15},{8,24},{9,1... | collective-permute-start | bytes 442376 | tf_op jit(solution)/shard_map/ppermute | solution.py:345
  18.7 2.2 %collective-permute-start.9 = (bf16[64,1152]{1,0:T(8,128)(2,1)S(1)}, bf16[64,1152]{1,0:T(8,128)(2,1)S(1)}, u32[]{:S(2)}, u32[]{:S(2)}) collective-permute-start(bf16[64,1152]{1,0:T(8,128)(2,1)S(1)} %get-tuple-element.49), channel_id=1, source_target_pairs={{0,18},{1,11},{2,16},{3,9},{4,22},{5,15},{6,20},{7,13},{8,26},{9,3... | collective-permute-start | bytes 442376 | tf_op jit(solution)/shard_map/ppermute | solution.py:345
  20.9 3.0 %collective-permute-done.10.refs_7_ = bf16[64,1152]{1,0:T(8,128)(2,1)S(1)} collective-permute-done((bf16[64,1152]{1,0:T(8,128)(2,1)S(1)}, bf16[64,1152]{1,0:T(8,128)(2,1)S(1)}, u32[]{:S(2)}, u32[]{:S(2)}) %collective-permute-start.10) | collective-permute-done | bytes 147488 | tf_op jit(solution)/shard_map/ppermute | solution.py:337
  23.9 2.6 %collective-permute-done.9.refs_6_ = bf16[64,1152]{1,0:T(8,128)(2,1)S(1)} collective-permute-done((bf16[64,1152]{1,0:T(8,128)(2,1)S(1)}, bf16[64,1152]{1,0:T(8,128)(2,1)S(1)}, u32[]{:S(2)}, u32[]{:S(2)}) %collective-permute-start.9) | collective-permute-done | bytes 147488 | tf_op jit(solution)/shard_map/ppermute | solution.py:345
  26.6 0.1 shard_map.83
  26.7 2.7 %collective-permute-start.11 = (bf16[64,1152]{1,0:T(8,128)(2,1)S(1)}, bf16[64,1152]{1,0:T(8,128)(2,1)S(1)}, u32[]{:S(2)}, u32[]{:S(2)}) collective-permute-start(bf16[64,1152]{1,0:T(8,128)(2,1)S(1)} %convert_element_type.13), channel_id=1, source_target_pairs={{0,4},{1,5},{2,6},{3,7},{4,0},{5,1},{6,2},{7,3},{8,12},{9,13},{10,... | collective-permute-start | bytes 442376 | tf_op jit(solution)/shard_map/ppermute | solution.py:337
  29.4 6.1 %collective-permute-done.11 = bf16[64,1152]{1,0:T(8,128)(2,1)S(1)} collective-permute-done((bf16[64,1152]{1,0:T(8,128)(2,1)S(1)}, bf16[64,1152]{1,0:T(8,128)(2,1)S(1)}, u32[]{:S(2)}, u32[]{:S(2)}) %collective-permute-start.11) | collective-permute-done | bytes 147488 | tf_op jit(solution)/shard_map/ppermute | solution.py:337
  35.6 0.7 %collective-permute-start.14 = (bf16[64,1152]{1,0:T(8,128)(2,1)S(1)}, bf16[64,1152]{1,0:T(8,128)(2,1)S(1)}, u32[]{:S(2)}, u32[]{:S(2)}) collective-permute-start(bf16[64,1152]{1,0:T(8,128)(2,1)S(1)} %add_convert_fusion.kept_ref), channel_id=1, source_target_pairs={{0,2},{1,3},{2,0},{3,1},{4,6},{5,7},{6,4},{7,5},{8,10},{9,11},{10,... | collective-permute-start | bytes 442376 | tf_op jit(solution)/shard_map/ppermute | solution.py:337
  36.3 1.9 %collective-permute-start.13 = (bf16[64,1152]{1,0:T(8,128)(2,1)S(1)}, bf16[64,1152]{1,0:T(8,128)(2,1)S(1)}, u32[]{:S(2)}, u32[]{:S(2)}) collective-permute-start(bf16[64,1152]{1,0:T(8,128)(2,1)S(1)} %add_convert_fusion.kept_ref), channel_id=1, source_target_pairs={{0,18},{1,11},{2,16},{3,9},{4,22},{5,15},{6,20},{7,13},{8,26},{9,3... | collective-permute-start | bytes 442376 | tf_op jit(solution)/shard_map/ppermute | solution.py:345
  38.2 0.9 %collective-permute-start.12 = (bf16[64,1152]{1,0:T(8,128)(2,1)S(1)}, bf16[64,1152]{1,0:T(8,128)(2,1)S(1)}, u32[]{:S(2)}, u32[]{:S(2)}) collective-permute-start(bf16[64,1152]{1,0:T(8,128)(2,1)S(1)} %add_convert_fusion.kept_ref), channel_id=1, source_target_pairs={{0,16},{1,9},{2,18},{3,11},{4,20},{5,13},{6,22},{7,15},{8,24},{9,1... | collective-permute-start | bytes 442376 | tf_op jit(solution)/shard_map/ppermute | solution.py:345
  39.1 1.6 %collective-permute-start.18 = (bf16[64,1152]{1,0:T(8,128)(2,1)S(1)}, bf16[64,1152]{1,0:T(8,128)(2,1)S(1)}, u32[]{:S(2)}, u32[]{:S(2)}) collective-permute-start(bf16[64,1152]{1,0:T(8,128)(2,1)S(1)} %add_convert_fusion.kept_ref), channel_id=1, source_target_pairs={{0,8},{1,17},{2,10},{3,19},{4,12},{5,21},{6,14},{7,23},{8,0},{9,25... | collective-permute-start | bytes 442376 | tf_op jit(solution)/shard_map/ppermute | solution.py:345
  40.7 1.6 %collective-permute-done.14.far_ref = bf16[64,1152]{1,0:T(8,128)(2,1)S(1)} collective-permute-done((bf16[64,1152]{1,0:T(8,128)(2,1)S(1)}, bf16[64,1152]{1,0:T(8,128)(2,1)S(1)}, u32[]{:S(2)}, u32[]{:S(2)}) %collective-permute-start.14) | collective-permute-done | bytes 147488 | tf_op jit(solution)/shard_map/ppermute | solution.py:337
  42.3 1.5 %collective-permute-start.19 = (bf16[64,1152]{1,0:T(8,128)(2,1)S(1)}, bf16[64,1152]{1,0:T(8,128)(2,1)S(1)}, u32[]{:S(2)}, u32[]{:S(2)}) collective-permute-start(bf16[64,1152]{1,0:T(8,128)(2,1)S(1)} %collective-permute-done.14.far_ref), channel_id=1, source_target_pairs={{0,8},{1,17},{2,10},{3,19},{4,12},{5,21},{6,14},{7,23},{8,0},{9,25... | collective-permute-start | bytes 442376 | tf_op jit(solution)/shard_map/ppermute | solution.py:345
  43.9 2.4 %shard_map.85 = (f32[128,256]{1,0:T(8,128)S(1)}, bf16[4,256,2304]{2,1,0:T(8,128)(2,1)}) custom-call(s32[2]{0:T(128)S(1)} %pad_add_fusion.pos, bf16[128,1152]{1,0:T(8,128)(2,1)S(1)} %shard_map.84.refs_0_, bf16[256,128]{1,0:T(8,128)(2,1)S(1)} %get-tuple-element.50.refs_1_.refs_5_, bf16[4,256,2304]{2,1,0:T(8,128)(2,1)} %bitcast.20), custom_call_target="tpu_custom_call" | custom-call | flops 1 | bytes 1 | tf_op jit(solution)/shard_map/pallas_call | solution.py:259
  46.4 0.6 collective-permute-start.17
  46.9 0.5 collective-permute-done.19.far_ref
  47.5 1.6 %collective-permute-start.15 = (bf16[128,1152]{1,0:T(8,128)(2,1)S(1)}, bf16[128,1152]{1,0:T(8,128)(2,1)S(1)}, u32[]{:S(2)}, u32[]{:S(2)}) collective-permute-start(bf16[128,1152]{1,0:T(8,128)(2,1)S(1)} %shard_map.86.refs_1_), channel_id=1, source_target_pairs={{0,8},{1,17},{2,10},{3,19},{4,12},{5,21},{6,14},{7,23},{8,0},{9,25... | collective-permute-start | bytes 884744 | tf_op jit(solution)/shard_map/ppermute | solution.py:345
  49.1 4.0 %shard_map.88 = (f32[128,256]{1,0:T(8,128)S(1)}, bf16[4,256,2304]{2,1,0:T(8,128)(2,1)}, bf16[256,1152]{1,0:T(8,128)(2,1)S(1)}, bf16[256,1152]{1,0:T(8,128)(2,1)S(1)}) custom-call(s32[2]{0:T(128)S(1)} %pad_add_fusion.pos, bf16[128,1152]{1,0:T(8,128)(2,1)S(1)} %collective-permute-done.16.refs_0_, ...), custom_call_target="tpu_custom_call", output_to_operand_aliasing={{1}: (9, {})} | custom-call | flops 1 | bytes 1 | tf_op jit(solution)/shard_map/pallas_call | solution.py:259
  53.2 1.1 %collective-permute-done.15.refs_0_ = bf16[128,1152]{1,0:T(8,128)(2,1)S(1)} collective-permute-done((bf16[128,1152]{1,0:T(8,128)(2,1)S(1)}, bf16[128,1152]{1,0:T(8,128)(2,1)S(1)}, u32[]{:S(2)}, u32[]{:S(2)}) %collective-permute-start.15) | collective-permute-done | bytes 294944 | tf_op jit(solution)/shard_map/ppermute | solution.py:345
  54.4 1.7 %shard_map.90 = (f32[128,256]{1,0:T(8,128)S(1)}, bf16[4,256,2304]{2,1,0:T(8,128)(2,1)}) custom-call(s32[2]{0:T(128)S(1)} %pad_add_fusion.pos, bf16[128,1152]{1,0:T(8,128)(2,1)S(1)} %shard_map.89.refs_0_, bf16[256,128]{1,0:T(8,128)(2,1)S(1)} %get-tuple-element.50.refs_1_.refs_5_, bf16[4,256,2304]{2,1,0:T(8,128)(2,1)} %bitcast.22, ...), custom_call_target="tpu_custom_call", output_to_operand_aliasing={{1}: (5, {})} | custom-call | flops 1 | bytes 1 | tf_op jit(solution)/shard_map/pallas_call | solution.py:259
  56.1 3.3 %shard_map.91 = (f32[128,256]{1,0:T(8,128)}, bf16[4,256,2304]{2,1,0:T(8,128)(2,1)}, bf16[2304,256]{1,0:T(8,128)(2,1)}, f32[1,256]{1,0:T(1,128)}) custom-call(s32[2]{0:T(128)S(1)} %pad_add_fusion.pos, bf16[128,1152]{1,0:T(8,128)(2,1)S(1)} %collective-permute-done.21.refs_0_, ...), custom_call_target="tpu_custom_call", output_to_operand_aliasing={{1}: (5, {})} | custom-call | flops 1 | bytes 1 | tf_op jit(solution)/shard_map/pallas_call | solution.py:259
  (40 shorter events, 1.3 us)
Async XLA Ops:
  0.7 5.5 %copy-start.1 = (bf16[1,128,288]{1,2,0:T(8,128)(2,1)S(1)}, bf16[1,128,288]{1,2,0:T(8,128)(2,1)}, u32[]{:S(2)}) copy-start(bf16[1,128,288]{1,2,0:T(8,128)(2,1)} %param.6) | copy-start | bytes 221188
  3.4 2.9 %collective-permute-start = (bf16[128,1152]{1,0:T(8,128)(2,1)S(1)}, bf16[128,1152]{1,0:T(8,128)(2,1)S(1)}, u32[]{:S(2)}, u32[]{:S(2)}) collective-permute-start(bf16[128,1152]{1,0:T(8,128)(2,1)S(1)} %get-tuple-element.36), channel_id=1, source_target_pairs={{0,1},{1,0},{2,3},{3,2},{4,5},{5,4},{6,7},{7,6},{8,9},{9,8},{10,11... | collective-permute-start | bytes 884744 | tf_op jit(solution)/shard_map/ppermute | solution.py:337
  6.0 6.3 %collective-permute-start.3 = (bf16[128,1152]{1,0:T(8,128)(2,1)S(1)}, bf16[128,1152]{1,0:T(8,128)(2,1)S(1)}, u32[]{:S(2)}, u32[]{:S(2)}) collective-permute-start(bf16[128,1152]{1,0:T(8,128)(2,1)S(1)} %get-tuple-element.43), channel_id=1, source_target_pairs={{0,1},{1,0},{2,3},{3,2},{4,5},{5,4},{6,7},{7,6},{8,9},{9,8},{10,11... | collective-permute-start | bytes 884744 | tf_op jit(solution)/shard_map/ppermute | solution.py:337
  6.4 9.2 %collective-permute-start.2 = (bf16[128,288]{1,0:T(8,128)(2,1)S(1)}, bf16[128,288]{1,0:T(8,128)(2,1)S(1)}, u32[]{:S(2)}, u32[]{:S(2)}) collective-permute-start(bf16[128,288]{1,0:T(8,128)(2,1)S(1)} %bitcast.26), channel_id=1, source_target_pairs={{0,1},{1,0},{2,3},{3,2},{4,5},{5,4},{6,7},{7,6},{8,9},{9,8},{10,11... | collective-permute-start | bytes 221192 | tf_op jit(solution)/shard_map/ppermute | solution.py:337
  6.9 10.8 %collective-permute-start.6 = (bf16[128,1152]{1,0:T(8,128)(2,1)S(1)}, bf16[128,1152]{1,0:T(8,128)(2,1)S(1)}, u32[]{:S(2)}, u32[]{:S(2)}) collective-permute-start(bf16[128,1152]{1,0:T(8,128)(2,1)S(1)} %shard_map.78), channel_id=1, source_target_pairs={{0,8},{1,17},{2,10},{3,19},{4,12},{5,21},{6,14},{7,23},{8,0},{9,25... | collective-permute-start | bytes 884744 | tf_op jit(solution)/shard_map/ppermute | solution.py:345
  12.4 8.5 %collective-permute-start.4 = (bf16[64,1152]{1,0:T(8,128)(2,1)S(1)}, bf16[64,1152]{1,0:T(8,128)(2,1)S(1)}, u32[]{:S(2)}, u32[]{:S(2)}) collective-permute-start(bf16[64,1152]{1,0:T(8,128)(2,1)S(1)} %get-tuple-element.44), channel_id=1, source_target_pairs={{0,8},{1,17},{2,10},{3,19},{4,12},{5,21},{6,14},{7,23},{8,0},{9,25... | collective-permute-start | bytes 442376 | tf_op jit(solution)/shard_map/ppermute | solution.py:345
  12.5 8.4 %collective-permute-start.5 = (bf16[64,1152]{1,0:T(8,128)(2,1)S(1)}, bf16[64,1152]{1,0:T(8,128)(2,1)S(1)}, u32[]{:S(2)}, u32[]{:S(2)}) collective-permute-start(bf16[64,1152]{1,0:T(8,128)(2,1)S(1)} %get-tuple-element.45), channel_id=1, source_target_pairs={{0,10},{1,19},{2,8},{3,17},{4,14},{5,23},{6,12},{7,21},{8,2},{9,27... | collective-permute-start | bytes 442376 | tf_op jit(solution)/shard_map/ppermute | solution.py:345
  15.6 1.6 %collective-permute-start.1 = (bf16[128,1152]{1,0:T(8,128)(2,1)S(1)}, bf16[128,1152]{1,0:T(8,128)(2,1)S(1)}, u32[]{:S(2)}, u32[]{:S(2)}) collective-permute-start(bf16[128,1152]{1,0:T(8,128)(2,1)S(1)} %get-tuple-element.39), channel_id=1, source_target_pairs={{0,1},{1,0},{2,3},{3,2},{4,5},{5,4},{6,7},{7,6},{8,9},{9,8},{10,11... | collective-permute-start | bytes 884744 | tf_op jit(solution)/shard_map/ppermute | solution.py:337
  15.6 2.1 %collective-permute-start.7 = (bf16[128,1152]{1,0:T(8,128)(2,1)S(1)}, bf16[128,1152]{1,0:T(8,128)(2,1)S(1)}, u32[]{:S(2)}, u32[]{:S(2)}) collective-permute-start(bf16[128,1152]{1,0:T(8,128)(2,1)S(1)} %get-tuple-element.47), channel_id=1, source_target_pairs={{0,1},{1,0},{2,3},{3,2},{4,5},{5,4},{6,7},{7,6},{8,9},{9,8},{10,11... | collective-permute-start | bytes 884744 | tf_op jit(solution)/shard_map/ppermute | solution.py:337
  17.2 6.8 %collective-permute-start.10 = (bf16[64,1152]{1,0:T(8,128)(2,1)S(1)}, bf16[64,1152]{1,0:T(8,128)(2,1)S(1)}, u32[]{:S(2)}, u32[]{:S(2)}) collective-permute-start(bf16[64,1152]{1,0:T(8,128)(2,1)S(1)} %shard_map.82), channel_id=1, source_target_pairs={{0,2},{1,3},{2,0},{3,1},{4,6},{5,7},{6,4},{7,5},{8,10},{9,11},{10,... | collective-permute-start | bytes 442376 | tf_op jit(solution)/shard_map/ppermute | solution.py:337
  17.8 6.1 %collective-permute-start.8 = (bf16[64,1152]{1,0:T(8,128)(2,1)S(1)}, bf16[64,1152]{1,0:T(8,128)(2,1)S(1)}, u32[]{:S(2)}, u32[]{:S(2)}) collective-permute-start(bf16[64,1152]{1,0:T(8,128)(2,1)S(1)} %get-tuple-element.48), channel_id=1, source_target_pairs={{0,16},{1,9},{2,18},{3,11},{4,20},{5,13},{6,22},{7,15},{8,24},{9,1... | collective-permute-start | bytes 442376 | tf_op jit(solution)/shard_map/ppermute | solution.py:345
  18.7 7.9 %collective-permute-start.9 = (bf16[64,1152]{1,0:T(8,128)(2,1)S(1)}, bf16[64,1152]{1,0:T(8,128)(2,1)S(1)}, u32[]{:S(2)}, u32[]{:S(2)}) collective-permute-start(bf16[64,1152]{1,0:T(8,128)(2,1)S(1)} %get-tuple-element.49), channel_id=1, source_target_pairs={{0,18},{1,11},{2,16},{3,9},{4,22},{5,15},{6,20},{7,13},{8,26},{9,3... | collective-permute-start | bytes 442376 | tf_op jit(solution)/shard_map/ppermute | solution.py:345
  26.7 8.8 %collective-permute-start.11 = (bf16[64,1152]{1,0:T(8,128)(2,1)S(1)}, bf16[64,1152]{1,0:T(8,128)(2,1)S(1)}, u32[]{:S(2)}, u32[]{:S(2)}) collective-permute-start(bf16[64,1152]{1,0:T(8,128)(2,1)S(1)} %convert_element_type.13), channel_id=1, source_target_pairs={{0,4},{1,5},{2,6},{3,7},{4,0},{5,1},{6,2},{7,3},{8,12},{9,13},{10,... | collective-permute-start | bytes 442376 | tf_op jit(solution)/shard_map/ppermute | solution.py:337
  35.6 6.7 %collective-permute-start.14 = (bf16[64,1152]{1,0:T(8,128)(2,1)S(1)}, bf16[64,1152]{1,0:T(8,128)(2,1)S(1)}, u32[]{:S(2)}, u32[]{:S(2)}) collective-permute-start(bf16[64,1152]{1,0:T(8,128)(2,1)S(1)} %add_convert_fusion.kept_ref), channel_id=1, source_target_pairs={{0,2},{1,3},{2,0},{3,1},{4,6},{5,7},{6,4},{7,5},{8,10},{9,11},{10,... | collective-permute-start | bytes 442376 | tf_op jit(solution)/shard_map/ppermute | solution.py:337
  36.3 10.0 %collective-permute-start.13 = (bf16[64,1152]{1,0:T(8,128)(2,1)S(1)}, bf16[64,1152]{1,0:T(8,128)(2,1)S(1)}, u32[]{:S(2)}, u32[]{:S(2)}) collective-permute-start(bf16[64,1152]{1,0:T(8,128)(2,1)S(1)} %add_convert_fusion.kept_ref), channel_id=1, source_target_pairs={{0,18},{1,11},{2,16},{3,9},{4,22},{5,15},{6,20},{7,13},{8,26},{9,3... | collective-permute-start | bytes 442376 | tf_op jit(solution)/shard_map/ppermute | solution.py:345
  38.2 8.1 %collective-permute-start.12 = (bf16[64,1152]{1,0:T(8,128)(2,1)S(1)}, bf16[64,1152]{1,0:T(8,128)(2,1)S(1)}, u32[]{:S(2)}, u32[]{:S(2)}) collective-permute-start(bf16[64,1152]{1,0:T(8,128)(2,1)S(1)} %add_convert_fusion.kept_ref), channel_id=1, source_target_pairs={{0,16},{1,9},{2,18},{3,11},{4,20},{5,13},{6,22},{7,15},{8,24},{9,1... | collective-permute-start | bytes 442376 | tf_op jit(solution)/shard_map/ppermute | solution.py:345
  39.1 7.8 %collective-permute-start.18 = (bf16[64,1152]{1,0:T(8,128)(2,1)S(1)}, bf16[64,1152]{1,0:T(8,128)(2,1)S(1)}, u32[]{:S(2)}, u32[]{:S(2)}) collective-permute-start(bf16[64,1152]{1,0:T(8,128)(2,1)S(1)} %add_convert_fusion.kept_ref), channel_id=1, source_target_pairs={{0,8},{1,17},{2,10},{3,19},{4,12},{5,21},{6,14},{7,23},{8,0},{9,25... | collective-permute-start | bytes 442376 | tf_op jit(solution)/shard_map/ppermute | solution.py:345
  42.3 5.1 %collective-permute-start.19 = (bf16[64,1152]{1,0:T(8,128)(2,1)S(1)}, bf16[64,1152]{1,0:T(8,128)(2,1)S(1)}, u32[]{:S(2)}, u32[]{:S(2)}) collective-permute-start(bf16[64,1152]{1,0:T(8,128)(2,1)S(1)} %collective-permute-done.14.far_ref), channel_id=1, source_target_pairs={{0,8},{1,17},{2,10},{3,19},{4,12},{5,21},{6,14},{7,23},{8,0},{9,25... | collective-permute-start | bytes 442376 | tf_op jit(solution)/shard_map/ppermute | solution.py:345
  43.8 5.3 %collective-permute-start.16 = (bf16[128,1152]{1,0:T(8,128)(2,1)S(1)}, bf16[128,1152]{1,0:T(8,128)(2,1)S(1)}, u32[]{:S(2)}, u32[]{:S(2)}) collective-permute-start(bf16[128,1152]{1,0:T(8,128)(2,1)S(1)} %shard_map.84.refs_0_), channel_id=1, source_target_pairs={{0,1},{1,0},{2,3},{3,2},{4,5},{5,4},{6,7},{7,6},{8,9},{9,8},{10,11... | collective-permute-start | bytes 884744 | tf_op jit(solution)/shard_map/ppermute | solution.py:337
  46.4 2.8 %collective-permute-start.17 = (bf16[128,1152]{1,0:T(8,128)(2,1)S(1)}, bf16[128,1152]{1,0:T(8,128)(2,1)S(1)}, u32[]{:S(2)}, u32[]{:S(2)}) collective-permute-start(bf16[128,1152]{1,0:T(8,128)(2,1)S(1)} %shard_map.86.refs_1_), channel_id=1, source_target_pairs={{0,1},{1,0},{2,3},{3,2},{4,5},{5,4},{6,7},{7,6},{8,9},{9,8},{10,11... | collective-permute-start | bytes 884744 | tf_op jit(solution)/shard_map/ppermute | solution.py:337
  47.4 1.7 %collective-permute-start.20 = (bf16[128,1152]{1,0:T(8,128)(2,1)S(1)}, bf16[128,1152]{1,0:T(8,128)(2,1)S(1)}, u32[]{:S(2)}, u32[]{:S(2)}) collective-permute-start(bf16[128,1152]{1,0:T(8,128)(2,1)S(1)} %shard_map.87.refs_3_), channel_id=1, source_target_pairs={{0,1},{1,0},{2,3},{3,2},{4,5},{5,4},{6,7},{7,6},{8,9},{9,8},{10,11... | collective-permute-start | bytes 884744 | tf_op jit(solution)/shard_map/ppermute | solution.py:337
  47.5 6.8 %collective-permute-start.15 = (bf16[128,1152]{1,0:T(8,128)(2,1)S(1)}, bf16[128,1152]{1,0:T(8,128)(2,1)S(1)}, u32[]{:S(2)}, u32[]{:S(2)}) collective-permute-start(bf16[128,1152]{1,0:T(8,128)(2,1)S(1)} %shard_map.86.refs_1_), channel_id=1, source_target_pairs={{0,8},{1,17},{2,10},{3,19},{4,12},{5,21},{6,14},{7,23},{8,0},{9,25... | collective-permute-start | bytes 884744 | tf_op jit(solution)/shard_map/ppermute | solution.py:345
  54.3 1.8 %collective-permute-start.21 = (bf16[128,1152]{1,0:T(8,128)(2,1)S(1)}, bf16[128,1152]{1,0:T(8,128)(2,1)S(1)}, u32[]{:S(2)}, u32[]{:S(2)}) collective-permute-start(bf16[128,1152]{1,0:T(8,128)(2,1)S(1)} %shard_map.89.refs_0_), channel_id=1, source_target_pairs={{0,1},{1,0},{2,3},{3,2},{4,5},{5,4},{6,7},{7,6},{8,9},{9,8},{10,11... | collective-permute-start | bytes 884744 | tf_op jit(solution)/shard_map/ppermute | solution.py:337
  54.4 1.7 %copy-start = (bf16[1,128,2304]{2,1,0:T(8,128)(2,1)S(1)}, bf16[1,128,2304]{2,1,0:T(8,128)(2,1)}, u32[]{:S(2)}) copy-start(bf16[1,128,2304]{2,1,0:T(8,128)(2,1)} %param.5) | copy-start | bytes 1769476

commit v4 on v3

--- a/solution.py
+++ b/solution.py
@@ -48,11 +48,11 @@
     bits = layers.bit_length() - 1
     copies, live = [], []
     for i, (slot, part) in enumerate(jobs):
-        side = pos[1] if part == 0 else 1 - pos[1]
-        target = pos[0] ^ slot_offset(slot, side, bits)
+        side = (pos[0] & 1) if part == 0 else 1 - (pos[0] & 1)
+        target = (pos[0] >> 1) ^ slot_offset(slot, side, bits)
         cols = pl.ds(pl.multiple_of(side * half, half), half)
         copies.append(pltpu.make_async_copy(wd_hbm.at[target, :, cols], w_ref.at[i], sems.at[i]))
-        live.append(target >= pos[0])
+        live.append(target >= (pos[0] >> 1))
     return copies, live
 
 
@@ -167,23 +167,24 @@
         old_ref = take(2)[0] if carry is not None else None
         w_refs = take(count) if weights is not None else None
         x_ref, pre_ref = take(2) if last is not None else (None, None)
-        sum_ref, grad_hbm = take(2)
+        sum_ref = take(1)[0] if last is None else None
+        grad_hbm = take(1)[0]
         ahead_refs = take(len(ahead))
-        genc_hbm, gb_ref = take(2) if last is not None else (None, None)
+        genc_hbm, gb_hbm = take(2) if last is not None else (None, None)
         grad_ref, grad_sems = take(2)
         load_ref, load_sems = take(2) if weights is None else (None, None)
         ahead_sems = take(1)[0] if ahead else None
-        genc_ref, enc_sems = take(2) if last is not None else (None, None)
+        genc_ref, gb_ref, total_ref, enc_sems = take(4) if last is not None else (None,) * 4
 
         def place(slot, part):
-            side = pos[1] if part == 0 else 1 - pos[1]
-            target = pos[0] ^ slot_offset(slot, side, bits)
+            side = (pos[0] & 1) if part == 0 else 1 - (pos[0] & 1)
+            target = (pos[0] >> 1) ^ slot_offset(slot, side, bits)
             return target, pl.ds(pl.multiple_of(side * half, half), half)
 
         loads, writes, live, later = [], [], [], []
         for i, job in enumerate(jobs):
             target, span = place(*job)
-            live.append(target >= pos[0])
+            live.append(target >= (pos[0] >> 1))
             writes.append(pltpu.make_async_copy(grad_ref.at[i], grad_hbm.at[target, :, span], grad_sems.at[i]))
             if weights is None:
                 loads.append(pltpu.make_async_copy(wd_hbm.at[target, :, span], load_ref.at[i], load_sems.at[i]))
@@ -195,6 +196,8 @@
         if weights is None:
             w_refs = [load_ref.at[i] for i in range(count)]
 
+        if last is not None:
+            sum_ref = total_ref
         sum_ref[...] = jnp.zeros_like(sum_ref) if carry is None else old_ref[...]
         for i in range(count):
 
@@ -221,6 +224,8 @@
         if last is not None:
             pre_grad = jnp.where(pre_ref[...] > 0, sum_ref[...] * scale, 0.0).astype(BF16)
             gb_ref[...] = jnp.sum(pre_grad.astype(F32), axis=0, keepdims=True)
+            writes.append(pltpu.make_async_copy(gb_ref, gb_hbm, enc_sems.at[pieces]))
+            writes[-1].start()
             for i in range(pieces):
                 span = pl.ds(i * (cols // pieces), cols // pieces)
                 genc_ref[span] = lax.dot_general(
@@ -234,15 +239,16 @@
 
     in_specs = [IN_SMEM] + [IN_VMEM] * (count + 1) + [IN_PLACE]
     args = [pos] + [in_vmem(a) for a in (*errs, act_t)] + [in_hbm(w_dec)]
-    out_specs = [IN_VMEM, IN_PLACE] + [IN_VMEM] * len(ahead)
-    out_shape = [pltpu.VMEM((toks, width), F32), pltpu.HBM((layers, width, cols), BF16)]
+    sums = 0 if last is not None else 1
+    out_specs = [IN_VMEM] * sums + [IN_PLACE] + [IN_VMEM] * len(ahead)
+    out_shape = [pltpu.VMEM((toks, width), F32)] * sums + [pltpu.HBM((layers, width, cols), BF16)]
     out_shape += [pltpu.VMEM((width, half), BF16)] * len(ahead)
     scratch = [pltpu.VMEM((count, width, half), BF16), pltpu.SemaphoreType.DMA((count,))]
     aliases = {}
     if carry is not None:
         in_specs += [IN_VMEM, IN_PLACE]
         args += [in_vmem(carry[0]), carry[1]]
-        aliases = {len(args) - 1: 1}
+        aliases = {len(args) - 1: sums}
     if weights is None:
         scratch += [pltpu.VMEM((count, width, half), BF16), pltpu.SemaphoreType.DMA((count,))]
     else:
@@ -253,9 +259,14 @@
     if last is not None:
         in_specs += [IN_VMEM] * 2
         args += [in_vmem(a) for a in last]
-        out_specs += [IN_PLACE, IN_VMEM]
-        out_shape += [pltpu.HBM((cols, width), BF16), jax.ShapeDtypeStruct((1, width), F32)]
-        scratch += [pltpu.VMEM((cols, width), BF16), pltpu.SemaphoreType.DMA((pieces,))]
+        out_specs += [IN_PLACE] * 2
+        out_shape += [pltpu.HBM((cols, width), BF16), pltpu.HBM((1, width), F32)]
+        scratch += [
+            pltpu.VMEM((cols, width), BF16),
+            pltpu.VMEM((1, width), F32),
+            pltpu.VMEM((toks, width), F32),
+            pltpu.SemaphoreType.DMA((pieces + 1,)),
+        ]
     return pl.pallas_call(
         kernel,
         in_specs=in_specs,
@@ -330,7 +341,7 @@
     half = cols // 2
     own_layer, own_feat = lax.axis_index("layer"), lax.axis_index("feat")
     core = own_feat & 1
-    pos = jnp.stack([own_layer, core]).astype(jnp.int32)
+    pos = (own_layer * 2 + core).astype(jnp.int32).reshape(1)
     x, tgt, wd = inputs[0], targets[0], w_dec[0]
 
     def swap_feat(value, bit):
@@ -370,11 +381,11 @@
         for s in reversed(range(n)):
             if step == 0 and n + s == final:
                 continue
-            if s > 0:
+            if s > 0 or step < bits - 1:
                 slots[s].append(swap_layer(add_up(slots[n + s], BF16), step))
             else:
                 kept, away = add_rows(high, (0, 1), slots[n], ([], []), BF16)
-                rows += [swap_layer(kept, step), swap_layer(away, step, cross=True)]
+                rows += [swap_layer(kept, step), add_up([swap_layer(away, step, cross=True)], BF16, 100000000000)]
 
     pair_tgt = swap_feat(tgt, 0)
     pair = jnp.where(core == 0, jnp.stack([tgt, pair_tgt]), jnp.stack([pair_tgt, tgt]))
@@ -386,7 +397,7 @@
         padded = jnp.pad(pair, ((0, 0), (i * span, half - (i + 1) * span)))
         spread = jnp.where(chip == core * (chips // 2) + i, padded, spread)
 
-    (away,) = add_rows(high, (1,), [*slots[0], spread], ([],), BF16)
+    (away,) = add_rows(high, (1,), [*slots[0], after(spread, kept)], ([],), BF16)
     rows.append(swap_feat(away, 1))
     (rows,) = add_rows(high, (0,), [*slots[0], spread], (rows,), F32)
     for bit in range(2, feat_bits - 1):
@@ -411,7 +422,7 @@
             if s > 0:
                 slots.append(swap_layer(slots[s], step))
             elif i > 0:
-                slots.append(join_rows(high, near[i], swap_layer(far, step)))
+                slots.append(join_rows(high, near[i], swap_layer(far, step), 1))
             else:
                 slots.append(join_rows(high, near[i], after(cross, start[0]), 1))
     middle = [(0, 1)] + [(s, part) for s in range(1, final) for part in (0, 1)]
@@ -421,7 +432,7 @@
     other = swap_feat(own, 0)
     carry = backward(pos, [(final, 0)], [own], act_t, wd, carry, [w_own])
     carry = backward(pos, [(final, 1)], [other], act_t, wd, carry, [w_other], last=(x, pre))
-    act_sum, grad_dec, grad_enc, grad_benc = carry
+    grad_dec, grad_enc, grad_benc = carry
     return grad_enc[None], grad_dec[None], grad_benc
 
 

time: 59.7 us -> 54.1 us (0.906)
  starting transfers between devices: 22.6 us -> 17.2 us
  Pallas kernels: 19.6 us -> 15.1 us
  waiting for transfers between devices: 15.8 us -> 20.1 us
    ppermute x10 -> x9, starting transfers between devices: 16.2 us -> 10 us  [swap_layer(): return lax.ppermute(value, ('layer', 'feat'), pairs)]
    ppermute x10 -> x9, waiting for transfers between devices: 4.27 us -> 8.38 us  [swap_layer(): return lax.ppermute(value, ('layer', 'feat'), pairs)]
    pallas_call x4, Pallas kernels: 11.4 us -> 8.48 us  [backward(): pl.pallas_call(kernel, in_specs=in_specs, out_specs=out_specs, out_shape=...]
    pallas_call x2, Pallas kernels: 5.1 us -> 4.01 us  [decode(): pl.pallas_call(kernel, in_specs=[IN_SMEM, IN_VMEM, IN_PLACE], out_specs=[...]
    ppermute x12, starting transfers between devices: 6.34 us -> 7.14 us  [swap_feat(): lax.ppermute(value, 'feat', [(f, f ^ 1 << bit) for f in range(feats)])]
  transfers between devices with their start and end apart: 22 -> 21, of which waited for: 7 -> 11; matrix products, arithmetic and copies ran while one was open for 1% -> 1% of each run, Pallas kernels for 23% -> 20%
where the time goes in v4:
time: 54.1 us; the launch traced here: 53.8 us
  waiting for transfers between devices  20.1 us (37%)
  starting transfers between devices  17.2 us (32%)
  Pallas kernels  15.1 us (28%)
  between operations  0.87 us (2%)
    ppermute x12, waiting for transfers between devices, swap_feat(): lax.ppermute(value, 'feat', [(f, f ^ 1 << bit) for f in range(feats)])  11.7 us
    ppermute x9, starting transfers between devices, swap_layer(): return lax.ppermute(value, ('layer', 'feat'), pairs)  10 us
    pallas_call x4, Pallas kernels, backward(): pl.pallas_call(kernel, in_specs=in_specs, out_specs=out_specs, out_shape=...  8.48 us
    ppermute x9, waiting for transfers between devices, swap_layer(): return lax.ppermute(value, ('layer', 'feat'), pairs)  8.38 us
    ppermute x12, starting transfers between devices, swap_feat(): lax.ppermute(value, 'feat', [(f, f ^ 1 << bit) for f in range(feats)])  7.14 us
    pallas_call x2, Pallas kernels, decode(): pl.pallas_call(kernel, in_specs=[IN_SMEM, IN_VMEM, IN_PLACE], out_specs=[...  4.01 us
    pallas_call x1, Pallas kernels, encode(): pl.pallas_call(kernel, in_specs=[IN_SMEM] + [IN_PLACE] * 4, out_specs=[IN...  2.15 us
  transfers between devices with their start and end apart: 21, of which 11 were waited for; matrix products, arithmetic and copies ran while one was open for 1% of the time, Pallas kernels for 20%

profile of v4, /device:TPU:0, one launch (start us, length us, event | category | flops | bytes accessed | tf_op | source)
XLA Modules:
  0.0 53.8 jit_solution(4266908005491226733)
XLA Ops:
  0.6 2.1 %shard_map.76 = (f32[128,256]{1,0:T(8,128)S(1)}, bf16[128,256]{1,0:T(8,128)(2,1)S(1)}, bf16[256,128]{1,0:T(8,128)(2,1)S(1)}, bf16[128,1152]{1,0:T(8,128)(2,1)S(1)}) custom-call(s32[1]{0:T(128)} %bitcast.pos, bf16[128,2304]{1,0:T(8,128)(2,1)} %bitcast.14, bf16[2304,256]{1,0:T(8,128)(2,1)} %bitcast.24, f32[1,256]{1,0:T(1,128)} %b_hbm.1, ...), custom_call_target="tpu_custom_call" | custom-call | flops 1 | bytes 1 | tf_op jit(solution)/shard_map/pallas_call | solution.py:107
  2.8 0.5 collective-permute-start
  3.3 1.6 %shard_map.77 = (f32[128,1152]{1,0:T(8,128)S(1)}, bf16[128,1152]{1,0:T(8,128)(2,1)S(1)}) custom-call(s32[1]{0:T(128)} %bitcast.pos, bf16[128,256]{1,0:T(8,128)(2,1)S(1)} %get-tuple-element.36.act_ref, bf16[4,256,2304]{2,1,0:T(8,128)(2,1)} %bitcast.17), custom_call_target="tpu_custom_call" | custom-call | flops 1 | bytes 1 | tf_op jit(solution)/shard_map/pallas_call | solution.py:141
  5.2 0.5 collective-permute-start.4
  5.8 2.5 %collective-permute-start.5 = (bf16[128,1152]{1,0:T(8,128)(2,1)S(1)}, bf16[128,1152]{1,0:T(8,128)(2,1)S(1)}, u32[]{:S(2)}, u32[]{:S(2)}) collective-permute-start(bf16[128,1152]{1,0:T(8,128)(2,1)S(1)} %shard_map.78), channel_id=1, source_target_pairs={{0,8},{1,17},{2,10},{3,19},{4,12},{5,21},{6,14},{7,23},{8,0},{9,25... | collective-permute-start | bytes 884744 | tf_op jit(solution)/shard_map/ppermute | solution.py:356
  8.3 2.4 %shard_map.79 = (f32[128,1152]{1,0:T(8,128)S(1)}, bf16[128,1152]{1,0:T(8,128)(2,1)S(1)}, f32[128,1152]{1,0:T(8,128)S(1)}, bf16[128,1152]{1,0:T(8,128)(2,1)S(1)}, f32[128,1152]{1,0:T(8,128)S(1)}) custom-call(s32[1]{0:T(128)} %bitcast.pos, bf16[128,256]{1,0:T(8,128)(2,1)S(1)} %get-tuple-element.36.act_ref, bf16[4,256,2304]{2,1,0:T(8,128)(2,1)} %bitcast.18), custom_call_target="tpu_custom_call" | custom-call | flops 1 | bytes 1 | tf_op jit(solution)/shard_map/pallas_call | solution.py:141
  10.9 0.5 collective-permute-start.6
  11.6 1.3 %collective-permute-done.5.refs_0_ = bf16[128,1152]{1,0:T(8,128)(2,1)S(1)} collective-permute-done((bf16[128,1152]{1,0:T(8,128)(2,1)S(1)}, bf16[128,1152]{1,0:T(8,128)(2,1)S(1)}, u32[]{:S(2)}, u32[]{:S(2)}) %collective-permute-start.5) | collective-permute-done | bytes 294944 | tf_op jit(solution)/shard_map/ppermute | solution.py:356
  13.1 2.9 %collective-permute-start.8 = (bf16[64,1152]{1,0:T(8,128)(2,1)S(1)}, bf16[64,1152]{1,0:T(8,128)(2,1)S(1)}, u32[]{:S(2)}, u32[]{:S(2)}) collective-permute-start(bf16[64,1152]{1,0:T(8,128)(2,1)S(1)} %get-tuple-element.46), channel_id=1, source_target_pairs={{0,18},{1,11},{2,16},{3,9},{4,22},{5,15},{6,20},{7,13},{8,26},{9,3... | collective-permute-start | bytes 442376 | tf_op jit(solution)/shard_map/ppermute | solution.py:356
  16.1 0.9 %collective-permute-start.7 = (bf16[64,1152]{1,0:T(8,128)(2,1)S(1)}, bf16[64,1152]{1,0:T(8,128)(2,1)S(1)}, u32[]{:S(2)}, u32[]{:S(2)}) collective-permute-start(bf16[64,1152]{1,0:T(8,128)(2,1)S(1)} %get-tuple-element.45), channel_id=1, source_target_pairs={{0,16},{1,9},{2,18},{3,11},{4,20},{5,13},{6,22},{7,15},{8,24},{9,1... | collective-permute-start | bytes 442376 | tf_op jit(solution)/shard_map/ppermute | solution.py:356
  17.0 2.5 %collective-permute-done.3.refs_2_ = bf16[128,1152]{1,0:T(8,128)(2,1)S(1)} collective-permute-done((bf16[128,1152]{1,0:T(8,128)(2,1)S(1)}, bf16[128,1152]{1,0:T(8,128)(2,1)S(1)}, u32[]{:S(2)}, u32[]{:S(2)}) %collective-permute-start.3) | collective-permute-done | bytes 294944 | tf_op jit(solution)/shard_map/ppermute | solution.py:356
  19.6 1.6 %collective-permute-start.9 = (bf16[64,1152]{1,0:T(8,128)(2,1)S(1)}, bf16[64,1152]{1,0:T(8,128)(2,1)S(1)}, u32[]{:S(2)}, u32[]{:S(2)}) collective-permute-start(bf16[64,1152]{1,0:T(8,128)(2,1)S(1)} %shard_map.83), channel_id=1, source_target_pairs={{0,2},{1,3},{2,0},{3,1},{4,6},{5,7},{6,4},{7,5},{8,10},{9,11},{10,... | collective-permute-start | bytes 442376 | tf_op jit(solution)/shard_map/ppermute | solution.py:348
  21.2 3.6 %collective-permute-done.9.refs_6_ = bf16[64,1152]{1,0:T(8,128)(2,1)S(1)} collective-permute-done((bf16[64,1152]{1,0:T(8,128)(2,1)S(1)}, bf16[64,1152]{1,0:T(8,128)(2,1)S(1)}, u32[]{:S(2)}, u32[]{:S(2)}) %collective-permute-start.9) | collective-permute-done | bytes 147488 | tf_op jit(solution)/shard_map/ppermute | solution.py:348
  24.8 0.1 shard_map.84
  25.0 2.8 %collective-permute-start.10 = (bf16[64,1152]{1,0:T(8,128)(2,1)S(1)}, bf16[64,1152]{1,0:T(8,128)(2,1)S(1)}, u32[]{:S(2)}, u32[]{:S(2)}) collective-permute-start(bf16[64,1152]{1,0:T(8,128)(2,1)S(1)} %convert_element_type.13), channel_id=1, source_target_pairs={{0,4},{1,5},{2,6},{3,7},{4,0},{5,1},{6,2},{7,3},{8,12},{9,13},{10,... | collective-permute-start | bytes 442376 | tf_op jit(solution)/shard_map/ppermute | solution.py:348
  27.8 4.9 %collective-permute-done.10 = bf16[64,1152]{1,0:T(8,128)(2,1)S(1)} collective-permute-done((bf16[64,1152]{1,0:T(8,128)(2,1)S(1)}, bf16[64,1152]{1,0:T(8,128)(2,1)S(1)}, u32[]{:S(2)}, u32[]{:S(2)}) %collective-permute-start.10) | collective-permute-done | bytes 147488 | tf_op jit(solution)/shard_map/ppermute | solution.py:348
  32.8 0.7 %collective-permute-start.13 = (bf16[64,1152]{1,0:T(8,128)(2,1)S(1)}, bf16[64,1152]{1,0:T(8,128)(2,1)S(1)}, u32[]{:S(2)}, u32[]{:S(2)}) collective-permute-start(bf16[64,1152]{1,0:T(8,128)(2,1)S(1)} %add_convert_fusion.kept_ref), channel_id=1, source_target_pairs={{0,2},{1,3},{2,0},{3,1},{4,6},{5,7},{6,4},{7,5},{8,10},{9,11},{10,... | collective-permute-start | bytes 442376 | tf_op jit(solution)/shard_map/ppermute | solution.py:348
  33.5 1.3 %collective-permute-start.12 = (bf16[64,1152]{1,0:T(8,128)(2,1)S(1)}, bf16[64,1152]{1,0:T(8,128)(2,1)S(1)}, u32[]{:S(2)}, u32[]{:S(2)}) collective-permute-start(bf16[64,1152]{1,0:T(8,128)(2,1)S(1)} %add_convert_fusion.kept_ref), channel_id=1, source_target_pairs={{0,18},{1,11},{2,16},{3,9},{4,22},{5,15},{6,20},{7,13},{8,26},{9,3... | collective-permute-start | bytes 442376 | tf_op jit(solution)/shard_map/ppermute | solution.py:356
  34.8 1.6 %collective-permute-start.11 = (bf16[64,1152]{1,0:T(8,128)(2,1)S(1)}, bf16[64,1152]{1,0:T(8,128)(2,1)S(1)}, u32[]{:S(2)}, u32[]{:S(2)}) collective-permute-start(bf16[64,1152]{1,0:T(8,128)(2,1)S(1)} %add_convert_fusion.kept_ref), channel_id=1, source_target_pairs={{0,16},{1,9},{2,18},{3,11},{4,20},{5,13},{6,22},{7,15},{8,24},{9,1... | collective-permute-start | bytes 442376 | tf_op jit(solution)/shard_map/ppermute | solution.py:356
  36.3 1.6 %collective-permute-done.13.far_ref = bf16[64,1152]{1,0:T(8,128)(2,1)S(1)} collective-permute-done((bf16[64,1152]{1,0:T(8,128)(2,1)S(1)}, bf16[64,1152]{1,0:T(8,128)(2,1)S(1)}, u32[]{:S(2)}, u32[]{:S(2)}) %collective-permute-start.13) | collective-permute-done | bytes 147488 | tf_op jit(solution)/shard_map/ppermute | solution.py:348
  38.0 0.4 collective-permute-start.18
  38.5 1.5 %shard_map.86 = (f32[128,256]{1,0:T(8,128)S(1)}, bf16[4,256,2304]{2,1,0:T(8,128)(2,1)}) custom-call(s32[1]{0:T(128)} %bitcast.pos, bf16[128,1152]{1,0:T(8,128)(2,1)S(1)} %shard_map.85.refs_0_, bf16[256,128]{1,0:T(8,128)(2,1)S(1)} %get-tuple-element.48.refs_1_.refs_5_, bf16[4,256,2304]{2,1,0:T(8,128)(2,1)} %bitcast.19), custom_call_target="tpu_custom_call" | custom-call | flops 1 | bytes 1 | tf_op jit(solution)/shard_map/pallas_call | solution.py:270
  40.0 0.5 collective-permute-done.12.far_ref
  40.5 1.1 %collective-permute-done.11.kept_ref = bf16[64,1152]{1,0:T(8,128)(2,1)S(1)} collective-permute-done((bf16[64,1152]{1,0:T(8,128)(2,1)S(1)}, bf16[64,1152]{1,0:T(8,128)(2,1)S(1)}, u32[]{:S(2)}, u32[]{:S(2)}) %collective-permute-start.11) | collective-permute-done | bytes 147488 | tf_op jit(solution)/shard_map/ppermute | solution.py:356
  41.6 1.5 %collective-permute-done.18.far_ref = bf16[64,1152]{1,0:T(8,128)(2,1)S(1)} collective-permute-done((bf16[64,1152]{1,0:T(8,128)(2,1)S(1)}, bf16[64,1152]{1,0:T(8,128)(2,1)S(1)}, u32[]{:S(2)}, u32[]{:S(2)}) %collective-permute-start.18) | collective-permute-done | bytes 147488 | tf_op jit(solution)/shard_map/ppermute | solution.py:356
  43.2 0.4 collective-permute-start.14
  43.7 1.1 %collective-permute-done.19.refs_4_ = bf16[128,1152]{1,0:T(8,128)(2,1)S(1)} collective-permute-done((bf16[128,1152]{1,0:T(8,128)(2,1)S(1)}, bf16[128,1152]{1,0:T(8,128)(2,1)S(1)}, u32[]{:S(2)}, u32[]{:S(2)}) %collective-permute-start.19) | collective-permute-done | bytes 294944 | tf_op jit(solution)/shard_map/ppermute | solution.py:348
  44.8 3.8 %shard_map.89 = (f32[128,256]{1,0:T(8,128)S(1)}, bf16[4,256,2304]{2,1,0:T(8,128)(2,1)}, bf16[256,1152]{1,0:T(8,128)(2,1)S(1)}, bf16[256,1152]{1,0:T(8,128)(2,1)S(1)}) custom-call(s32[1]{0:T(128)} %bitcast.pos, bf16[128,1152]{1,0:T(8,128)(2,1)S(1)} %collective-permute-done.15.refs_0_, ...), custom_call_target="tpu_custom_call", output_to_operand_aliasing={{1}: (9, {})} | custom-call | flops 1 | bytes 1 | tf_op jit(solution)/shard_map/pallas_call | solution.py:270
  48.6 1.5 %collective-permute-done.14.refs_0_ = bf16[128,1152]{1,0:T(8,128)(2,1)S(1)} collective-permute-done((bf16[128,1152]{1,0:T(8,128)(2,1)S(1)}, bf16[128,1152]{1,0:T(8,128)(2,1)S(1)}, u32[]{:S(2)}, u32[]{:S(2)}) %collective-permute-start.14) | collective-permute-done | bytes 294944 | tf_op jit(solution)/shard_map/ppermute | solution.py:356
  50.1 1.1 %shard_map.91 = (f32[128,256]{1,0:T(8,128)S(1)}, bf16[4,256,2304]{2,1,0:T(8,128)(2,1)}) custom-call(s32[1]{0:T(128)} %bitcast.pos, bf16[128,1152]{1,0:T(8,128)(2,1)S(1)} %shard_map.90.refs_0_, bf16[256,128]{1,0:T(8,128)(2,1)S(1)} %get-tuple-element.48.refs_1_.refs_5_, bf16[4,256,2304]{2,1,0:T(8,128)(2,1)} %bitcast.21, ...), custom_call_target="tpu_custom_call", output_to_operand_aliasing={{1}: (5, {})} | custom-call | flops 1 | bytes 1 | tf_op jit(solution)/shard_map/pallas_call | solution.py:270
  51.3 0.4 collective-permute-done.20.refs_0_
  51.7 2.1 %shard_map.92 = (bf16[4,256,2304]{2,1,0:T(8,128)(2,1)}, bf16[2304,256]{1,0:T(8,128)(2,1)}, f32[1,256]{1,0:T(1,128)}) custom-call(s32[1]{0:T(128)} %bitcast.pos, bf16[128,1152]{1,0:T(8,128)(2,1)S(1)} %collective-permute-done.20.refs_0_, bf16[256,128]{1,0:T(8,128)(2,1)S(1)} %get-tuple-element.48.refs_1_.refs_5_, ...), custom_call_target="tpu_custom_call", output_to_operand_aliasing={{0}: (5, {})} | custom-call | flops 1 | bytes 1 | tf_op jit(solution)/shard_map/pallas_call | solution.py:270
  (38 shorter events, 1.5 us)
Async XLA Ops:
  0.6 4.4 %copy-start.1 = (bf16[1,128,288]{1,2,0:T(8,128)(2,1)S(1)}, bf16[1,128,288]{1,2,0:T(8,128)(2,1)}, u32[]{:S(2)}) copy-start(bf16[1,128,288]{1,2,0:T(8,128)(2,1)} %param.6) | copy-start | bytes 221188
  2.8 2.4 %collective-permute-start = (bf16[128,1152]{1,0:T(8,128)(2,1)S(1)}, bf16[128,1152]{1,0:T(8,128)(2,1)S(1)}, u32[]{:S(2)}, u32[]{:S(2)}) collective-permute-start(bf16[128,1152]{1,0:T(8,128)(2,1)S(1)} %get-tuple-element.35), channel_id=1, source_target_pairs={{0,1},{1,0},{2,3},{3,2},{4,5},{5,4},{6,7},{7,6},{8,9},{9,8},{10,11... | collective-permute-start | bytes 884744 | tf_op jit(solution)/shard_map/ppermute | solution.py:348
  4.9 5.8 %collective-permute-start.2 = (bf16[128,1152]{1,0:T(8,128)(2,1)S(1)}, bf16[128,1152]{1,0:T(8,128)(2,1)S(1)}, u32[]{:S(2)}, u32[]{:S(2)}) collective-permute-start(bf16[128,1152]{1,0:T(8,128)(2,1)S(1)} %get-tuple-element.41), channel_id=1, source_target_pairs={{0,1},{1,0},{2,3},{3,2},{4,5},{5,4},{6,7},{7,6},{8,9},{9,8},{10,11... | collective-permute-start | bytes 884744 | tf_op jit(solution)/shard_map/ppermute | solution.py:348
  5.2 6.2 %collective-permute-start.4 = (bf16[128,288]{1,0:T(8,128)(2,1)S(1)}, bf16[128,288]{1,0:T(8,128)(2,1)S(1)}, u32[]{:S(2)}, u32[]{:S(2)}) collective-permute-start(bf16[128,288]{1,0:T(8,128)(2,1)S(1)} %bitcast.25), channel_id=1, source_target_pairs={{0,1},{1,0},{2,3},{3,2},{4,5},{5,4},{6,7},{7,6},{8,9},{9,8},{10,11... | collective-permute-start | bytes 221192 | tf_op jit(solution)/shard_map/ppermute | solution.py:348
  5.8 7.2 %collective-permute-start.5 = (bf16[128,1152]{1,0:T(8,128)(2,1)S(1)}, bf16[128,1152]{1,0:T(8,128)(2,1)S(1)}, u32[]{:S(2)}, u32[]{:S(2)}) collective-permute-start(bf16[128,1152]{1,0:T(8,128)(2,1)S(1)} %shard_map.78), channel_id=1, source_target_pairs={{0,8},{1,17},{2,10},{3,19},{4,12},{5,21},{6,14},{7,23},{8,0},{9,25... | collective-permute-start | bytes 884744 | tf_op jit(solution)/shard_map/ppermute | solution.py:356
  10.8 8.7 %collective-permute-start.3 = (bf16[128,1152]{1,0:T(8,128)(2,1)S(1)}, bf16[128,1152]{1,0:T(8,128)(2,1)S(1)}, u32[]{:S(2)}, u32[]{:S(2)}) collective-permute-start(bf16[128,1152]{1,0:T(8,128)(2,1)S(1)} %shard_map.80), channel_id=1, source_target_pairs={{0,8},{1,17},{2,10},{3,19},{4,12},{5,21},{6,14},{7,23},{8,0},{9,25... | collective-permute-start | bytes 884744 | tf_op jit(solution)/shard_map/ppermute | solution.py:356
  10.9 8.7 %collective-permute-start.1 = (bf16[128,1152]{1,0:T(8,128)(2,1)S(1)}, bf16[128,1152]{1,0:T(8,128)(2,1)S(1)}, u32[]{:S(2)}, u32[]{:S(2)}) collective-permute-start(bf16[128,1152]{1,0:T(8,128)(2,1)S(1)} %get-tuple-element.38), channel_id=1, source_target_pairs={{0,1},{1,0},{2,3},{3,2},{4,5},{5,4},{6,7},{7,6},{8,9},{9,8},{10,11... | collective-permute-start | bytes 884744 | tf_op jit(solution)/shard_map/ppermute | solution.py:348
  10.9 2.0 %collective-permute-start.6 = (bf16[128,1152]{1,0:T(8,128)(2,1)S(1)}, bf16[128,1152]{1,0:T(8,128)(2,1)S(1)}, u32[]{:S(2)}, u32[]{:S(2)}) collective-permute-start(bf16[128,1152]{1,0:T(8,128)(2,1)S(1)} %get-tuple-element.44), channel_id=1, source_target_pairs={{0,1},{1,0},{2,3},{3,2},{4,5},{5,4},{6,7},{7,6},{8,9},{9,8},{10,11... | collective-permute-start | bytes 884744 | tf_op jit(solution)/shard_map/ppermute | solution.py:348
  13.1 8.1 %collective-permute-start.8 = (bf16[64,1152]{1,0:T(8,128)(2,1)S(1)}, bf16[64,1152]{1,0:T(8,128)(2,1)S(1)}, u32[]{:S(2)}, u32[]{:S(2)}) collective-permute-start(bf16[64,1152]{1,0:T(8,128)(2,1)S(1)} %get-tuple-element.46), channel_id=1, source_target_pairs={{0,18},{1,11},{2,16},{3,9},{4,22},{5,15},{6,20},{7,13},{8,26},{9,3... | collective-permute-start | bytes 442376 | tf_op jit(solution)/shard_map/ppermute | solution.py:356
  16.1 8.7 %collective-permute-start.7 = (bf16[64,1152]{1,0:T(8,128)(2,1)S(1)}, bf16[64,1152]{1,0:T(8,128)(2,1)S(1)}, u32[]{:S(2)}, u32[]{:S(2)}) collective-permute-start(bf16[64,1152]{1,0:T(8,128)(2,1)S(1)} %get-tuple-element.45), channel_id=1, source_target_pairs={{0,16},{1,9},{2,18},{3,11},{4,20},{5,13},{6,22},{7,15},{8,24},{9,1... | collective-permute-start | bytes 442376 | tf_op jit(solution)/shard_map/ppermute | solution.py:356
  19.6 5.2 %collective-permute-start.9 = (bf16[64,1152]{1,0:T(8,128)(2,1)S(1)}, bf16[64,1152]{1,0:T(8,128)(2,1)S(1)}, u32[]{:S(2)}, u32[]{:S(2)}) collective-permute-start(bf16[64,1152]{1,0:T(8,128)(2,1)S(1)} %shard_map.83), channel_id=1, source_target_pairs={{0,2},{1,3},{2,0},{3,1},{4,6},{5,7},{6,4},{7,5},{8,10},{9,11},{10,... | collective-permute-start | bytes 442376 | tf_op jit(solution)/shard_map/ppermute | solution.py:348
  25.0 7.8 %collective-permute-start.10 = (bf16[64,1152]{1,0:T(8,128)(2,1)S(1)}, bf16[64,1152]{1,0:T(8,128)(2,1)S(1)}, u32[]{:S(2)}, u32[]{:S(2)}) collective-permute-start(bf16[64,1152]{1,0:T(8,128)(2,1)S(1)} %convert_element_type.13), channel_id=1, source_target_pairs={{0,4},{1,5},{2,6},{3,7},{4,0},{5,1},{6,2},{7,3},{8,12},{9,13},{10,... | collective-permute-start | bytes 442376 | tf_op jit(solution)/shard_map/ppermute | solution.py:348
  32.8 5.2 %collective-permute-start.13 = (bf16[64,1152]{1,0:T(8,128)(2,1)S(1)}, bf16[64,1152]{1,0:T(8,128)(2,1)S(1)}, u32[]{:S(2)}, u32[]{:S(2)}) collective-permute-start(bf16[64,1152]{1,0:T(8,128)(2,1)S(1)} %add_convert_fusion.kept_ref), channel_id=1, source_target_pairs={{0,2},{1,3},{2,0},{3,1},{4,6},{5,7},{6,4},{7,5},{8,10},{9,11},{10,... | collective-permute-start | bytes 442376 | tf_op jit(solution)/shard_map/ppermute | solution.py:348
  33.5 7.0 %collective-permute-start.12 = (bf16[64,1152]{1,0:T(8,128)(2,1)S(1)}, bf16[64,1152]{1,0:T(8,128)(2,1)S(1)}, u32[]{:S(2)}, u32[]{:S(2)}) collective-permute-start(bf16[64,1152]{1,0:T(8,128)(2,1)S(1)} %add_convert_fusion.kept_ref), channel_id=1, source_target_pairs={{0,18},{1,11},{2,16},{3,9},{4,22},{5,15},{6,20},{7,13},{8,26},{9,3... | collective-permute-start | bytes 442376 | tf_op jit(solution)/shard_map/ppermute | solution.py:356
  34.8 6.7 %collective-permute-start.11 = (bf16[64,1152]{1,0:T(8,128)(2,1)S(1)}, bf16[64,1152]{1,0:T(8,128)(2,1)S(1)}, u32[]{:S(2)}, u32[]{:S(2)}) collective-permute-start(bf16[64,1152]{1,0:T(8,128)(2,1)S(1)} %add_convert_fusion.kept_ref), channel_id=1, source_target_pairs={{0,16},{1,9},{2,18},{3,11},{4,20},{5,13},{6,22},{7,15},{8,24},{9,1... | collective-permute-start | bytes 442376 | tf_op jit(solution)/shard_map/ppermute | solution.py:356
  36.3 5.3 %collective-permute-start.17 = (bf16[64,1152]{1,0:T(8,128)(2,1)S(1)}, bf16[64,1152]{1,0:T(8,128)(2,1)S(1)}, u32[]{:S(2)}, u32[]{:S(2)}) collective-permute-start(bf16[64,1152]{1,0:T(8,128)(2,1)S(1)} %add_convert_fusion.kept_ref), channel_id=1, source_target_pairs={{0,8},{1,17},{2,10},{3,19},{4,12},{5,21},{6,14},{7,23},{8,0},{9,25... | collective-permute-start | bytes 442376 | tf_op jit(solution)/shard_map/ppermute | solution.py:356
  38.0 5.1 %collective-permute-start.18 = (bf16[64,1152]{1,0:T(8,128)(2,1)S(1)}, bf16[64,1152]{1,0:T(8,128)(2,1)S(1)}, u32[]{:S(2)}, u32[]{:S(2)}) collective-permute-start(bf16[64,1152]{1,0:T(8,128)(2,1)S(1)} %collective-permute-done.13.far_ref), channel_id=1, source_target_pairs={{0,8},{1,17},{2,10},{3,19},{4,12},{5,21},{6,14},{7,23},{8,0},{9,25... | collective-permute-start | bytes 442376 | tf_op jit(solution)/shard_map/ppermute | solution.py:356
  38.4 5.3 %collective-permute-start.15 = (bf16[128,1152]{1,0:T(8,128)(2,1)S(1)}, bf16[128,1152]{1,0:T(8,128)(2,1)S(1)}, u32[]{:S(2)}, u32[]{:S(2)}) collective-permute-start(bf16[128,1152]{1,0:T(8,128)(2,1)S(1)} %shard_map.85.refs_0_), channel_id=1, source_target_pairs={{0,1},{1,0},{2,3},{3,2},{4,5},{5,4},{6,7},{7,6},{8,9},{9,8},{10,11... | collective-permute-start | bytes 884744 | tf_op jit(solution)/shard_map/ppermute | solution.py:348
  41.5 2.2 %collective-permute-start.16 = (bf16[128,1152]{1,0:T(8,128)(2,1)S(1)}, bf16[128,1152]{1,0:T(8,128)(2,1)S(1)}, u32[]{:S(2)}, u32[]{:S(2)}) collective-permute-start(bf16[128,1152]{1,0:T(8,128)(2,1)S(1)} %shard_map.87.refs_1_), channel_id=1, source_target_pairs={{0,1},{1,0},{2,3},{3,2},{4,5},{5,4},{6,7},{7,6},{8,9},{9,8},{10,11... | collective-permute-start | bytes 884744 | tf_op jit(solution)/shard_map/ppermute | solution.py:348
  43.2 1.6 %collective-permute-start.19 = (bf16[128,1152]{1,0:T(8,128)(2,1)S(1)}, bf16[128,1152]{1,0:T(8,128)(2,1)S(1)}, u32[]{:S(2)}, u32[]{:S(2)}) collective-permute-start(bf16[128,1152]{1,0:T(8,128)(2,1)S(1)} %shard_map.88.refs_3_), channel_id=1, source_target_pairs={{0,1},{1,0},{2,3},{3,2},{4,5},{5,4},{6,7},{7,6},{8,9},{9,8},{10,11... | collective-permute-start | bytes 884744 | tf_op jit(solution)/shard_map/ppermute | solution.py:348
  43.2 6.8 %collective-permute-start.14 = (bf16[128,1152]{1,0:T(8,128)(2,1)S(1)}, bf16[128,1152]{1,0:T(8,128)(2,1)S(1)}, u32[]{:S(2)}, u32[]{:S(2)}) collective-permute-start(bf16[128,1152]{1,0:T(8,128)(2,1)S(1)} %shard_map.87.refs_1_), channel_id=1, source_target_pairs={{0,8},{1,17},{2,10},{3,19},{4,12},{5,21},{6,14},{7,23},{8,0},{9,25... | collective-permute-start | bytes 884744 | tf_op jit(solution)/shard_map/ppermute | solution.py:356
  50.1 1.6 %collective-permute-start.20 = (bf16[128,1152]{1,0:T(8,128)(2,1)S(1)}, bf16[128,1152]{1,0:T(8,128)(2,1)S(1)}, u32[]{:S(2)}, u32[]{:S(2)}) collective-permute-start(bf16[128,1152]{1,0:T(8,128)(2,1)S(1)} %shard_map.90.refs_0_), channel_id=1, source_target_pairs={{0,1},{1,0},{2,3},{3,2},{4,5},{5,4},{6,7},{7,6},{8,9},{9,8},{10,11... | collective-permute-start | bytes 884744 | tf_op jit(solution)/shard_map/ppermute | solution.py:348
  50.1 1.6 %copy-start = (bf16[1,128,2304]{2,1,0:T(8,128)(2,1)S(1)}, bf16[1,128,2304]{2,1,0:T(8,128)(2,1)}, u32[]{:S(2)}) copy-start(bf16[1,128,2304]{2,1,0:T(8,128)(2,1)} %param.5) | copy-start | bytes 1769476

commit v5 on v4

--- a/solution.py
+++ b/solution.py
@@ -422,16 +422,19 @@
             if s > 0:
                 slots.append(swap_layer(slots[s], step))
             elif i > 0:
-                slots.append(join_rows(high, near[i], swap_layer(far, step), 1))
+                slots.append(join_rows(high, near[i], swap_layer(far, step), 10000000000))
             else:
                 slots.append(join_rows(high, near[i], after(cross, start[0]), 1))
-    middle = [(0, 1)] + [(s, part) for s in range(1, final) for part in (0, 1)]
-    errs = [slots[s] if part == 0 else swap_feat(slots[0] if s == 0 else slots[s], 0) for s, part in middle]
-    *carry, w_own, w_other = backward(pos, middle, errs, act_t, wd, start, ahead=[(final, 0), (final, 1)])
-    own = add_up([after(slots[final], carry[0])], BF16, 100000000000)
-    other = swap_feat(own, 0)
-    carry = backward(pos, [(final, 0)], [own], act_t, wd, carry, [w_own])
-    carry = backward(pos, [(final, 1)], [other], act_t, wd, carry, [w_other], last=(x, pre))
+    between = range(2, final)
+    work = [(0, 1), (1, 0), (1, 1)] + [(s, 0) for s in between]
+    errs = [swap_feat(slots[0], 0), slots[1], swap_feat(slots[1], 0)] + [slots[s] for s in between]
+    others = [swap_feat(slots[s], 0) for s in between]
+    rest = [(s, 1) for s in between] + [(final, 0)]
+    carry = backward(pos, work, errs, act_t, wd, start, ahead=rest + [(final, 1)])
+    carry, w_rest, w_last = carry[:2], carry[2:-1], carry[-1]
+    others.append(swap_feat(after(slots[final], carry[0]), 0))
+    carry = backward(pos, rest, [*others[:-1], slots[final]], act_t, wd, carry, w_rest)
+    carry = backward(pos, [(final, 1)], others[-1:], act_t, wd, carry, [w_last], last=(x, pre))
     grad_dec, grad_enc, grad_benc = carry
     return grad_enc[None], grad_dec[None], grad_benc
 

time: 54.1 us -> 52.8 us (0.976)
  waiting for transfers between devices: 20.1 us -> 18.4 us
    ppermute x9, starting transfers between devices: 10 us -> 12.7 us  [swap_layer(): return lax.ppermute(value, ('layer', 'feat'), pairs)]
    ppermute x12, starting transfers between devices: 7.14 us -> 4.97 us  [swap_feat(): lax.ppermute(value, 'feat', [(f, f ^ 1 << bit) for f in range(feats)])]
    ppermute x9, waiting for transfers between devices: 8.38 us -> 6.22 us  [swap_layer(): return lax.ppermute(value, ('layer', 'feat'), pairs)]
  transfers between devices with their start and end apart: 21 -> 21, of which waited for: 11 -> 10; matrix products, arithmetic and copies ran while one was open for 1% -> 1% of each run, Pallas kernels for 20% -> 20%
where the time goes in v5:
time: 52.8 us; the launch traced here: 52.5 us
  waiting for transfers between devices  18.4 us (35%)
  starting transfers between devices  17.7 us (34%)
  Pallas kernels  15 us (28%)
  between operations  0.87 us (2%)
    ppermute x9, starting transfers between devices, swap_layer(): return lax.ppermute(value, ('layer', 'feat'), pairs)  12.7 us
    ppermute x12, waiting for transfers between devices, swap_feat(): lax.ppermute(value, 'feat', [(f, f ^ 1 << bit) for f in range(feats)])  12.2 us
    pallas_call x4, Pallas kernels, backward(): pl.pallas_call(kernel, in_specs=in_specs, out_specs=out_specs, out_shape=...  8.4 us
    ppermute x9, waiting for transfers between devices, swap_layer(): return lax.ppermute(value, ('layer', 'feat'), pairs)  6.22 us
    ppermute x12, starting transfers between devices, swap_feat(): lax.ppermute(value, 'feat', [(f, f ^ 1 << bit) for f in range(feats)])  4.97 us
    pallas_call x2, Pallas kernels, decode(): pl.pallas_call(kernel, in_specs=[IN_SMEM, IN_VMEM, IN_PLACE], out_specs=[...  4.01 us
    pallas_call x1, Pallas kernels, encode(): pl.pallas_call(kernel, in_specs=[IN_SMEM] + [IN_PLACE] * 4, out_specs=[IN...  2.15 us
  transfers between devices with their start and end apart: 21, of which 10 were waited for; matrix products, arithmetic and copies ran while one was open for 1% of the time, Pallas kernels for 20%

profile of v5, /device:TPU:0, one launch (start us, length us, event | category | flops | bytes accessed | tf_op | source)
XLA Modules:
  0.0 52.5 jit_solution(16732513625295491797)
XLA Ops:
  0.6 2.1 %shard_map.76 = (f32[128,256]{1,0:T(8,128)S(1)}, bf16[128,256]{1,0:T(8,128)(2,1)S(1)}, bf16[256,128]{1,0:T(8,128)(2,1)S(1)}, bf16[128,1152]{1,0:T(8,128)(2,1)S(1)}) custom-call(s32[1]{0:T(128)} %bitcast.pos, bf16[128,2304]{1,0:T(8,128)(2,1)} %bitcast.14, bf16[2304,256]{1,0:T(8,128)(2,1)} %bitcast.24, f32[1,256]{1,0:T(1,128)} %b_hbm.1, ...), custom_call_target="tpu_custom_call" | custom-call | flops 1 | bytes 1 | tf_op jit(solution)/shard_map/pallas_call | solution.py:107
  2.8 0.5 collective-permute-start
  3.3 1.6 %shard_map.77 = (f32[128,1152]{1,0:T(8,128)S(1)}, bf16[128,1152]{1,0:T(8,128)(2,1)S(1)}) custom-call(s32[1]{0:T(128)} %bitcast.pos, bf16[128,256]{1,0:T(8,128)(2,1)S(1)} %get-tuple-element.37.act_ref, bf16[4,256,2304]{2,1,0:T(8,128)(2,1)} %bitcast.17), custom_call_target="tpu_custom_call" | custom-call | flops 1 | bytes 1 | tf_op jit(solution)/shard_map/pallas_call | solution.py:141
  4.9 0.1 collective-permute-start.2
  5.0 0.1 copy.11
  5.2 0.5 collective-permute-start.4
  5.8 2.5 %collective-permute-start.5 = (bf16[128,1152]{1,0:T(8,128)(2,1)S(1)}, bf16[128,1152]{1,0:T(8,128)(2,1)S(1)}, u32[]{:S(2)}, u32[]{:S(2)}) collective-permute-start(bf16[128,1152]{1,0:T(8,128)(2,1)S(1)} %shard_map.78), channel_id=1, source_target_pairs={{0,8},{1,17},{2,10},{3,19},{4,12},{5,21},{6,14},{7,23},{8,0},{9,25... | collective-permute-start | bytes 884744 | tf_op jit(solution)/shard_map/ppermute | solution.py:356
  8.3 2.4 %shard_map.79 = (f32[128,1152]{1,0:T(8,128)S(1)}, bf16[128,1152]{1,0:T(8,128)(2,1)S(1)}, f32[128,1152]{1,0:T(8,128)S(1)}, bf16[128,1152]{1,0:T(8,128)(2,1)S(1)}, f32[128,1152]{1,0:T(8,128)S(1)}) custom-call(s32[1]{0:T(128)} %bitcast.pos, bf16[128,256]{1,0:T(8,128)(2,1)S(1)} %get-tuple-element.37.act_ref, bf16[4,256,2304]{2,1,0:T(8,128)(2,1)} %bitcast.18), custom_call_target="tpu_custom_call" | custom-call | flops 1 | bytes 1 | tf_op jit(solution)/shard_map/pallas_call | solution.py:141
  10.9 1.0 %collective-permute-start.3 = (bf16[128,1152]{1,0:T(8,128)(2,1)S(1)}, bf16[128,1152]{1,0:T(8,128)(2,1)S(1)}, u32[]{:S(2)}, u32[]{:S(2)}) collective-permute-start(bf16[128,1152]{1,0:T(8,128)(2,1)S(1)} %shard_map.80), channel_id=1, source_target_pairs={{0,8},{1,17},{2,10},{3,19},{4,12},{5,21},{6,14},{7,23},{8,0},{9,25... | collective-permute-start | bytes 884744 | tf_op jit(solution)/shard_map/ppermute | solution.py:356
  12.2 0.2 collective-permute-done.6.refs_2_
  12.3 0.6 %collective-permute-done.5.refs_0_ = bf16[128,1152]{1,0:T(8,128)(2,1)S(1)} collective-permute-done((bf16[128,1152]{1,0:T(8,128)(2,1)S(1)}, bf16[128,1152]{1,0:T(8,128)(2,1)S(1)}, u32[]{:S(2)}, u32[]{:S(2)}) %collective-permute-start.5) | collective-permute-done | bytes 294944 | tf_op jit(solution)/shard_map/ppermute | solution.py:356
  13.1 2.9 %collective-permute-start.8 = (bf16[64,1152]{1,0:T(8,128)(2,1)S(1)}, bf16[64,1152]{1,0:T(8,128)(2,1)S(1)}, u32[]{:S(2)}, u32[]{:S(2)}) collective-permute-start(bf16[64,1152]{1,0:T(8,128)(2,1)S(1)} %get-tuple-element.47), channel_id=1, source_target_pairs={{0,18},{1,11},{2,16},{3,9},{4,22},{5,15},{6,20},{7,13},{8,26},{9,3... | collective-permute-start | bytes 442376 | tf_op jit(solution)/shard_map/ppermute | solution.py:356
  16.0 0.1 select_select_fusion.refs_3_
  16.1 0.9 %collective-permute-start.7 = (bf16[64,1152]{1,0:T(8,128)(2,1)S(1)}, bf16[64,1152]{1,0:T(8,128)(2,1)S(1)}, u32[]{:S(2)}, u32[]{:S(2)}) collective-permute-start(bf16[64,1152]{1,0:T(8,128)(2,1)S(1)} %get-tuple-element.46), channel_id=1, source_target_pairs={{0,16},{1,9},{2,18},{3,11},{4,20},{5,13},{6,22},{7,15},{8,24},{9,1... | collective-permute-start | bytes 442376 | tf_op jit(solution)/shard_map/ppermute | solution.py:356
  17.0 3.3 %collective-permute-done.3.refs_2_ = bf16[128,1152]{1,0:T(8,128)(2,1)S(1)} collective-permute-done((bf16[128,1152]{1,0:T(8,128)(2,1)S(1)}, bf16[128,1152]{1,0:T(8,128)(2,1)S(1)}, u32[]{:S(2)}, u32[]{:S(2)}) %collective-permute-start.3) | collective-permute-done | bytes 294944 | tf_op jit(solution)/shard_map/ppermute | solution.py:356
  20.4 1.3 %collective-permute-start.9 = (bf16[64,1152]{1,0:T(8,128)(2,1)S(1)}, bf16[64,1152]{1,0:T(8,128)(2,1)S(1)}, u32[]{:S(2)}, u32[]{:S(2)}) collective-permute-start(bf16[64,1152]{1,0:T(8,128)(2,1)S(1)} %shard_map.83), channel_id=1, source_target_pairs={{0,2},{1,3},{2,0},{3,1},{4,6},{5,7},{6,4},{7,5},{8,10},{9,11},{10,... | collective-permute-start | bytes 442376 | tf_op jit(solution)/shard_map/ppermute | solution.py:348
  21.6 5.0 %collective-permute-done.9.refs_6_ = bf16[64,1152]{1,0:T(8,128)(2,1)S(1)} collective-permute-done((bf16[64,1152]{1,0:T(8,128)(2,1)S(1)}, bf16[64,1152]{1,0:T(8,128)(2,1)S(1)}, u32[]{:S(2)}, u32[]{:S(2)}) %collective-permute-start.9) | collective-permute-done | bytes 147488 | tf_op jit(solution)/shard_map/ppermute | solution.py:348
  26.6 0.1 shard_map.84
  26.8 2.1 %collective-permute-start.10 = (bf16[64,1152]{1,0:T(8,128)(2,1)S(1)}, bf16[64,1152]{1,0:T(8,128)(2,1)S(1)}, u32[]{:S(2)}, u32[]{:S(2)}) collective-permute-start(bf16[64,1152]{1,0:T(8,128)(2,1)S(1)} %convert_element_type.13), channel_id=1, source_target_pairs={{0,4},{1,5},{2,6},{3,7},{4,0},{5,1},{6,2},{7,3},{8,12},{9,13},{10,... | collective-permute-start | bytes 442376 | tf_op jit(solution)/shard_map/ppermute | solution.py:348
  28.9 5.3 %collective-permute-done.10 = bf16[64,1152]{1,0:T(8,128)(2,1)S(1)} collective-permute-done((bf16[64,1152]{1,0:T(8,128)(2,1)S(1)}, bf16[64,1152]{1,0:T(8,128)(2,1)S(1)}, u32[]{:S(2)}, u32[]{:S(2)}) %collective-permute-start.10) | collective-permute-done | bytes 147488 | tf_op jit(solution)/shard_map/ppermute | solution.py:348
  34.3 0.9 %collective-permute-start.12 = (bf16[64,1152]{1,0:T(8,128)(2,1)S(1)}, bf16[64,1152]{1,0:T(8,128)(2,1)S(1)}, u32[]{:S(2)}, u32[]{:S(2)}) collective-permute-start(bf16[64,1152]{1,0:T(8,128)(2,1)S(1)} %add_convert_fusion.kept_ref), channel_id=1, source_target_pairs={{0,18},{1,11},{2,16},{3,9},{4,22},{5,15},{6,20},{7,13},{8,26},{9,3... | collective-permute-start | bytes 442376 | tf_op jit(solution)/shard_map/ppermute | solution.py:356
  35.2 2.6 %collective-permute-start.11 = (bf16[64,1152]{1,0:T(8,128)(2,1)S(1)}, bf16[64,1152]{1,0:T(8,128)(2,1)S(1)}, u32[]{:S(2)}, u32[]{:S(2)}) collective-permute-start(bf16[64,1152]{1,0:T(8,128)(2,1)S(1)} %add_convert_fusion.kept_ref), channel_id=1, source_target_pairs={{0,16},{1,9},{2,18},{3,11},{4,20},{5,13},{6,22},{7,15},{8,24},{9,1... | collective-permute-start | bytes 442376 | tf_op jit(solution)/shard_map/ppermute | solution.py:356
  37.7 1.6 %collective-permute-done.13.far_ref = bf16[64,1152]{1,0:T(8,128)(2,1)S(1)} collective-permute-done((bf16[64,1152]{1,0:T(8,128)(2,1)S(1)}, bf16[64,1152]{1,0:T(8,128)(2,1)S(1)}, u32[]{:S(2)}, u32[]{:S(2)}) %collective-permute-start.13) | collective-permute-done | bytes 147488 | tf_op jit(solution)/shard_map/ppermute | solution.py:348
  39.4 0.4 collective-permute-start.18
  39.9 1.5 %shard_map.86 = (f32[128,256]{1,0:T(8,128)S(1)}, bf16[4,256,2304]{2,1,0:T(8,128)(2,1)}) custom-call(s32[1]{0:T(128)} %bitcast.pos, bf16[128,1152]{1,0:T(8,128)(2,1)S(1)} %shard_map.85.refs_0_, bf16[256,128]{1,0:T(8,128)(2,1)S(1)} %get-tuple-element.49.refs_1_.refs_4_.refs_2_, bf16[4,256,2304]{2,1,0:T(8,128)(2,1)} %bitcast.19), custom_call_target="tpu_custom_call" | custom-call | flops 1 | bytes 1 | tf_op jit(solution)/shard_map/pallas_call | solution.py:270
  41.4 0.6 %collective-permute-done.11.kept_ref = bf16[64,1152]{1,0:T(8,128)(2,1)S(1)} collective-permute-done((bf16[64,1152]{1,0:T(8,128)(2,1)S(1)}, bf16[64,1152]{1,0:T(8,128)(2,1)S(1)}, u32[]{:S(2)}, u32[]{:S(2)}) %collective-permute-start.11) | collective-permute-done | bytes 147488 | tf_op jit(solution)/shard_map/ppermute | solution.py:356
  42.1 1.6 %collective-permute-start.14 = (bf16[128,1152]{1,0:T(8,128)(2,1)S(1)}, bf16[128,1152]{1,0:T(8,128)(2,1)S(1)}, u32[]{:S(2)}, u32[]{:S(2)}) collective-permute-start(bf16[128,1152]{1,0:T(8,128)(2,1)S(1)} %shard_map.87.refs_1_), channel_id=1, source_target_pairs={{0,8},{1,17},{2,10},{3,19},{4,12},{5,21},{6,14},{7,23},{8,0},{9,25... | collective-permute-start | bytes 884744 | tf_op jit(solution)/shard_map/ppermute | solution.py:356
  43.7 0.9 %collective-permute-done.18.far_ref = bf16[64,1152]{1,0:T(8,128)(2,1)S(1)} collective-permute-done((bf16[64,1152]{1,0:T(8,128)(2,1)S(1)}, bf16[64,1152]{1,0:T(8,128)(2,1)S(1)}, u32[]{:S(2)}, u32[]{:S(2)}) %collective-permute-start.18) | collective-permute-done | bytes 147488 | tf_op jit(solution)/shard_map/ppermute | solution.py:356
  44.7 3.4 %shard_map.89 = (f32[128,256]{1,0:T(8,128)S(1)}, bf16[4,256,2304]{2,1,0:T(8,128)(2,1)}, bf16[256,1152]{1,0:T(8,128)(2,1)S(1)}, bf16[256,1152]{1,0:T(8,128)(2,1)S(1)}, bf16[256,1152]{1,0:T(8,128)(2,1)S(1)}) custom-call(s32[1]{0:T(128)} %bitcast.pos, bf16[128,1152]{1,0:T(8,128)(2,1)S(1)} %collective-permute-done.15.refs_0_, ...), custom_call_target="tpu_custom_call", output_to_operand_aliasing={{1}: (8, {})} | custom-call | flops 1 | bytes 1 | tf_op jit(solution)/shard_map/pallas_call | solution.py:270
  48.0 0.8 %collective-permute-done.14.refs_1_ = bf16[128,1152]{1,0:T(8,128)(2,1)S(1)} collective-permute-done((bf16[128,1152]{1,0:T(8,128)(2,1)S(1)}, bf16[128,1152]{1,0:T(8,128)(2,1)S(1)}, u32[]{:S(2)}, u32[]{:S(2)}) %collective-permute-start.14) | collective-permute-done | bytes 294944 | tf_op jit(solution)/shard_map/ppermute | solution.py:356
  48.9 1.5 %shard_map.90 = (f32[128,256]{1,0:T(8,128)S(1)}, bf16[4,256,2304]{2,1,0:T(8,128)(2,1)}) custom-call(s32[1]{0:T(128)} %bitcast.pos, bf16[128,1152]{1,0:T(8,128)(2,1)S(1)} %collective-permute-done.20.refs_0_, bf16[128,1152]{1,0:T(8,128)(2,1)S(1)} %collective-permute-done.14.refs_1_, ...), custom_call_target="tpu_custom_call", output_to_operand_aliasing={{1}: (6, {})} | custom-call | flops 1 | bytes 1 | tf_op jit(solution)/shard_map/pallas_call | solution.py:270
  50.4 2.1 %shard_map.91 = (bf16[4,256,2304]{2,1,0:T(8,128)(2,1)}, bf16[2304,256]{1,0:T(8,128)(2,1)}, f32[1,256]{1,0:T(1,128)}) custom-call(s32[1]{0:T(128)} %bitcast.pos, bf16[128,1152]{1,0:T(8,128)(2,1)S(1)} %collective-permute-done.19.refs_0_, bf16[256,128]{1,0:T(8,128)(2,1)S(1)} %get-tuple-element.49.refs_1_.refs_4_.refs_2_, ...), custom_call_target="tpu_custom_call", output_to_operand_aliasing={{0}: (5, {})} | custom-call | flops 1 | bytes 1 | tf_op jit(solution)/shard_map/pallas_call | solution.py:270
  (37 shorter events, 1.2 us)
Async XLA Ops:
  0.6 4.4 %copy-start.1 = (bf16[1,128,288]{1,2,0:T(8,128)(2,1)S(1)}, bf16[1,128,288]{1,2,0:T(8,128)(2,1)}, u32[]{:S(2)}) copy-start(bf16[1,128,288]{1,2,0:T(8,128)(2,1)} %param.6) | copy-start | bytes 221188
  2.8 2.4 %collective-permute-start = (bf16[128,1152]{1,0:T(8,128)(2,1)S(1)}, bf16[128,1152]{1,0:T(8,128)(2,1)S(1)}, u32[]{:S(2)}, u32[]{:S(2)}) collective-permute-start(bf16[128,1152]{1,0:T(8,128)(2,1)S(1)} %get-tuple-element.36), channel_id=1, source_target_pairs={{0,1},{1,0},{2,3},{3,2},{4,5},{5,4},{6,7},{7,6},{8,9},{9,8},{10,11... | collective-permute-start | bytes 884744 | tf_op jit(solution)/shard_map/ppermute | solution.py:348
  4.9 5.9 %collective-permute-start.2 = (bf16[128,1152]{1,0:T(8,128)(2,1)S(1)}, bf16[128,1152]{1,0:T(8,128)(2,1)S(1)}, u32[]{:S(2)}, u32[]{:S(2)}) collective-permute-start(bf16[128,1152]{1,0:T(8,128)(2,1)S(1)} %get-tuple-element.42), channel_id=1, source_target_pairs={{0,1},{1,0},{2,3},{3,2},{4,5},{5,4},{6,7},{7,6},{8,9},{9,8},{10,11... | collective-permute-start | bytes 884744 | tf_op jit(solution)/shard_map/ppermute | solution.py:348
  5.2 6.7 %collective-permute-start.4 = (bf16[128,288]{1,0:T(8,128)(2,1)S(1)}, bf16[128,288]{1,0:T(8,128)(2,1)S(1)}, u32[]{:S(2)}, u32[]{:S(2)}) collective-permute-start(bf16[128,288]{1,0:T(8,128)(2,1)S(1)} %bitcast.25), channel_id=1, source_target_pairs={{0,1},{1,0},{2,3},{3,2},{4,5},{5,4},{6,7},{7,6},{8,9},{9,8},{10,11... | collective-permute-start | bytes 221192 | tf_op jit(solution)/shard_map/ppermute | solution.py:348
  5.8 7.2 %collective-permute-start.5 = (bf16[128,1152]{1,0:T(8,128)(2,1)S(1)}, bf16[128,1152]{1,0:T(8,128)(2,1)S(1)}, u32[]{:S(2)}, u32[]{:S(2)}) collective-permute-start(bf16[128,1152]{1,0:T(8,128)(2,1)S(1)} %shard_map.78), channel_id=1, source_target_pairs={{0,8},{1,17},{2,10},{3,19},{4,12},{5,21},{6,14},{7,23},{8,0},{9,25... | collective-permute-start | bytes 884744 | tf_op jit(solution)/shard_map/ppermute | solution.py:356
  10.7 1.6 %collective-permute-start.6 = (bf16[128,1152]{1,0:T(8,128)(2,1)S(1)}, bf16[128,1152]{1,0:T(8,128)(2,1)S(1)}, u32[]{:S(2)}, u32[]{:S(2)}) collective-permute-start(bf16[128,1152]{1,0:T(8,128)(2,1)S(1)} %get-tuple-element.45), channel_id=1, source_target_pairs={{0,1},{1,0},{2,3},{3,2},{4,5},{5,4},{6,7},{7,6},{8,9},{9,8},{10,11... | collective-permute-start | bytes 884744 | tf_op jit(solution)/shard_map/ppermute | solution.py:348
  10.9 9.4 %collective-permute-start.3 = (bf16[128,1152]{1,0:T(8,128)(2,1)S(1)}, bf16[128,1152]{1,0:T(8,128)(2,1)S(1)}, u32[]{:S(2)}, u32[]{:S(2)}) collective-permute-start(bf16[128,1152]{1,0:T(8,128)(2,1)S(1)} %shard_map.80), channel_id=1, source_target_pairs={{0,8},{1,17},{2,10},{3,19},{4,12},{5,21},{6,14},{7,23},{8,0},{9,25... | collective-permute-start | bytes 884744 | tf_op jit(solution)/shard_map/ppermute | solution.py:356
  11.9 8.4 %collective-permute-start.1 = (bf16[128,1152]{1,0:T(8,128)(2,1)S(1)}, bf16[128,1152]{1,0:T(8,128)(2,1)S(1)}, u32[]{:S(2)}, u32[]{:S(2)}) collective-permute-start(bf16[128,1152]{1,0:T(8,128)(2,1)S(1)} %get-tuple-element.39), channel_id=1, source_target_pairs={{0,1},{1,0},{2,3},{3,2},{4,5},{5,4},{6,7},{7,6},{8,9},{9,8},{10,11... | collective-permute-start | bytes 884744 | tf_op jit(solution)/shard_map/ppermute | solution.py:348
  13.1 8.6 %collective-permute-start.8 = (bf16[64,1152]{1,0:T(8,128)(2,1)S(1)}, bf16[64,1152]{1,0:T(8,128)(2,1)S(1)}, u32[]{:S(2)}, u32[]{:S(2)}) collective-permute-start(bf16[64,1152]{1,0:T(8,128)(2,1)S(1)} %get-tuple-element.47), channel_id=1, source_target_pairs={{0,18},{1,11},{2,16},{3,9},{4,22},{5,15},{6,20},{7,13},{8,26},{9,3... | collective-permute-start | bytes 442376 | tf_op jit(solution)/shard_map/ppermute | solution.py:356
  16.1 10.6 %collective-permute-start.7 = (bf16[64,1152]{1,0:T(8,128)(2,1)S(1)}, bf16[64,1152]{1,0:T(8,128)(2,1)S(1)}, u32[]{:S(2)}, u32[]{:S(2)}) collective-permute-start(bf16[64,1152]{1,0:T(8,128)(2,1)S(1)} %get-tuple-element.46), channel_id=1, source_target_pairs={{0,16},{1,9},{2,18},{3,11},{4,20},{5,13},{6,22},{7,15},{8,24},{9,1... | collective-permute-start | bytes 442376 | tf_op jit(solution)/shard_map/ppermute | solution.py:356
  20.4 6.3 %collective-permute-start.9 = (bf16[64,1152]{1,0:T(8,128)(2,1)S(1)}, bf16[64,1152]{1,0:T(8,128)(2,1)S(1)}, u32[]{:S(2)}, u32[]{:S(2)}) collective-permute-start(bf16[64,1152]{1,0:T(8,128)(2,1)S(1)} %shard_map.83), channel_id=1, source_target_pairs={{0,2},{1,3},{2,0},{3,1},{4,6},{5,7},{6,4},{7,5},{8,10},{9,11},{10,... | collective-permute-start | bytes 442376 | tf_op jit(solution)/shard_map/ppermute | solution.py:348
  26.8 7.4 %collective-permute-start.10 = (bf16[64,1152]{1,0:T(8,128)(2,1)S(1)}, bf16[64,1152]{1,0:T(8,128)(2,1)S(1)}, u32[]{:S(2)}, u32[]{:S(2)}) collective-permute-start(bf16[64,1152]{1,0:T(8,128)(2,1)S(1)} %convert_element_type.13), channel_id=1, source_target_pairs={{0,4},{1,5},{2,6},{3,7},{4,0},{5,1},{6,2},{7,3},{8,12},{9,13},{10,... | collective-permute-start | bytes 442376 | tf_op jit(solution)/shard_map/ppermute | solution.py:348
  34.2 5.2 %collective-permute-start.13 = (bf16[64,1152]{1,0:T(8,128)(2,1)S(1)}, bf16[64,1152]{1,0:T(8,128)(2,1)S(1)}, u32[]{:S(2)}, u32[]{:S(2)}) collective-permute-start(bf16[64,1152]{1,0:T(8,128)(2,1)S(1)} %add_convert_fusion.kept_ref), channel_id=1, source_target_pairs={{0,2},{1,3},{2,0},{3,1},{4,6},{5,7},{6,4},{7,5},{8,10},{9,11},{10,... | collective-permute-start | bytes 442376 | tf_op jit(solution)/shard_map/ppermute | solution.py:348
  34.3 7.1 %collective-permute-start.12 = (bf16[64,1152]{1,0:T(8,128)(2,1)S(1)}, bf16[64,1152]{1,0:T(8,128)(2,1)S(1)}, u32[]{:S(2)}, u32[]{:S(2)}) collective-permute-start(bf16[64,1152]{1,0:T(8,128)(2,1)S(1)} %add_convert_fusion.kept_ref), channel_id=1, source_target_pairs={{0,18},{1,11},{2,16},{3,9},{4,22},{5,15},{6,20},{7,13},{8,26},{9,3... | collective-permute-start | bytes 442376 | tf_op jit(solution)/shard_map/ppermute | solution.py:356
  35.2 6.8 %collective-permute-start.11 = (bf16[64,1152]{1,0:T(8,128)(2,1)S(1)}, bf16[64,1152]{1,0:T(8,128)(2,1)S(1)}, u32[]{:S(2)}, u32[]{:S(2)}) collective-permute-start(bf16[64,1152]{1,0:T(8,128)(2,1)S(1)} %add_convert_fusion.kept_ref), channel_id=1, source_target_pairs={{0,16},{1,9},{2,18},{3,11},{4,20},{5,13},{6,22},{7,15},{8,24},{9,1... | collective-permute-start | bytes 442376 | tf_op jit(solution)/shard_map/ppermute | solution.py:356
  37.7 5.9 %collective-permute-start.17 = (bf16[64,1152]{1,0:T(8,128)(2,1)S(1)}, bf16[64,1152]{1,0:T(8,128)(2,1)S(1)}, u32[]{:S(2)}, u32[]{:S(2)}) collective-permute-start(bf16[64,1152]{1,0:T(8,128)(2,1)S(1)} %add_convert_fusion.kept_ref), channel_id=1, source_target_pairs={{0,8},{1,17},{2,10},{3,19},{4,12},{5,21},{6,14},{7,23},{8,0},{9,25... | collective-permute-start | bytes 442376 | tf_op jit(solution)/shard_map/ppermute | solution.py:356
  39.4 5.1 %collective-permute-start.18 = (bf16[64,1152]{1,0:T(8,128)(2,1)S(1)}, bf16[64,1152]{1,0:T(8,128)(2,1)S(1)}, u32[]{:S(2)}, u32[]{:S(2)}) collective-permute-start(bf16[64,1152]{1,0:T(8,128)(2,1)S(1)} %collective-permute-done.13.far_ref), channel_id=1, source_target_pairs={{0,8},{1,17},{2,10},{3,19},{4,12},{5,21},{6,14},{7,23},{8,0},{9,25... | collective-permute-start | bytes 442376 | tf_op jit(solution)/shard_map/ppermute | solution.py:356
  39.8 4.9 %collective-permute-start.15 = (bf16[128,1152]{1,0:T(8,128)(2,1)S(1)}, bf16[128,1152]{1,0:T(8,128)(2,1)S(1)}, u32[]{:S(2)}, u32[]{:S(2)}) collective-permute-start(bf16[128,1152]{1,0:T(8,128)(2,1)S(1)} %shard_map.85.refs_0_), channel_id=1, source_target_pairs={{0,1},{1,0},{2,3},{3,2},{4,5},{5,4},{6,7},{7,6},{8,9},{9,8},{10,11... | collective-permute-start | bytes 884744 | tf_op jit(solution)/shard_map/ppermute | solution.py:348
  42.0 2.7 %collective-permute-start.16 = (bf16[128,1152]{1,0:T(8,128)(2,1)S(1)}, bf16[128,1152]{1,0:T(8,128)(2,1)S(1)}, u32[]{:S(2)}, u32[]{:S(2)}) collective-permute-start(bf16[128,1152]{1,0:T(8,128)(2,1)S(1)} %shard_map.87.refs_1_), channel_id=1, source_target_pairs={{0,1},{1,0},{2,3},{3,2},{4,5},{5,4},{6,7},{7,6},{8,9},{9,8},{10,11... | collective-permute-start | bytes 884744 | tf_op jit(solution)/shard_map/ppermute | solution.py:348
  42.1 6.8 %collective-permute-start.14 = (bf16[128,1152]{1,0:T(8,128)(2,1)S(1)}, bf16[128,1152]{1,0:T(8,128)(2,1)S(1)}, u32[]{:S(2)}, u32[]{:S(2)}) collective-permute-start(bf16[128,1152]{1,0:T(8,128)(2,1)S(1)} %shard_map.87.refs_1_), channel_id=1, source_target_pairs={{0,8},{1,17},{2,10},{3,19},{4,12},{5,21},{6,14},{7,23},{8,0},{9,25... | collective-permute-start | bytes 884744 | tf_op jit(solution)/shard_map/ppermute | solution.py:356
  44.6 4.3 %collective-permute-start.20 = (bf16[128,1152]{1,0:T(8,128)(2,1)S(1)}, bf16[128,1152]{1,0:T(8,128)(2,1)S(1)}, u32[]{:S(2)}, u32[]{:S(2)}) collective-permute-start(bf16[128,1152]{1,0:T(8,128)(2,1)S(1)} %shard_map.88.refs_3_), channel_id=1, source_target_pairs={{0,1},{1,0},{2,3},{3,2},{4,5},{5,4},{6,7},{7,6},{8,9},{9,8},{10,11... | collective-permute-start | bytes 884744 | tf_op jit(solution)/shard_map/ppermute | solution.py:348
  48.9 1.6 %collective-permute-start.19 = (bf16[128,1152]{1,0:T(8,128)(2,1)S(1)}, bf16[128,1152]{1,0:T(8,128)(2,1)S(1)}, u32[]{:S(2)}, u32[]{:S(2)}) collective-permute-start(bf16[128,1152]{1,0:T(8,128)(2,1)S(1)} %collective-permute-done.14.refs_1_), channel_id=1, source_target_pairs={{0,1},{1,0},{2,3},{3,2},{4,5},{5,4},{6,7},{7,6},{8,9},{9,8},{10,11... | collective-permute-start | bytes 884744 | tf_op jit(solution)/shard_map/ppermute | solution.py:348
  48.9 1.6 %copy-start = (bf16[1,128,2304]{2,1,0:T(8,128)(2,1)S(1)}, bf16[1,128,2304]{2,1,0:T(8,128)(2,1)}, u32[]{:S(2)}) copy-start(bf16[1,128,2304]{2,1,0:T(8,128)(2,1)} %param.5) | copy-start | bytes 1769476

commit v6 on v5

--- a/solution.py
+++ b/solution.py
@@ -158,7 +158,7 @@
     bits = layers.bit_length() - 1
     scale = toks ** (-0.5)
     count = len(jobs)
-    pieces = 3 if cols % (3 * 128) == 0 else 1
+    pieces = 9 if cols % (9 * 128) == 0 else 1
 
     def kernel(pos, *refs):
         refs = list(refs)

time: 52.8 us -> 52.7 us (level)
  no operation moved by 1% of the time
where the time goes in v6:
time: 52.7 us; the launch traced here: 52.4 us
  waiting for transfers between devices  18.4 us (35%)
  starting transfers between devices  17.7 us (34%)
  Pallas kernels  15 us (28%)
  between operations  0.87 us (2%)
    ppermute x9, starting transfers between devices, swap_layer(): return lax.ppermute(value, ('layer', 'feat'), pairs)  12.7 us
    ppermute x12, waiting for transfers between devices, swap_feat(): lax.ppermute(value, 'feat', [(f, f ^ 1 << bit) for f in range(feats)])  12.2 us
    pallas_call x4, Pallas kernels, backward(): pl.pallas_call(kernel, in_specs=in_specs, out_specs=out_specs, out_shape=...  8.33 us
    ppermute x9, waiting for transfers between devices, swap_layer(): return lax.ppermute(value, ('layer', 'feat'), pairs)  6.22 us
    ppermute x12, starting transfers between devices, swap_feat(): lax.ppermute(value, 'feat', [(f, f ^ 1 << bit) for f in range(feats)])  4.97 us
    pallas_call x2, Pallas kernels, decode(): pl.pallas_call(kernel, in_specs=[IN_SMEM, IN_VMEM, IN_PLACE], out_specs=[...  4.01 us
    pallas_call x1, Pallas kernels, encode(): pl.pallas_call(kernel, in_specs=[IN_SMEM] + [IN_PLACE] * 4, out_specs=[IN...  2.15 us
  transfers between devices with their start and end apart: 21, of which 10 were waited for; matrix products, arithmetic and copies ran while one was open for 1% of the time, Pallas kernels for 20%

profile of v6, /device:TPU:0, one launch (start us, length us, event | category | flops | bytes accessed | tf_op | source)
XLA Modules:
  0.0 52.4 jit_solution(6231740989444571902)
XLA Ops:
  0.6 2.1 %shard_map.76 = (f32[128,256]{1,0:T(8,128)S(1)}, bf16[128,256]{1,0:T(8,128)(2,1)S(1)}, bf16[256,128]{1,0:T(8,128)(2,1)S(1)}, bf16[128,1152]{1,0:T(8,128)(2,1)S(1)}) custom-call(s32[1]{0:T(128)} %bitcast.pos, bf16[128,2304]{1,0:T(8,128)(2,1)} %bitcast.14, bf16[2304,256]{1,0:T(8,128)(2,1)} %bitcast.24, f32[1,256]{1,0:T(1,128)} %b_hbm.1, ...), custom_call_target="tpu_custom_call" | custom-call | flops 1 | bytes 1 | tf_op jit(solution)/shard_map/pallas_call | solution.py:107
  2.8 0.5 collective-permute-start
  3.3 1.6 %shard_map.77 = (f32[128,1152]{1,0:T(8,128)S(1)}, bf16[128,1152]{1,0:T(8,128)(2,1)S(1)}) custom-call(s32[1]{0:T(128)} %bitcast.pos, bf16[128,256]{1,0:T(8,128)(2,1)S(1)} %get-tuple-element.37.act_ref, bf16[4,256,2304]{2,1,0:T(8,128)(2,1)} %bitcast.17), custom_call_target="tpu_custom_call" | custom-call | flops 1 | bytes 1 | tf_op jit(solution)/shard_map/pallas_call | solution.py:141
  4.9 0.1 collective-permute-start.2
  5.0 0.1 copy.11
  5.2 0.5 collective-permute-start.4
  5.8 2.5 %collective-permute-start.5 = (bf16[128,1152]{1,0:T(8,128)(2,1)S(1)}, bf16[128,1152]{1,0:T(8,128)(2,1)S(1)}, u32[]{:S(2)}, u32[]{:S(2)}) collective-permute-start(bf16[128,1152]{1,0:T(8,128)(2,1)S(1)} %shard_map.78), channel_id=1, source_target_pairs={{0,8},{1,17},{2,10},{3,19},{4,12},{5,21},{6,14},{7,23},{8,0},{9,25... | collective-permute-start | bytes 884744 | tf_op jit(solution)/shard_map/ppermute | solution.py:356
  8.3 2.4 %shard_map.79 = (f32[128,1152]{1,0:T(8,128)S(1)}, bf16[128,1152]{1,0:T(8,128)(2,1)S(1)}, f32[128,1152]{1,0:T(8,128)S(1)}, bf16[128,1152]{1,0:T(8,128)(2,1)S(1)}, f32[128,1152]{1,0:T(8,128)S(1)}) custom-call(s32[1]{0:T(128)} %bitcast.pos, bf16[128,256]{1,0:T(8,128)(2,1)S(1)} %get-tuple-element.37.act_ref, bf16[4,256,2304]{2,1,0:T(8,128)(2,1)} %bitcast.18), custom_call_target="tpu_custom_call" | custom-call | flops 1 | bytes 1 | tf_op jit(solution)/shard_map/pallas_call | solution.py:141
  10.9 1.0 %collective-permute-start.3 = (bf16[128,1152]{1,0:T(8,128)(2,1)S(1)}, bf16[128,1152]{1,0:T(8,128)(2,1)S(1)}, u32[]{:S(2)}, u32[]{:S(2)}) collective-permute-start(bf16[128,1152]{1,0:T(8,128)(2,1)S(1)} %shard_map.80), channel_id=1, source_target_pairs={{0,8},{1,17},{2,10},{3,19},{4,12},{5,21},{6,14},{7,23},{8,0},{9,25... | collective-permute-start | bytes 884744 | tf_op jit(solution)/shard_map/ppermute | solution.py:356
  12.2 0.2 collective-permute-done.6.refs_2_
  12.3 0.6 %collective-permute-done.5.refs_0_ = bf16[128,1152]{1,0:T(8,128)(2,1)S(1)} collective-permute-done((bf16[128,1152]{1,0:T(8,128)(2,1)S(1)}, bf16[128,1152]{1,0:T(8,128)(2,1)S(1)}, u32[]{:S(2)}, u32[]{:S(2)}) %collective-permute-start.5) | collective-permute-done | bytes 294944 | tf_op jit(solution)/shard_map/ppermute | solution.py:356
  13.1 2.9 %collective-permute-start.8 = (bf16[64,1152]{1,0:T(8,128)(2,1)S(1)}, bf16[64,1152]{1,0:T(8,128)(2,1)S(1)}, u32[]{:S(2)}, u32[]{:S(2)}) collective-permute-start(bf16[64,1152]{1,0:T(8,128)(2,1)S(1)} %get-tuple-element.47), channel_id=1, source_target_pairs={{0,18},{1,11},{2,16},{3,9},{4,22},{5,15},{6,20},{7,13},{8,26},{9,3... | collective-permute-start | bytes 442376 | tf_op jit(solution)/shard_map/ppermute | solution.py:356
  16.0 0.1 select_select_fusion.refs_3_
  16.1 0.9 %collective-permute-start.7 = (bf16[64,1152]{1,0:T(8,128)(2,1)S(1)}, bf16[64,1152]{1,0:T(8,128)(2,1)S(1)}, u32[]{:S(2)}, u32[]{:S(2)}) collective-permute-start(bf16[64,1152]{1,0:T(8,128)(2,1)S(1)} %get-tuple-element.46), channel_id=1, source_target_pairs={{0,16},{1,9},{2,18},{3,11},{4,20},{5,13},{6,22},{7,15},{8,24},{9,1... | collective-permute-start | bytes 442376 | tf_op jit(solution)/shard_map/ppermute | solution.py:356
  17.0 3.3 %collective-permute-done.3.refs_2_ = bf16[128,1152]{1,0:T(8,128)(2,1)S(1)} collective-permute-done((bf16[128,1152]{1,0:T(8,128)(2,1)S(1)}, bf16[128,1152]{1,0:T(8,128)(2,1)S(1)}, u32[]{:S(2)}, u32[]{:S(2)}) %collective-permute-start.3) | collective-permute-done | bytes 294944 | tf_op jit(solution)/shard_map/ppermute | solution.py:356
  20.4 1.3 %collective-permute-start.9 = (bf16[64,1152]{1,0:T(8,128)(2,1)S(1)}, bf16[64,1152]{1,0:T(8,128)(2,1)S(1)}, u32[]{:S(2)}, u32[]{:S(2)}) collective-permute-start(bf16[64,1152]{1,0:T(8,128)(2,1)S(1)} %shard_map.83), channel_id=1, source_target_pairs={{0,2},{1,3},{2,0},{3,1},{4,6},{5,7},{6,4},{7,5},{8,10},{9,11},{10,... | collective-permute-start | bytes 442376 | tf_op jit(solution)/shard_map/ppermute | solution.py:348
  21.6 5.0 %collective-permute-done.9.refs_6_ = bf16[64,1152]{1,0:T(8,128)(2,1)S(1)} collective-permute-done((bf16[64,1152]{1,0:T(8,128)(2,1)S(1)}, bf16[64,1152]{1,0:T(8,128)(2,1)S(1)}, u32[]{:S(2)}, u32[]{:S(2)}) %collective-permute-start.9) | collective-permute-done | bytes 147488 | tf_op jit(solution)/shard_map/ppermute | solution.py:348
  26.6 0.1 shard_map.84
  26.8 2.1 %collective-permute-start.10 = (bf16[64,1152]{1,0:T(8,128)(2,1)S(1)}, bf16[64,1152]{1,0:T(8,128)(2,1)S(1)}, u32[]{:S(2)}, u32[]{:S(2)}) collective-permute-start(bf16[64,1152]{1,0:T(8,128)(2,1)S(1)} %convert_element_type.13), channel_id=1, source_target_pairs={{0,4},{1,5},{2,6},{3,7},{4,0},{5,1},{6,2},{7,3},{8,12},{9,13},{10,... | collective-permute-start | bytes 442376 | tf_op jit(solution)/shard_map/ppermute | solution.py:348
  28.9 5.3 %collective-permute-done.10 = bf16[64,1152]{1,0:T(8,128)(2,1)S(1)} collective-permute-done((bf16[64,1152]{1,0:T(8,128)(2,1)S(1)}, bf16[64,1152]{1,0:T(8,128)(2,1)S(1)}, u32[]{:S(2)}, u32[]{:S(2)}) %collective-permute-start.10) | collective-permute-done | bytes 147488 | tf_op jit(solution)/shard_map/ppermute | solution.py:348
  34.3 0.9 %collective-permute-start.12 = (bf16[64,1152]{1,0:T(8,128)(2,1)S(1)}, bf16[64,1152]{1,0:T(8,128)(2,1)S(1)}, u32[]{:S(2)}, u32[]{:S(2)}) collective-permute-start(bf16[64,1152]{1,0:T(8,128)(2,1)S(1)} %add_convert_fusion.kept_ref), channel_id=1, source_target_pairs={{0,18},{1,11},{2,16},{3,9},{4,22},{5,15},{6,20},{7,13},{8,26},{9,3... | collective-permute-start | bytes 442376 | tf_op jit(solution)/shard_map/ppermute | solution.py:356
  35.2 2.6 %collective-permute-start.11 = (bf16[64,1152]{1,0:T(8,128)(2,1)S(1)}, bf16[64,1152]{1,0:T(8,128)(2,1)S(1)}, u32[]{:S(2)}, u32[]{:S(2)}) collective-permute-start(bf16[64,1152]{1,0:T(8,128)(2,1)S(1)} %add_convert_fusion.kept_ref), channel_id=1, source_target_pairs={{0,16},{1,9},{2,18},{3,11},{4,20},{5,13},{6,22},{7,15},{8,24},{9,1... | collective-permute-start | bytes 442376 | tf_op jit(solution)/shard_map/ppermute | solution.py:356
  37.7 1.6 %collective-permute-done.13.far_ref = bf16[64,1152]{1,0:T(8,128)(2,1)S(1)} collective-permute-done((bf16[64,1152]{1,0:T(8,128)(2,1)S(1)}, bf16[64,1152]{1,0:T(8,128)(2,1)S(1)}, u32[]{:S(2)}, u32[]{:S(2)}) %collective-permute-start.13) | collective-permute-done | bytes 147488 | tf_op jit(solution)/shard_map/ppermute | solution.py:348
  39.4 0.4 collective-permute-start.18
  39.9 1.5 %shard_map.86 = (f32[128,256]{1,0:T(8,128)S(1)}, bf16[4,256,2304]{2,1,0:T(8,128)(2,1)}) custom-call(s32[1]{0:T(128)} %bitcast.pos, bf16[128,1152]{1,0:T(8,128)(2,1)S(1)} %shard_map.85.refs_0_, bf16[256,128]{1,0:T(8,128)(2,1)S(1)} %get-tuple-element.49.refs_1_.refs_4_.refs_2_, bf16[4,256,2304]{2,1,0:T(8,128)(2,1)} %bitcast.19), custom_call_target="tpu_custom_call" | custom-call | flops 1 | bytes 1 | tf_op jit(solution)/shard_map/pallas_call | solution.py:270
  41.4 0.6 %collective-permute-done.11.kept_ref = bf16[64,1152]{1,0:T(8,128)(2,1)S(1)} collective-permute-done((bf16[64,1152]{1,0:T(8,128)(2,1)S(1)}, bf16[64,1152]{1,0:T(8,128)(2,1)S(1)}, u32[]{:S(2)}, u32[]{:S(2)}) %collective-permute-start.11) | collective-permute-done | bytes 147488 | tf_op jit(solution)/shard_map/ppermute | solution.py:356
  42.1 1.6 %collective-permute-start.14 = (bf16[128,1152]{1,0:T(8,128)(2,1)S(1)}, bf16[128,1152]{1,0:T(8,128)(2,1)S(1)}, u32[]{:S(2)}, u32[]{:S(2)}) collective-permute-start(bf16[128,1152]{1,0:T(8,128)(2,1)S(1)} %shard_map.87.refs_1_), channel_id=1, source_target_pairs={{0,8},{1,17},{2,10},{3,19},{4,12},{5,21},{6,14},{7,23},{8,0},{9,25... | collective-permute-start | bytes 884744 | tf_op jit(solution)/shard_map/ppermute | solution.py:356
  43.7 0.9 %collective-permute-done.18.far_ref = bf16[64,1152]{1,0:T(8,128)(2,1)S(1)} collective-permute-done((bf16[64,1152]{1,0:T(8,128)(2,1)S(1)}, bf16[64,1152]{1,0:T(8,128)(2,1)S(1)}, u32[]{:S(2)}, u32[]{:S(2)}) %collective-permute-start.18) | collective-permute-done | bytes 147488 | tf_op jit(solution)/shard_map/ppermute | solution.py:356
  44.7 3.4 %shard_map.89 = (f32[128,256]{1,0:T(8,128)S(1)}, bf16[4,256,2304]{2,1,0:T(8,128)(2,1)}, bf16[256,1152]{1,0:T(8,128)(2,1)S(1)}, bf16[256,1152]{1,0:T(8,128)(2,1)S(1)}, bf16[256,1152]{1,0:T(8,128)(2,1)S(1)}) custom-call(s32[1]{0:T(128)} %bitcast.pos, bf16[128,1152]{1,0:T(8,128)(2,1)S(1)} %collective-permute-done.15.refs_0_, ...), custom_call_target="tpu_custom_call", output_to_operand_aliasing={{1}: (8, {})} | custom-call | flops 1 | bytes 1 | tf_op jit(solution)/shard_map/pallas_call | solution.py:270
  48.0 0.8 %collective-permute-done.14.refs_1_ = bf16[128,1152]{1,0:T(8,128)(2,1)S(1)} collective-permute-done((bf16[128,1152]{1,0:T(8,128)(2,1)S(1)}, bf16[128,1152]{1,0:T(8,128)(2,1)S(1)}, u32[]{:S(2)}, u32[]{:S(2)}) %collective-permute-start.14) | collective-permute-done | bytes 294944 | tf_op jit(solution)/shard_map/ppermute | solution.py:356
  48.9 1.5 %shard_map.90 = (f32[128,256]{1,0:T(8,128)S(1)}, bf16[4,256,2304]{2,1,0:T(8,128)(2,1)}) custom-call(s32[1]{0:T(128)} %bitcast.pos, bf16[128,1152]{1,0:T(8,128)(2,1)S(1)} %collective-permute-done.20.refs_0_, bf16[128,1152]{1,0:T(8,128)(2,1)S(1)} %collective-permute-done.14.refs_1_, ...), custom_call_target="tpu_custom_call", output_to_operand_aliasing={{1}: (6, {})} | custom-call | flops 1 | bytes 1 | tf_op jit(solution)/shard_map/pallas_call | solution.py:270
  50.4 2.0 %shard_map.91 = (bf16[4,256,2304]{2,1,0:T(8,128)(2,1)}, bf16[2304,256]{1,0:T(8,128)(2,1)}, f32[1,256]{1,0:T(1,128)}) custom-call(s32[1]{0:T(128)} %bitcast.pos, bf16[128,1152]{1,0:T(8,128)(2,1)S(1)} %collective-permute-done.19.refs_0_, bf16[256,128]{1,0:T(8,128)(2,1)S(1)} %get-tuple-element.49.refs_1_.refs_4_.refs_2_, ...), custom_call_target="tpu_custom_call", output_to_operand_aliasing={{0}: (5, {})} | custom-call | flops 1 | bytes 1 | tf_op jit(solution)/shard_map/pallas_call | solution.py:270
  (37 shorter events, 1.2 us)
Async XLA Ops:
  0.6 4.4 %copy-start.1 = (bf16[1,128,288]{1,2,0:T(8,128)(2,1)S(1)}, bf16[1,128,288]{1,2,0:T(8,128)(2,1)}, u32[]{:S(2)}) copy-start(bf16[1,128,288]{1,2,0:T(8,128)(2,1)} %param.6) | copy-start | bytes 221188
  2.8 2.4 %collective-permute-start = (bf16[128,1152]{1,0:T(8,128)(2,1)S(1)}, bf16[128,1152]{1,0:T(8,128)(2,1)S(1)}, u32[]{:S(2)}, u32[]{:S(2)}) collective-permute-start(bf16[128,1152]{1,0:T(8,128)(2,1)S(1)} %get-tuple-element.36), channel_id=1, source_target_pairs={{0,1},{1,0},{2,3},{3,2},{4,5},{5,4},{6,7},{7,6},{8,9},{9,8},{10,11... | collective-permute-start | bytes 884744 | tf_op jit(solution)/shard_map/ppermute | solution.py:348
  4.9 5.9 %collective-permute-start.2 = (bf16[128,1152]{1,0:T(8,128)(2,1)S(1)}, bf16[128,1152]{1,0:T(8,128)(2,1)S(1)}, u32[]{:S(2)}, u32[]{:S(2)}) collective-permute-start(bf16[128,1152]{1,0:T(8,128)(2,1)S(1)} %get-tuple-element.42), channel_id=1, source_target_pairs={{0,1},{1,0},{2,3},{3,2},{4,5},{5,4},{6,7},{7,6},{8,9},{9,8},{10,11... | collective-permute-start | bytes 884744 | tf_op jit(solution)/shard_map/ppermute | solution.py:348
  5.2 6.7 %collective-permute-start.4 = (bf16[128,288]{1,0:T(8,128)(2,1)S(1)}, bf16[128,288]{1,0:T(8,128)(2,1)S(1)}, u32[]{:S(2)}, u32[]{:S(2)}) collective-permute-start(bf16[128,288]{1,0:T(8,128)(2,1)S(1)} %bitcast.25), channel_id=1, source_target_pairs={{0,1},{1,0},{2,3},{3,2},{4,5},{5,4},{6,7},{7,6},{8,9},{9,8},{10,11... | collective-permute-start | bytes 221192 | tf_op jit(solution)/shard_map/ppermute | solution.py:348
  5.8 7.2 %collective-permute-start.5 = (bf16[128,1152]{1,0:T(8,128)(2,1)S(1)}, bf16[128,1152]{1,0:T(8,128)(2,1)S(1)}, u32[]{:S(2)}, u32[]{:S(2)}) collective-permute-start(bf16[128,1152]{1,0:T(8,128)(2,1)S(1)} %shard_map.78), channel_id=1, source_target_pairs={{0,8},{1,17},{2,10},{3,19},{4,12},{5,21},{6,14},{7,23},{8,0},{9,25... | collective-permute-start | bytes 884744 | tf_op jit(solution)/shard_map/ppermute | solution.py:356
  10.7 1.6 %collective-permute-start.6 = (bf16[128,1152]{1,0:T(8,128)(2,1)S(1)}, bf16[128,1152]{1,0:T(8,128)(2,1)S(1)}, u32[]{:S(2)}, u32[]{:S(2)}) collective-permute-start(bf16[128,1152]{1,0:T(8,128)(2,1)S(1)} %get-tuple-element.45), channel_id=1, source_target_pairs={{0,1},{1,0},{2,3},{3,2},{4,5},{5,4},{6,7},{7,6},{8,9},{9,8},{10,11... | collective-permute-start | bytes 884744 | tf_op jit(solution)/shard_map/ppermute | solution.py:348
  10.9 9.4 %collective-permute-start.3 = (bf16[128,1152]{1,0:T(8,128)(2,1)S(1)}, bf16[128,1152]{1,0:T(8,128)(2,1)S(1)}, u32[]{:S(2)}, u32[]{:S(2)}) collective-permute-start(bf16[128,1152]{1,0:T(8,128)(2,1)S(1)} %shard_map.80), channel_id=1, source_target_pairs={{0,8},{1,17},{2,10},{3,19},{4,12},{5,21},{6,14},{7,23},{8,0},{9,25... | collective-permute-start | bytes 884744 | tf_op jit(solution)/shard_map/ppermute | solution.py:356
  11.9 8.4 %collective-permute-start.1 = (bf16[128,1152]{1,0:T(8,128)(2,1)S(1)}, bf16[128,1152]{1,0:T(8,128)(2,1)S(1)}, u32[]{:S(2)}, u32[]{:S(2)}) collective-permute-start(bf16[128,1152]{1,0:T(8,128)(2,1)S(1)} %get-tuple-element.39), channel_id=1, source_target_pairs={{0,1},{1,0},{2,3},{3,2},{4,5},{5,4},{6,7},{7,6},{8,9},{9,8},{10,11... | collective-permute-start | bytes 884744 | tf_op jit(solution)/shard_map/ppermute | solution.py:348
  13.1 8.6 %collective-permute-start.8 = (bf16[64,1152]{1,0:T(8,128)(2,1)S(1)}, bf16[64,1152]{1,0:T(8,128)(2,1)S(1)}, u32[]{:S(2)}, u32[]{:S(2)}) collective-permute-start(bf16[64,1152]{1,0:T(8,128)(2,1)S(1)} %get-tuple-element.47), channel_id=1, source_target_pairs={{0,18},{1,11},{2,16},{3,9},{4,22},{5,15},{6,20},{7,13},{8,26},{9,3... | collective-permute-start | bytes 442376 | tf_op jit(solution)/shard_map/ppermute | solution.py:356
  16.1 10.6 %collective-permute-start.7 = (bf16[64,1152]{1,0:T(8,128)(2,1)S(1)}, bf16[64,1152]{1,0:T(8,128)(2,1)S(1)}, u32[]{:S(2)}, u32[]{:S(2)}) collective-permute-start(bf16[64,1152]{1,0:T(8,128)(2,1)S(1)} %get-tuple-element.46), channel_id=1, source_target_pairs={{0,16},{1,9},{2,18},{3,11},{4,20},{5,13},{6,22},{7,15},{8,24},{9,1... | collective-permute-start | bytes 442376 | tf_op jit(solution)/shard_map/ppermute | solution.py:356
  20.4 6.3 %collective-permute-start.9 = (bf16[64,1152]{1,0:T(8,128)(2,1)S(1)}, bf16[64,1152]{1,0:T(8,128)(2,1)S(1)}, u32[]{:S(2)}, u32[]{:S(2)}) collective-permute-start(bf16[64,1152]{1,0:T(8,128)(2,1)S(1)} %shard_map.83), channel_id=1, source_target_pairs={{0,2},{1,3},{2,0},{3,1},{4,6},{5,7},{6,4},{7,5},{8,10},{9,11},{10,... | collective-permute-start | bytes 442376 | tf_op jit(solution)/shard_map/ppermute | solution.py:348
  26.8 7.4 %collective-permute-start.10 = (bf16[64,1152]{1,0:T(8,128)(2,1)S(1)}, bf16[64,1152]{1,0:T(8,128)(2,1)S(1)}, u32[]{:S(2)}, u32[]{:S(2)}) collective-permute-start(bf16[64,1152]{1,0:T(8,128)(2,1)S(1)} %convert_element_type.13), channel_id=1, source_target_pairs={{0,4},{1,5},{2,6},{3,7},{4,0},{5,1},{6,2},{7,3},{8,12},{9,13},{10,... | collective-permute-start | bytes 442376 | tf_op jit(solution)/shard_map/ppermute | solution.py:348
  34.2 5.2 %collective-permute-start.13 = (bf16[64,1152]{1,0:T(8,128)(2,1)S(1)}, bf16[64,1152]{1,0:T(8,128)(2,1)S(1)}, u32[]{:S(2)}, u32[]{:S(2)}) collective-permute-start(bf16[64,1152]{1,0:T(8,128)(2,1)S(1)} %add_convert_fusion.kept_ref), channel_id=1, source_target_pairs={{0,2},{1,3},{2,0},{3,1},{4,6},{5,7},{6,4},{7,5},{8,10},{9,11},{10,... | collective-permute-start | bytes 442376 | tf_op jit(solution)/shard_map/ppermute | solution.py:348
  34.3 7.1 %collective-permute-start.12 = (bf16[64,1152]{1,0:T(8,128)(2,1)S(1)}, bf16[64,1152]{1,0:T(8,128)(2,1)S(1)}, u32[]{:S(2)}, u32[]{:S(2)}) collective-permute-start(bf16[64,1152]{1,0:T(8,128)(2,1)S(1)} %add_convert_fusion.kept_ref), channel_id=1, source_target_pairs={{0,18},{1,11},{2,16},{3,9},{4,22},{5,15},{6,20},{7,13},{8,26},{9,3... | collective-permute-start | bytes 442376 | tf_op jit(solution)/shard_map/ppermute | solution.py:356
  35.2 6.8 %collective-permute-start.11 = (bf16[64,1152]{1,0:T(8,128)(2,1)S(1)}, bf16[64,1152]{1,0:T(8,128)(2,1)S(1)}, u32[]{:S(2)}, u32[]{:S(2)}) collective-permute-start(bf16[64,1152]{1,0:T(8,128)(2,1)S(1)} %add_convert_fusion.kept_ref), channel_id=1, source_target_pairs={{0,16},{1,9},{2,18},{3,11},{4,20},{5,13},{6,22},{7,15},{8,24},{9,1... | collective-permute-start | bytes 442376 | tf_op jit(solution)/shard_map/ppermute | solution.py:356
  37.7 5.9 %collective-permute-start.17 = (bf16[64,1152]{1,0:T(8,128)(2,1)S(1)}, bf16[64,1152]{1,0:T(8,128)(2,1)S(1)}, u32[]{:S(2)}, u32[]{:S(2)}) collective-permute-start(bf16[64,1152]{1,0:T(8,128)(2,1)S(1)} %add_convert_fusion.kept_ref), channel_id=1, source_target_pairs={{0,8},{1,17},{2,10},{3,19},{4,12},{5,21},{6,14},{7,23},{8,0},{9,25... | collective-permute-start | bytes 442376 | tf_op jit(solution)/shard_map/ppermute | solution.py:356
  39.4 5.1 %collective-permute-start.18 = (bf16[64,1152]{1,0:T(8,128)(2,1)S(1)}, bf16[64,1152]{1,0:T(8,128)(2,1)S(1)}, u32[]{:S(2)}, u32[]{:S(2)}) collective-permute-start(bf16[64,1152]{1,0:T(8,128)(2,1)S(1)} %collective-permute-done.13.far_ref), channel_id=1, source_target_pairs={{0,8},{1,17},{2,10},{3,19},{4,12},{5,21},{6,14},{7,23},{8,0},{9,25... | collective-permute-start | bytes 442376 | tf_op jit(solution)/shard_map/ppermute | solution.py:356
  39.8 4.9 %collective-permute-start.15 = (bf16[128,1152]{1,0:T(8,128)(2,1)S(1)}, bf16[128,1152]{1,0:T(8,128)(2,1)S(1)}, u32[]{:S(2)}, u32[]{:S(2)}) collective-permute-start(bf16[128,1152]{1,0:T(8,128)(2,1)S(1)} %shard_map.85.refs_0_), channel_id=1, source_target_pairs={{0,1},{1,0},{2,3},{3,2},{4,5},{5,4},{6,7},{7,6},{8,9},{9,8},{10,11... | collective-permute-start | bytes 884744 | tf_op jit(solution)/shard_map/ppermute | solution.py:348
  42.0 2.7 %collective-permute-start.16 = (bf16[128,1152]{1,0:T(8,128)(2,1)S(1)}, bf16[128,1152]{1,0:T(8,128)(2,1)S(1)}, u32[]{:S(2)}, u32[]{:S(2)}) collective-permute-start(bf16[128,1152]{1,0:T(8,128)(2,1)S(1)} %shard_map.87.refs_1_), channel_id=1, source_target_pairs={{0,1},{1,0},{2,3},{3,2},{4,5},{5,4},{6,7},{7,6},{8,9},{9,8},{10,11... | collective-permute-start | bytes 884744 | tf_op jit(solution)/shard_map/ppermute | solution.py:348
  42.1 6.8 %collective-permute-start.14 = (bf16[128,1152]{1,0:T(8,128)(2,1)S(1)}, bf16[128,1152]{1,0:T(8,128)(2,1)S(1)}, u32[]{:S(2)}, u32[]{:S(2)}) collective-permute-start(bf16[128,1152]{1,0:T(8,128)(2,1)S(1)} %shard_map.87.refs_1_), channel_id=1, source_target_pairs={{0,8},{1,17},{2,10},{3,19},{4,12},{5,21},{6,14},{7,23},{8,0},{9,25... | collective-permute-start | bytes 884744 | tf_op jit(solution)/shard_map/ppermute | solution.py:356
  44.6 4.3 %collective-permute-start.20 = (bf16[128,1152]{1,0:T(8,128)(2,1)S(1)}, bf16[128,1152]{1,0:T(8,128)(2,1)S(1)}, u32[]{:S(2)}, u32[]{:S(2)}) collective-permute-start(bf16[128,1152]{1,0:T(8,128)(2,1)S(1)} %shard_map.88.refs_3_), channel_id=1, source_target_pairs={{0,1},{1,0},{2,3},{3,2},{4,5},{5,4},{6,7},{7,6},{8,9},{9,8},{10,11... | collective-permute-start | bytes 884744 | tf_op jit(solution)/shard_map/ppermute | solution.py:348
  48.9 1.6 %collective-permute-start.19 = (bf16[128,1152]{1,0:T(8,128)(2,1)S(1)}, bf16[128,1152]{1,0:T(8,128)(2,1)S(1)}, u32[]{:S(2)}, u32[]{:S(2)}) collective-permute-start(bf16[128,1152]{1,0:T(8,128)(2,1)S(1)} %collective-permute-done.14.refs_1_), channel_id=1, source_target_pairs={{0,1},{1,0},{2,3},{3,2},{4,5},{5,4},{6,7},{7,6},{8,9},{9,8},{10,11... | collective-permute-start | bytes 884744 | tf_op jit(solution)/shard_map/ppermute | solution.py:348
  48.9 1.6 %copy-start = (bf16[1,128,2304]{2,1,0:T(8,128)(2,1)S(1)}, bf16[1,128,2304]{2,1,0:T(8,128)(2,1)}, u32[]{:S(2)}) copy-start(bf16[1,128,2304]{2,1,0:T(8,128)(2,1)} %param.5) | copy-start | bytes 1769476
